TPU v7x, 128 devices: a whole 4x4x4 slice. The times are simulated.
128 devices in a mesh: dp: 64 (over y_hi, x, z, core), tensor: 2 (over y_lo).
Axes of the slice: x: 4, y: 4 (y_hi: 2, y_lo: 2; y = y_hi * 2 + y_lo), z: 4, core: 2. Of those that a mesh axis runs over, the one named last changes fastest.
Arguments:
- inputs: bfloat16 [2, 16384, 1536], P(None, ('dp', 'tensor')), may hold values from -24 to 24
- out_grad: bfloat16 [2, 16384, 1536], P(None, ('dp', 'tensor')), may hold values from -24 to 24
- lengths: int32 [2, 64], P(None, 'dp'), may hold values from 64 to 256, as said below
- query_weight: bfloat16 [1536, 1536], P('dp', 'tensor'), may hold values from -0.21875 to 0.21875
- key_matrix: bfloat16 [1536, 768], P('dp', 'tensor'), may hold values from -0.15625 to 0.15625
- value_matrix: bfloat16 [1536, 768], P('dp', 'tensor'), may hold values from -0.15625 to 0.15625
- output_weight: bfloat16 [1536, 1536], P('tensor', 'dp'), may hold values from -0.625 to 0.625
- gate_weight: bfloat16 [1536, 4096], P('dp', 'tensor'), may hold values from -0.15625 to 0.15625
- up_weight: bfloat16 [1536, 4096], P('dp', 'tensor'), may hold values from -0.15625 to 0.15625
- down_weight: bfloat16 [4096, 1536], P('tensor', 'dp'), may hold values from -0.09375 to 0.09375
- attn_gain: bfloat16 [1536], P('dp'), may hold values from 0.5 to 1.5
- mlp_gain: bfloat16 [1536], P('dp'), may hold values from 0.5 to 1.5
Outputs:
- outputs: bfloat16 [2, 16384, 1536], P(None, ('dp', 'tensor'))
- input_grad: float32 [2, 16384, 1536], P(None, ('dp', 'tensor'))
- query_grad: float32 [1536, 1536], P('dp', 'tensor')
- key_grad: float32 [1536, 768], P('dp', 'tensor')
- value_grad: float32 [1536, 768], P('dp', 'tensor')
- output_grad: float32 [1536, 1536], P('tensor', 'dp')
- gate_grad: float32 [1536, 4096], P('dp', 'tensor')
- up_grad: float32 [1536, 4096], P('dp', 'tensor')
- down_grad: float32 [4096, 1536], P('tensor', 'dp')
- attn_gain_grad: float32 [1536], P('dp')
- mlp_gain_grad: float32 [1536], P('dp')
Inputs may be any that keep to these rules, and one draw needn't show every extreme that they name: `lengths`: in every group one micro-batch, drawn from the seed, has length 256.
All inputs are finite; a program needn't handle non-finite values.
Results may differ from a plain program's by a relative error of at most 0.015.
Values may be sent and summed in bfloat16 or wider, within the bound.
A program may use at most 320 MiB of HBM per device.

v0:
```python
import math

import jax
import jax.numpy as jnp
from jax import lax
from jax.sharding import PartitionSpec as P

HEAD_SIZE = 96


epsilon = 1e-05
rope_base = 100000.0


def turned_gather(arrays, axis, dims):
    turned = [jnp.moveaxis(a, dim, 0) for a, dim in zip(arrays, dims)]
    both = jnp.concatenate([t.reshape(len(t), -1) for t in turned], axis=1)
    out, at, finished = (lax.all_gather(both, axis, axis=0, tiled=True), 0, [])
    for t, dim in zip(turned, dims):
        piece = out[:, at : at + t[0].size].reshape(-1, *t.shape[1:])
        finished.append(jnp.moveaxis(piece, 0, dim))
        at += t[0].size
    return tuple(finished)


def in_blocks(array, dim, peers):
    before, after = (array.shape[:dim], array.shape[dim + 1 :])
    return jnp.moveaxis(array.reshape(*before, peers, -1, *after), dim, 0)


def sum_at_owner(array, axis, dim):
    peers = lax.axis_size(axis)
    tiles = lax.all_to_all(in_blocks(array, dim, peers), axis, 0, 0, tiled=True)
    return jnp.sum(tiles, axis=0)


def sum_at_owner_2(array, axis, dim):
    tiles = in_blocks(array, dim, lax.axis_size(axis))
    arrived = lax.all_to_all(tiles, axis, split_axis=0, concat_axis=0, tiled=True)
    return arrived.astype(jnp.float32).sum(axis=0)


def in_one_piece(arrays, axis, dim, along):
    widths = [math.prod(a.shape[along:]) for a in arrays]
    both = jnp.concatenate(
        [a.reshape(*a.shape[:along], w) for a, w in zip(arrays, widths)], axis=along
    )
    out = lax.psum_scatter(both, axis, scatter_dimension=dim, tiled=True)
    tiles = jnp.split(out, [sum(widths[:k]) for k in range(1, len(widths))], axis=along)
    return tuple((b.reshape(*out.shape[:along], *a.shape[along:]) for a, b in zip(arrays, tiles)))


def rope_tables(element_count, width):
    half_width = width // 2
    inverse = rope_base ** (-(jnp.arange(half_width, dtype=jnp.float32) * 2.0) / width)
    angle = jnp.arange(element_count, dtype=jnp.float32)[:, None] * inverse[None, :]
    cosine_table = jnp.cos(angle)
    sine_table = jnp.sin(angle)
    return (
        jnp.concatenate([cosine_table, cosine_table], -1),
        jnp.concatenate([sine_table, sine_table], -1),
    )


def rotary_apply(values, cosine_table, sine_table):
    half_width = values.shape[-1] // 2
    turned = jnp.concatenate([-values[..., half_width:], values[..., :half_width]], -1)
    return values * cosine_table[:, None, :] + turned * sine_table[:, None, :]


def rotate_back(grads, cosine_table, sine_table):
    half_width = grads.shape[-1] // 2
    shifted = grads * sine_table[:, None, :]
    turned = jnp.concatenate([shifted[..., half_width:], -shifted[..., :half_width]], -1)
    return grads * cosine_table[:, None, :] + turned


def normalize(values):
    inverse_rms = lax.rsqrt(jnp.mean(values * values, -1, keepdims=True) + epsilon)
    return (values * inverse_rms, inverse_rms)


def norm_back(grad_normed, unit_rows, inverse_rms, gain):
    scaled = grad_normed * gain
    return inverse_rms * (scaled - unit_rows * jnp.mean(scaled * unit_rows, -1, keepdims=True))


def outer_sum(left, right):
    return lax.dot_general(
        left, right, (((0,), (0,)), ((), ())), preferred_element_type=jnp.float32
    )


def against(left, right):
    return lax.dot_general(
        left, right, (((1,), (1,)), ((), ())), preferred_element_type=jnp.float32
    )


def masked_scores(query_rows_all, key_rows, length):
    element_count = key_rows.shape[0]
    scores = jnp.einsum(
        "qkgd,skd->kgqs", query_rows_all, key_rows, preferred_element_type=jnp.float32
    )
    scores = scores * (1.0 / math.sqrt(HEAD_SIZE))
    positions = jnp.arange(element_count)
    keep = (positions[None, :] <= positions[:, None]) & (positions[None, :] < length)
    return jnp.where(keep, scores, -1e30)


def body(
    inputs,
    out_grad,
    lengths,
    query_weight,
    key_matrix,
    value_matrix,
    output_weight,
    gate_weight,
    up_weight,
    down_weight,
    attn_gain,
    mlp_gain,
):
    row_count = inputs.shape[1]
    seq_slots = row_count * lax.axis_size("tensor")
    cosine_table, sine_table = rope_tables(seq_slots, HEAD_SIZE)
    offset = lax.axis_index("tensor") * row_count
    totals = None
    shards = None
    result_rows = []
    grad_rows_out = []
    for micro_step in range(inputs.shape[0]):
        attn_set = turned_gather(
            (query_weight, key_matrix, value_matrix, output_weight, attn_gain),
            "dp",
            (0, 0, 0, 1, 0),
        )
        mlp_set = turned_gather((gate_weight, up_weight, down_weight, mlp_gain), "dp", (0, 0, 1, 0))
        full_query, full_key, full_value, full_output, gain_first = attn_set
        full_gate, full_upward, full_down, gain_second = mlp_set
        gain_one = gain_first.astype(jnp.float32)
        gain_two = gain_second.astype(jnp.float32)
        heads_query = full_query.shape[1] // HEAD_SIZE
        heads_kv = full_key.shape[1] // HEAD_SIZE
        query_groups = heads_query // heads_kv
        length = lengths[micro_step, 0]
        in_rows = inputs[micro_step].astype(jnp.float32)
        unit_one, inverse_one = normalize(in_rows)
        normed_first_input = lax.all_gather(
            (unit_one * gain_one).astype(jnp.bfloat16), "tensor", axis=0, tiled=True
        )
        query_lin = jnp.dot(normed_first_input, full_query, preferred_element_type=jnp.float32)
        query_rows_all = rotary_apply(
            query_lin.reshape(seq_slots, heads_query, HEAD_SIZE), cosine_table, sine_table
        ).astype(jnp.bfloat16)
        query_rows_all = query_rows_all.reshape(seq_slots, heads_kv, query_groups, HEAD_SIZE)
        key_lin = jnp.dot(normed_first_input, full_key, preferred_element_type=jnp.float32)
        key_rows = rotary_apply(
            key_lin.reshape(seq_slots, heads_kv, HEAD_SIZE), cosine_table, sine_table
        ).astype(jnp.bfloat16)
        value_rows = jnp.dot(
            normed_first_input, full_value, preferred_element_type=jnp.float32
        ).astype(jnp.bfloat16)
        value_rows = value_rows.reshape(seq_slots, heads_kv, HEAD_SIZE)
        scores = masked_scores(query_rows_all, key_rows, length)
        row_max = jnp.max(scores, -1, keepdims=True)
        exp_terms = jnp.exp(scores - row_max)
        row_total = jnp.sum(exp_terms, -1, keepdims=True)
        log_total = row_max + jnp.log(row_total)
        probs_low = (exp_terms / row_total).astype(jnp.bfloat16)
        mixed = jnp.einsum(
            "kgqs,skd->qkgd", probs_low, value_rows, preferred_element_type=jnp.float32
        )
        mixed = mixed.astype(jnp.bfloat16).reshape(seq_slots, heads_query * HEAD_SIZE)
        attn_out = sum_at_owner(
            jnp.dot(mixed, full_output, preferred_element_type=jnp.float32), "tensor", 0
        )
        hidden = in_rows + attn_out
        unit_two, inverse_two = normalize(hidden)
        second_normed = lax.all_gather(
            (unit_two * gain_two).astype(jnp.bfloat16), "tensor", axis=0, tiled=True
        )
        gate_lin = jnp.dot(second_normed, full_gate, preferred_element_type=jnp.float32)
        up_lin = jnp.dot(second_normed, full_upward, preferred_element_type=jnp.float32)
        sigma = jax.nn.sigmoid(gate_lin)
        active = (gate_lin * sigma * up_lin).astype(jnp.bfloat16)
        mlp_out = sum_at_owner_2(
            jnp.dot(active, full_down, preferred_element_type=jnp.float32).astype(jnp.bfloat16),
            "tensor",
            0,
        )
        result_rows.append((hidden + mlp_out).astype(jnp.bfloat16))
        valid_rows = (offset + jnp.arange(row_count) < length).astype(jnp.float32)
        grad_out = out_grad[micro_step].astype(jnp.float32) * valid_rows[:, None]
        grad_full = lax.all_gather(grad_out.astype(jnp.bfloat16), "tensor", axis=0, tiled=True)
        down_part_turned = outer_sum(grad_full, active)
        grad_active = against(grad_full, full_down)
        grad_gate = (grad_active * up_lin * sigma * (1.0 + gate_lin * (1.0 - sigma))).astype(
            jnp.bfloat16
        )
        grad_upward = (grad_active * gate_lin * sigma).astype(jnp.bfloat16)
        gate_part = outer_sum(second_normed, grad_gate)
        upward_part = outer_sum(second_normed, grad_upward)
        grad_second = lax.psum_scatter(
            against(grad_gate, full_gate) + against(grad_upward, full_upward),
            "tensor",
            scatter_dimension=0,
            tiled=True,
        )
        gain_two_part = jnp.sum(grad_second * unit_two, 0)
        grad_hidden = grad_out + norm_back(grad_second, unit_two, inverse_two, gain_two)
        grad_branch = lax.all_gather(grad_hidden.astype(jnp.bfloat16), "tensor", axis=0, tiled=True)
        output_part_turned = outer_sum(grad_branch, mixed)
        grad_mixed = against(grad_branch, full_output).astype(jnp.bfloat16)
        grad_mixed = grad_mixed.reshape(seq_slots, heads_kv, query_groups, HEAD_SIZE)
        scores_again = masked_scores(query_rows_all, key_rows, length)
        probs_again = jnp.exp(scores_again - log_total)
        grad_probs = jnp.einsum(
            "qkgd,skd->kgqs", grad_mixed, value_rows, preferred_element_type=jnp.float32
        )
        grad_scores = probs_again * (
            grad_probs - jnp.sum(grad_probs * probs_again, -1, keepdims=True)
        )
        grad_scores = grad_scores.astype(jnp.bfloat16)
        score_scale = 1.0 / math.sqrt(HEAD_SIZE)
        grad_queries = (
            jnp.einsum("kgqs,skd->qkgd", grad_scores, key_rows, preferred_element_type=jnp.float32)
            * score_scale
        )
        grad_keys = (
            jnp.einsum(
                "kgqs,qkgd->skd", grad_scores, query_rows_all, preferred_element_type=jnp.float32
            )
            * score_scale
        )
        grad_values = jnp.einsum(
            "kgqs,qkgd->skd",
            probs_again.astype(jnp.bfloat16),
            grad_mixed,
            preferred_element_type=jnp.float32,
        )
        query_back = rotate_back(
            grad_queries.reshape(seq_slots, heads_query, HEAD_SIZE), cosine_table, sine_table
        )
        query_back = query_back.astype(jnp.bfloat16).reshape(seq_slots, heads_query * HEAD_SIZE)
        key_back = (
            rotate_back(grad_keys, cosine_table, sine_table)
            .astype(jnp.bfloat16)
            .reshape(seq_slots, heads_kv * HEAD_SIZE)
        )
        value_back = grad_values.astype(jnp.bfloat16).reshape(seq_slots, heads_kv * HEAD_SIZE)
        query_part = outer_sum(normed_first_input, query_back)
        key_part = outer_sum(normed_first_input, key_back)
        value_part = outer_sum(normed_first_input, value_back)
        first_terms = (
            against(query_back, full_query)
            + against(key_back, full_key)
            + against(value_back, full_value)
        )
        grad_first = lax.psum_scatter(
            first_terms.astype(jnp.bfloat16), "tensor", scatter_dimension=0, tiled=True
        ).astype(jnp.float32)
        gain_one_part = jnp.sum(grad_first * unit_one, 0)
        grad_rows_out.append(grad_hidden + norm_back(grad_first, unit_one, inverse_one, gain_one))
        local = (
            query_part,
            key_part,
            value_part,
            output_part_turned,
            gate_part,
            upward_part,
            down_part_turned,
            gain_one_part,
            gain_two_part,
        )
        totals = (
            local
            if totals is None
            else tuple((a_part + b_part for a_part, b_part in zip(totals, local)))
        )
    shards = in_one_piece(
        (
            totals[0],
            totals[1],
            totals[2],
            totals[3],
            totals[4],
            totals[5],
            totals[6],
            totals[7],
            totals[8],
        ),
        "dp",
        0,
        1,
    )
    gain_sums = lax.psum((shards[7], shards[8]), "tensor")
    return (
        jnp.stack(result_rows),
        jnp.stack(grad_rows_out),
        shards[0],
        shards[1],
        shards[2],
        jnp.transpose(shards[3]),
        shards[4],
        shards[5],
        jnp.transpose(shards[6]),
        gain_sums[0],
        gain_sums[1],
    )


def solution(mesh):
    placed = (
        P(None, ("dp", "tensor"), None),
        P(None, ("dp", "tensor"), None),
        P(None, "dp"),
        P("dp", "tensor"),
        P("dp", "tensor"),
        P("dp", "tensor"),
        P("tensor", "dp"),
        P("dp", "tensor"),
        P("dp", "tensor"),
        P("tensor", "dp"),
        P("dp"),
        P("dp"),
    )
    return jax.shard_map(
        body,
        mesh=mesh,
        in_specs=placed,
        out_specs=(
            P(None, ("dp", "tensor"), None),
            P(None, ("dp", "tensor"), None),
            P("dp", "tensor"),
            P("dp", "tensor"),
            P("dp", "tensor"),
            P("tensor", "dp"),
            P("dp", "tensor"),
            P("dp", "tensor"),
            P("tensor", "dp"),
            P("dp"),
            P("dp"),
        ),
        check_vma=False,
    )
```

profile of v0, /device:TPU:1, one launch (start us, length us, event | category | flops | bytes accessed | tf_op | source)
XLA Modules:
  0.0 1323.0 jit_solution(5953307445742189060)
XLA Ops:
  17.4 1.9 compare_convert_fusion
  21.2 73.4 %all-gather.3.cloned.1.call-done = bf16[1536,2305]{1,0:T(8,128)(2,1)} async-done(((bf16[24,2305]{1,0:T(8,128)(2,1)}), bf16[1536,2305]{1,0:T(8,128)(2,1)}) %all-gather.3.cloned.1.call-update) | async-done | bytes 7080976 | tf_op jit(solution)/shard_map/all_gather | solution.py:18
  96.0 11.1 all_gather.33
  107.1 2.1 convolution_convert_fusion.3
  109.4 1.9 fusion.126
  111.4 2.8 fusion.64
  117.9 3.6 fusion.40
  121.5 3.8 all-to-all-start
  126.9 34.3 %all_gather.38 = bf16[256,1536]{1,0:T(8,128)(2,1)} all-gather(bf16[128,1536]{1,0:T(8,128)(2,1)S(1)} %get-tuple-element.57), channel_id=1, replica_groups=mesh['dp'=64,'tensor'=2] {'tensor'}, dimensions={0}, use_global_device_ids=true | all-gather | bytes 1179648 | tf_op jit(solution)/shard_map/all_gather | solution.py:196
  163.1 19.4 %all_gather.36 = bf16[256,1536]{1,0:T(8,128)(2,1)S(1)} all-gather(bf16[128,1536]{1,0:T(8,128)(2,1)S(1)} %fusion.103), channel_id=1, replica_groups=mesh['dp'=64,'tensor'=2] {'tensor'}, dimensions={0}, use_global_device_ids=true | all-gather | bytes 1179648 | tf_op jit(solution)/shard_map/all_gather | solution.py:150
  182.5 2.1 convolution_convert_fusion.2
  185.5 1.9 fusion.124
  187.5 2.7 fusion.62
  195.3 3.8 fusion.38
  199.1 4.8 all-to-all-start.2
  204.2 29.2 %all_gather.40 = bf16[256,1536]{1,0:T(8,128)(2,1)} all-gather(bf16[128,1536]{1,0:T(8,128)(2,1)} %get-tuple-element.56), channel_id=1, replica_groups=mesh['dp'=64,'tensor'=2] {'tensor'}, dimensions={0}, use_global_device_ids=true | all-gather | bytes 1179648 | tf_op jit(solution)/shard_map/all_gather | solution.py:196
  233.4 2.5 reduce_sum.197
  238.4 2.4 multiply_convert_fusion.7
  240.8 10.0 all_gather.35
  250.8 5.0 fusion.2
  255.8 5.3 fusion.14
  261.2 3.6 multiply_convert_fusion.3
  264.8 6.3 fusion.158
  273.0 3.0 fusion.24
  276.5 5.0 fusion
  281.5 7.4 fusion.159
  288.9 19.4 %all_gather.37 = bf16[256,1536]{1,0:T(8,128)(2,1)S(1)} all-gather(bf16[128,1536]{1,0:T(8,128)(2,1)S(1)} %copy-done.46), channel_id=1, replica_groups=mesh['dp'=64,'tensor'=2] {'tensor'}, dimensions={0}, use_global_device_ids=true | all-gather | bytes 1179648 | tf_op jit(solution)/shard_map/all_gather | solution.py:181
  308.3 5.0 fusion.12
  313.4 3.7 multiply_convert_fusion.1
  318.9 3.0 fusion.27
  322.2 3.4 fusion.160
  325.6 12.2 convolution_add_fusion.2
  337.8 7.9 convolution_add_fusion.1
  345.7 7.9 convolution_add_fusion
  353.7 3.2 multiply_reduce_fusion.1
  356.9 1.9 fusion.146
  358.8 9.1 all_gather.41
  368.8 3.2 fusion.66
  372.0 1.9 copy.105
  378.4 8.4 all_gather.39
  387.7 3.2 fusion.69
  390.9 1.9 copy.101
  392.8 2.4 fusion.45
  406.9 2.7 fusion.58
  410.1 1.9 convolution_add_fusion.8
  412.0 2.9 fusion.31
  416.2 2.9 convolution_add_fusion.4
  419.4 3.5 convolution_add_fusion.6
  423.0 6.1 copy.109
  429.0 3.1 copy.110
  432.5 1.9 convolution_add_fusion.5
  434.5 3.2 copy.111
  438.9 2.9 convolution_add_fusion.3
  441.8 6.1 copy.112
  453.2 58.6 %concatenate.73 = f32[1536,8450]{1,0:T(8,128)} concatenate(f32[1536,768]{1,0:T(8,128)} %copy.109, f32[1536,384]{1,0:T(8,128)S(1)} %copy-done.14, f32[1536,384]{1,0:T(8,128)} %copy.111, f32[1536,768]{1,0:T(8,128)} %copy.112, f32[1536,2048]{1,0:T(8,128)} %convolution_add_fusion.2, f32[1536,2048]{1,0:T(8,128)} %convolution_add_fusion.1, f32[1536,2048]{1,0:T(8,128)} %convolution_add_fusion, ...), dimensions={1} | concatenate | bytes 103833600 | tf_op jit(solution)/shard_map/concatenate | solution.py:45
  513.0 5.6 fusion.32
  518.6 3.5 all-to-all-start.1
  522.2 5.6 fusion.35
  527.8 2.2 all-to-all-done.1
  530.8 4.5 all-to-all-start.3
  537.9 4.6 all-to-all-done.3
  547.4 757.6 %all-reduce.4.cloned.1.call-done = f32[1536,8450]{1,0:T(8,128)} async-done(((f32[1536,8450]{1,0:T(8,128)}), f32[1536,8450]{1,0:T(8,128)}) %all-reduce.4.cloned.1.call-update) | async-done | bytes 51916816
  1306.0 4.3 all-reduce.1
  1313.6 2.1 dynamic-slice_bitcast_fusion
  (295 shorter events, 73.9 us)
Async XLA Ops:
  7.2 13.1 copy-start
  7.2 87.4 %all-gather.3.cloned.1.call-start = ((), (), s32[]{:S(2)}) async-start(), calls=%async_computation.8 | async-start | bytes 7587840 | tf_op jit(solution)/shard_map/all_gather | solution.py:18
  11.7 225.5 %all-gather.5.cloned.1.call-start = ((), (), s32[]{:S(2)}) async-start(), calls=%async_computation.9 | async-start | bytes 19568640 | tf_op jit(solution)/shard_map/all_gather | solution.py:18
  20.4 86.7 %copy-start.71 = (f32[128]{0:T(128)}, f32[128]{0:T(128)S(1)}, u32[]{:S(2)}) copy-start(f32[128]{0:T(128)S(1)} %add_rsqrt_fusion.3) | copy-start | bytes 1540
  95.8 67.1 %copy-start.60 = (f32[1536]{0:T(1024)}, f32[1536]{0:T(1024)S(1)}, u32[]{:S(2)}) copy-start(f32[1536]{0:T(1024)S(1)} %convert_reduce_fusion.3) | copy-start | bytes 18436
  107.1 4.3 copy-start.9
  111.4 3.0 copy-start.41
  121.5 3.8 copy-start.30
  121.5 40.5 %all-to-all-start = ((f32[2,128,1536]{2,1,0:T(8,128)}), f32[2,128,1536]{2,1,0:T(8,128)S(1)}, u32[]{:S(2)}, u32[]{:S(2)}) async-start(f32[2,128,1536]{2,1,0:T(8,128)} %fusion.40), calls=%async_computation | async-start | bytes 3145728 | tf_op jit(solution)/shard_map/all_to_all | solution.py:33
  125.3 35.9 %copy-start.75 = (pred[256]{0:T(512)(128)(4,1)S(1)}, pred[256]{0:T(512)(128)(4,1)}, u32[]{:S(2)}) copy-start(pred[256]{0:T(512)(128)(4,1)} %iota_compare_fusion.1) | copy-start | bytes 772
  162.1 22.5 %copy-start.3 = (f32[128,1536]{1,0:T(8,128)}, f32[128,1536]{1,0:T(8,128)S(1)}, u32[]{:S(2)}) copy-start(f32[128,1536]{1,0:T(8,128)S(1)} %reduce_sum.190) | copy-start | bytes 2359300
  162.9 21.7 %copy-start.73 = (f32[128]{0:T(128)}, f32[128]{0:T(128)S(1)}, u32[]{:S(2)}) copy-start(f32[128]{0:T(128)S(1)} %add_rsqrt_fusion.1) | copy-start | bytes 1540
  182.5 5.0 copy-start.12
  199.0 34.3 %copy-start.67 = (f32[4,2,256]{2,1,0:T(2,128)S(1)}, f32[4,2,256]{2,1,0:T(2,128)}, u32[]{:S(2)}) copy-start(f32[4,2,256]{2,1,0:T(2,128)} %copy-done.66) | copy-start | bytes 24580
  199.0 34.3 %copy-start.76 = (f32[128]{0:T(128)S(1)}, f32[128]{0:T(128)}, u32[]{:S(2)}) copy-start(f32[128]{0:T(128)} %get-tuple-element.25) | copy-start | bytes 1540
  199.1 34.3 %copy-start.64 = (f32[4,2,256]{2,1,0:T(2,128)S(1)}, f32[4,2,256]{2,1,0:T(2,128)}, u32[]{:S(2)}) copy-start(f32[4,2,256]{2,1,0:T(2,128)} %copy-done.63) | copy-start | bytes 24580
  199.1 34.4 %all-to-all-start.2 = ((f32[2,128,1536]{2,1,0:T(8,128)}), f32[2,128,1536]{2,1,0:T(8,128)}, u32[]{:S(2)}, u32[]{:S(2)}) async-start(f32[2,128,1536]{2,1,0:T(8,128)} %fusion.38), calls=%async_computation.2 | async-start | bytes 3145728 | tf_op jit(solution)/shard_map/all_to_all | solution.py:33
  203.9 149.7 %reduce-scatter.5.cloned.1.call-start = ((), (), s32[]{:S(2)}) async-start(), calls=%async_computation.10 | async-start | bytes 2359296 | tf_op jit(solution)/shard_map/reduce_scatter | solution.py:205
  238.4 12.3 copy-start.25
  250.8 14.0 %copy-start.15 = (bf16[256,1536]{1,0:T(8,128)(2,1)}, bf16[256,1536]{1,0:T(8,128)(2,1)S(1)}, u32[]{:S(2)}) copy-start(bf16[256,1536]{1,0:T(8,128)(2,1)S(1)} %all_gather.35) | copy-start | bytes 2359300
  250.8 10.4 copy-start.68
  264.8 6.4 copy-start.53
  276.0 77.6 %reduce-scatter.9.cloned.1.call-start = ((), (), s32[]{:S(2)}) async-start(), calls=%async_computation.12 | async-start | bytes 2359296 | tf_op jit(solution)/shard_map/reduce_scatter | solution.py:205
  276.4 5.0 copy-start.16
  276.5 5.0 copy-start.54
  276.5 36.8 %slice-start.5 = ((s8[19267584]{0:T(1024)(128)(4,1)}), s8[4194304]{0:T(1024)(128)(4,1)S(1)}, s32[]{:S(2)}) async-start(s8[19267584]{0:T(1024)(128)(4,1)} %bitcast.367), calls=%async_computation.20 | async-start | bytes 8388608
  276.5 36.8 %slice-start.6 = ((s8[19267584]{0:T(1024)(128)(4,1)}), s8[4194304]{0:T(1024)(128)(4,1)S(1)}, s32[]{:S(2)}) async-start(s8[19267584]{0:T(1024)(128)(4,1)} %bitcast.367), calls=%async_computation.21 | async-start | bytes 8388608
  281.5 7.4 copy-start.46
  281.5 31.8 %slice-start.7 = ((s8[19267584]{0:T(1024)(128)(4,1)}), s8[4194304]{0:T(1024)(128)(4,1)S(1)}, s32[]{:S(2)}) async-start(s8[19267584]{0:T(1024)(128)(4,1)} %bitcast.367), calls=%async_computation.22 | async-start | bytes 8388608
  281.5 31.8 %slice-start.8 = ((s8[19267584]{0:T(1024)(128)(4,1)}), s8[4194304]{0:T(1024)(128)(4,1)S(1)}, s32[]{:S(2)}) async-start(s8[19267584]{0:T(1024)(128)(4,1)} %bitcast.367), calls=%async_computation.23 | async-start | bytes 8388608
  308.3 5.0 copy-start.8
  308.3 5.0 slice-start.9
  321.9 127.2 %reduce-scatter.7.cloned.1.call-start = ((), (), s32[]{:S(2)}) async-start(), calls=%async_computation.11 | async-start | bytes 1179648 | tf_op jit(solution)/shard_map/reduce_scatter | solution.py:261
  322.1 15.6 %slice-start = ((s8[12582912]{0:T(1024)(128)(4,1)}), s8[4194304]{0:T(1024)(128)(4,1)S(1)}, s32[]{:S(2)}) async-start(s8[12582912]{0:T(1024)(128)(4,1)} %bitcast.318), calls=%async_computation.15 | async-start | bytes 8388608
  325.6 12.2 slice-start.1
  325.6 12.2 slice-start.2
  353.6 3.3 copy-start.69
  353.6 3.3 copy-start.70
  353.6 3.2 copy-start.4
  353.6 3.2 copy-start.6
  353.6 3.2 copy-start.26
  353.6 3.2 copy-start.27
  353.6 3.2 copy-start.31
  376.0 2.4 copy-start.43
  392.8 10.9 slice-start.3
  398.0 5.7 slice-start.4
  406.8 43.5 %reduce-scatter.11.cloned.1.call-start = ((), (), s32[]{:S(2)}) async-start(), calls=%async_computation.13 | async-start | bytes 1179648 | tf_op jit(solution)/shard_map/reduce_scatter | solution.py:261
  406.9 2.7 copy-start.19
  411.9 2.9 copy-start.11
  412.0 2.9 copy-start.40
  419.1 885.9 %all-reduce.4.cloned.1.call-start = ((), (), s32[]{:S(2)}) async-start(), calls=%async_computation.14 | async-start | bytes 105381888
  434.5 3.2 copy-start.29
  434.5 3.2 copy-start.38
  441.8 6.1 copy-start.65
  441.8 8.5 copy-start.61
  441.8 8.5 copy-start.72
  441.8 8.5 copy-start.74
  447.9 5.3 copy-start.14
  513.0 9.1 copy-start.50
  518.6 11.3 all-to-all-start.1
  522.2 13.1 copy-start.77
  530.8 13.0 copy-start.5
  530.8 13.0 copy-start.7
  530.8 11.7 all-to-all-start.3
  (35 other events, 43.2 us)
Sparse Core Ops, SparseCore 0:
  11.8 82.7 all-gather.2
  97.7 131.5 all-gather.4
  276.1 34.4 reduce-scatter.4
  322.0 26.7 reduce-scatter.8
  406.9 20.0 reduce-scatter.6
  429.4 20.9 reduce-scatter.10
  512.0 793.0 all-reduce.3
where the time goes:
time: 1340 us; the launch traced here: 1320 us
  waiting for transfers between devices  839 us (63%)
  matrix products  157 us (12%)
  blocking collectives  145 us (11%)
  local copies, waits for them, and re-layouts  111 us (8%)
  other arithmetic  35.7 us (3%)
  starting transfers between devices  18 us (1%)
  between operations  16.4 us (1%)
    unnamed x8, waiting for transfers between devices  758 us
    all_gather x2, waiting for transfers between devices, turned_gather(): out, at, finished = (lax.all_gather(both, axis, axis=0, tiled=True), 0, [])  73.4 us
    all_gather x2, blocking collectives, body(): lax.all_gather(grad_out.astype(jnp.bfloat16), 'tensor', axis=0, tiled=True)  63.5 us
    dot_general x14, matrix products, outer_sum(): lax.dot_general(left, right, (((0,), (0,)), ((), ())), preferred_element_...  60.3 us
    concatenate x1, local copies, waits for them, and re-layouts, in_one_piece(): jnp.concatenate([a.reshape(*a.shape[:along], w) for a, w in zip(arrays, w...  58.6 us
    dot_general x14, matrix products, against(): lax.dot_general(left, right, (((1,), (1,)), ((), ())), preferred_element_...  36.4 us
    all_gather x2, blocking collectives, body(): lax.all_gather((unit_one * gain_one).astype(jnp.bfloat16), 'tensor', axis...  30.6 us
    all_gather x2, blocking collectives, body(): lax.all_gather((unit_two * gain_two).astype(jnp.bfloat16), 'tensor', axis...  29.4 us
  transfers between devices with their start and end apart: 11, of which 5 were waited for; matrix products, arithmetic and copies ran while one was open for 12% of the time, Pallas kernels for 0%

commit v1 on v0

v1 whole, which is shorter than its diff:
```python
import math

import jax
import jax.numpy as jnp
from jax import lax
from jax.experimental import pallas as pl
from jax.experimental.pallas import tpu as pltpu
from jax.sharding import Mesh
from jax.sharding import PartitionSpec as P

HEAD = 96
EPS = 1e-05
ROPE_BASE = 100000.0
AXES = ("yh", "x", "z", "core", "yl")
DP = ("yh", "x", "z", "core")
MESH = pl.DeviceIdType.MESH
BF = jnp.bfloat16
F32 = jnp.float32
ORDERS = (("x", "y", "z"), ("y", "z", "x"), ("z", "x", "y"))


def coordinates():
    x, z, yh, yl = (lax.axis_index(a) for a in ("x", "z", "yh", "yl"))
    return {"x": x, "z": z, "y": yh * 2 + yl}


def around(value, by):
    return lax.rem(value + (by + 4), 4)


def peer(at, axis, by):
    moved = around(at[axis], by)
    if axis == "y":
        return {"yh": moved // 2, "yl": lax.rem(moved, 2)}
    return {axis: moved}


def place(at, whole=(), half=None, moved=None):
    out = []
    for axis in ("y", "x", "z"):
        if axis in whole:
            if half is not None and half[0] == axis:
                out.append(pl.ds(2 * half[1], 2))
            else:
                out.append(pl.ds(0, 4))
        else:
            value = at[axis] if moved is None or moved[0] != axis else around(at[axis], moved[1])
            out.append(lax.rem(value, 2) * 2 + value // 2 if axis == "y" else value)
    return tuple(out)


def greet(at):
    barrier = pltpu.get_barrier_semaphore()
    for axis in ("x", "y", "z"):
        for by in (1, -1, 2):
            pl.semaphore_signal(barrier, inc=1, device_id=peer(at, axis, by), device_id_type=MESH)
    pl.semaphore_wait(barrier, 9)


def halved(order):
    return "x" if order[2] == "y" else "y"


def gather_kernel(*refs):
    srcs, outs = refs[:3], refs[3:6]
    local, send, recv, last_send, last_recv = refs[6:]
    at = coordinates()
    greet(at)
    own = []
    for p in range(3):
        copy = pltpu.make_async_copy(srcs[p], outs[p].at[place(at)], local.at[p])
        copy.start()
        own.append(copy)
    started = {}
    for stage in range(2):
        for p, order in enumerate(ORDERS):
            if stage:
                own[p].wait()
                for copy in started[p, stage - 1]:
                    copy.wait()
            group = outs[p].at[place(at, order[:stage])]
            started[p, stage] = []
            for d, by in enumerate((1, -1, 2)):
                copy = pltpu.make_async_remote_copy(
                    src_ref=group if stage else srcs[p],
                    dst_ref=group,
                    send_sem=send.at[p, stage, d],
                    recv_sem=recv.at[p, stage, d],
                    device_id=peer(at, order[stage], by),
                    device_id_type=MESH,
                )
                copy.start()
                started[p, stage].append(copy)
    final = {}
    for p, order in enumerate(ORDERS):
        for copy in started[p, 1]:
            copy.wait()
        for turn in range(2):
            for d, by in enumerate((1, -1)):
                h = turn if by == 1 else 1 - turn
                block = outs[p].at[place(at, order[:2], (halved(order), h))]
                copy = pltpu.make_async_remote_copy(
                    src_ref=block,
                    dst_ref=block,
                    send_sem=last_send.at[p, d, h],
                    recv_sem=last_recv.at[p, d, h],
                    device_id=peer(at, order[2], by),
                    device_id_type=MESH,
                )
                copy.start()
                final[p, d, h] = copy
    for p, order in enumerate(ORDERS):
        for d, by in enumerate((1, -1)):
            final[p, d, d].wait_recv()
            block = outs[p].at[
                place(at, order[:2], (halved(order), d), (order[2], -by))
            ]
            copy = pltpu.make_async_remote_copy(
                src_ref=block,
                dst_ref=block,
                send_sem=last_send.at[p, d, 2],
                recv_sem=last_recv.at[p, d, 2],
                device_id=peer(at, order[2], by),
                device_id_type=MESH,
            )
            copy.start()
            final[p, d, 2] = copy
    for p in range(3):
        for d in range(2):
            final[p, d, 0].wait_send()
            final[p, d, 1].wait_send()
            final[p, d, 1 - d].wait_recv()
            final[p, d, 2].wait()


def gathered(pieces, collective_id, name):
    anywhere = pl.BlockSpec(memory_space=pl.ANY)
    size = sum(p.size for p in pieces) * 128
    return pl.pallas_call(
        gather_kernel,
        out_shape=[jax.ShapeDtypeStruct((4, 4, 4) + p.shape, p.dtype) for p in pieces],
        in_specs=[anywhere] * 3,
        out_specs=[anywhere] * 3,
        scratch_shapes=[
            pltpu.SemaphoreType.DMA((3,)),
            pltpu.SemaphoreType.DMA((3, 2, 3)),
            pltpu.SemaphoreType.DMA((3, 2, 3)),
            pltpu.SemaphoreType.DMA((3, 2, 3)),
            pltpu.SemaphoreType.DMA((3, 2, 3)),
        ],
        compiler_params=pltpu.CompilerParams(collective_id=collective_id, has_side_effects=True),
        cost_estimate=pl.CostEstimate(flops=0, bytes_accessed=2 * size, transcendentals=0),
        name=name,
    )(*pieces)


def reduce_kernel(widths, *refs):
    parts = len(widths)
    ins = refs[: 6 * parts]
    outs = refs[6 * parts : 6 * parts + 3]
    data, far, near, second, third = (refs[6 * parts + 3 + 3 * k : 6 * parts + 6 + 3 * k] for k in range(5))
    load, first_send, first_recv, send, recv = refs[6 * parts + 18 :]
    at = coordinates()
    loads = []
    for p in range(3):
        for yl in range(2):
            column = 0
            for k, width in enumerate(widths):
                copy = pltpu.make_async_copy(
                    ins[(p * 2 + yl) * parts + k],
                    data[p].at[pl.ds(2 * yl, 2), :, :, :, pl.ds(column, width)],
                    load.at[p, yl, k],
                )
                copy.start()
                loads.append(copy)
                column += width
    greet(at)
    for copy in loads:
        copy.wait()

    def sent(src, dst, s, r, axis, by):
        copy = pltpu.make_async_remote_copy(
            src_ref=src, dst_ref=dst, send_sem=s, recv_sem=r, device_id=peer(at, axis, by), device_id_type=MESH
        )
        copy.start()
        return copy

    opposite, neighbour = {}, {}
    for p, order in enumerate(ORDERS):
        axis = order[2]
        for d, by in enumerate((1, -1)):
            block = data[p].at[place(at, order[:2], (halved(order), d), (axis, 2))]
            opposite[p, d] = sent(block, far[p].at[d], first_send.at[p, d, 0], first_recv.at[p, d, 0], axis, by)
        for d, by in enumerate((1, -1)):
            h = 1 - d
            block = data[p].at[place(at, order[:2], (halved(order), h), (axis, by))]
            neighbour[p, d, 1] = sent(
                block, near[p].at[d, pl.ds(2 * h, 2)], first_send.at[p, d, 1], first_recv.at[p, d, 1], axis, by
            )
    for p, order in enumerate(ORDERS):
        axis = order[2]
        for d, by in enumerate((1, -1)):
            opposite[p, d].wait_recv()
            where = place(at, order[:2], (halved(order), d), (axis, by))
            block = data[p].at[where]

            @pl.loop(0, 8)
            def _(i, p=p, d=d, block=block):
                a, b = i // 4, lax.rem(i, 4)
                total = block[a, b].astype(F32) + far[p][d, a, b].astype(F32)
                block[a, b] = total.astype(BF)

            neighbour[p, d, 0] = sent(
                block, near[p].at[d, pl.ds(2 * d, 2)], first_send.at[p, d, 2], first_recv.at[p, d, 2], axis, by
            )
    later = {}
    for p, order in enumerate(ORDERS):
        for d in range(2):
            for h in range(2):
                neighbour[p, d, h].wait_recv()
        block = data[p].at[place(at, order[:2])]

        @pl.loop(0, 16)
        def _(i, p=p, block=block):
            a, b = i // 4, lax.rem(i, 4)
            total = block[a, b].astype(F32) + near[p][0, a, b].astype(F32) + near[p][1, a, b].astype(F32)
            block[a, b] = total.astype(BF)

        for d, by in enumerate((1, -1, 2)):
            later[p, 0, d] = sent(
                data[p].at[place(at, order[:1], None, (order[1], by))],
                second[p].at[d],
                send.at[p, 0, d],
                recv.at[p, 0, d],
                order[1],
                by,
            )
    for p, order in enumerate(ORDERS):
        for d in range(3):
            later[p, 0, d].wait_recv()
        block = data[p].at[place(at, order[:1])]

        @pl.loop(0, 4)
        def _(i, p=p, block=block):
            total = block[i].astype(F32)
            for d in range(3):
                total = total + second[p][d, i].astype(F32)
            block[i] = total.astype(BF)

        for d, by in enumerate((1, -1, 2)):
            later[p, 1, d] = sent(
                data[p].at[place(at, (), None, (order[0], by))],
                third[p].at[d],
                send.at[p, 1, d],
                recv.at[p, 1, d],
                order[0],
                by,
            )
    for p, order in enumerate(ORDERS):
        for d in range(3):
            later[p, 1, d].wait_recv()
        total = data[p][place(at)].astype(F32)
        for d in range(3):
            total = total + third[p][d].astype(F32)
        outs[p][...] = total
    for copy in (*opposite.values(), *neighbour.values(), *later.values()):
        copy.wait_send()


def reduced(pieces, widths, collective_id, name):
    anywhere = pl.BlockSpec(memory_space=pl.ANY)
    whole = sum(widths)
    flat = [array for piece in pieces for half in piece for array in half]

    def per_piece(*shape):
        return [pltpu.VMEM(shape + (48, whole), BF) for _ in range(3)]

    return pl.pallas_call(
        lambda *refs: reduce_kernel(widths, *refs),
        out_shape=[jax.ShapeDtypeStruct((48, whole), F32)] * 3,
        in_specs=[anywhere] * len(flat),
        out_specs=[pl.BlockSpec(memory_space=pltpu.VMEM)] * 3,
        scratch_shapes=[
            *per_piece(4, 4, 4),
            *per_piece(2, 2, 4),
            *per_piece(2, 4, 4),
            *per_piece(3, 4),
            *per_piece(3),
            pltpu.SemaphoreType.DMA((3, 2, len(widths))),
            pltpu.SemaphoreType.DMA((3, 2, 3)),
            pltpu.SemaphoreType.DMA((3, 2, 3)),
            pltpu.SemaphoreType.DMA((3, 2, 3)),
            pltpu.SemaphoreType.DMA((3, 2, 3)),
        ],
        compiler_params=pltpu.CompilerParams(
            collective_id=collective_id, has_side_effects=True, vmem_limit_bytes=60 * 1024 * 1024
        ),
        name=name,
    )(*flat)


def rope_tables(count):
    half = HEAD // 2
    inverse = ROPE_BASE ** (-(jnp.arange(half, dtype=F32) * 2.0) / HEAD)
    angle = jnp.arange(count, dtype=F32)[:, None] * inverse[None, :]
    cosine, sine = jnp.cos(angle), jnp.sin(angle)
    return jnp.concatenate([cosine, cosine], -1), jnp.concatenate([sine, sine], -1)


def rotary(values, cosine, sine):
    half = HEAD // 2
    turned = jnp.concatenate([-values[..., half:], values[..., :half]], -1)
    return values * cosine + turned * sine


def rotary_back(grads, cosine, sine):
    half = HEAD // 2
    shifted = grads * sine
    turned = jnp.concatenate([shifted[..., half:], -shifted[..., :half]], -1)
    return grads * cosine + turned


def normalize(values):
    inverse = lax.rsqrt(jnp.mean(values * values, -1, keepdims=True) + EPS)
    return values * inverse, inverse


def norm_back(grad, unit, inverse, gain):
    scaled = grad * gain
    return inverse * (scaled - unit * jnp.mean(scaled * unit, -1, keepdims=True))


def dot(spec, left, right, kind=F32):
    return jnp.einsum(spec, left, right, preferred_element_type=kind)


def body(
    inputs,
    out_grad,
    lengths,
    query_weight,
    key_matrix,
    value_matrix,
    output_weight,
    gate_weight,
    up_weight,
    down_weight,
    attn_gain,
    mlp_gain,
):
    rows, width = inputs.shape[1:]
    slots = 2 * rows
    core = lax.axis_index("core")
    yl = lax.axis_index("yl")

    def halves(weight):
        return weight.reshape(weight.shape[0], 2, -1)

    blocks = [
        halves(query_weight),
        halves(key_matrix),
        halves(value_matrix),
        halves(output_weight.T),
        halves(gate_weight),
        halves(up_weight),
        halves(down_weight.T),
    ]
    sizes = [b.shape[2] for b in blocks]
    packed = jnp.moveaxis(jnp.concatenate(blocks, -1), 1, 0)
    packed = lax.all_to_all(packed, "core", 0, 0, tiled=True).reshape(48, -1)
    gains = lax.all_gather(jnp.stack([attn_gain, mlp_gain], 1), DP, axis=0, tiled=True).astype(F32)
    gain_one, gain_two = gains[:, 0], gains[:, 1]
    third = sizes[0]
    attn_pieces = [packed[:, k * third : (k + 1) * third] for k in range(3)]
    wide = sizes[4]
    mlp_pieces = [packed[:, 3 * third + k * wide : 3 * third + (k + 1) * wide] for k in range(3)]

    both = jnp.stack([inputs, out_grad], 1)
    both = lax.all_to_all(both, "yl", 0, 2, tiled=True)
    both = lax.all_gather(both, "core", axis=0, tiled=True)
    length = lax.all_gather(lax.dynamic_index_in_dim(lengths, yl, 0), "core", axis=0, tiled=True)[:, 0]
    in_rows = both[:, 0].astype(F32)
    valid = (jnp.arange(slots)[None, :] < length[:, None]).astype(F32)
    grad_out = both[:, 1].astype(F32) * valid[:, :, None]

    attn_full = gathered(attn_pieces, 1, "gather_attn")
    mlp_full = gathered([lax.optimization_barrier((p, attn_full[0]))[0] for p in mlp_pieces], 2, "gather_mlp")
    full_query, full_kv, full_output = (w.reshape(2, width, -1) for w in attn_full)
    full_gate, full_up, full_down = (w.reshape(2, width, -1) for w in mlp_full)

    cosine, sine = rope_tables(slots)
    cosine, sine = cosine[:, None, :], sine[:, None, :]
    scale = 1.0 / math.sqrt(HEAD)

    unit_one, inverse_one = normalize(in_rows)
    normed_one = (unit_one * gain_one).astype(BF).reshape(2 * slots, width)
    normed_pair = jnp.broadcast_to(normed_one, (2,) + normed_one.shape)
    query = dot("ytm,ymc->ytc", normed_pair, full_query)
    query = rotary(query.reshape(2, 2, slots, -1, HEAD), cosine, sine).astype(BF)
    kv = dot("ytm,ymc->ytc", normed_pair, full_kv)
    key = rotary(kv[..., : sizes[1]].reshape(2, 2, slots, -1, HEAD), cosine, sine).astype(BF)
    value = kv[..., sizes[1] :].reshape(2, 2, slots, -1, HEAD).astype(BF)
    heads_kv = key.shape[3]
    query = query.reshape(2, 2, slots, heads_kv, -1, HEAD)
    positions = jnp.arange(slots)
    keep = (positions[None, None, :] <= positions[None, :, None]) & (
        positions[None, None, :] < length[:, None, None]
    )
    keep = keep[None, :, None, None]
    scores = dot("yntkgd,ynskd->ynkgts", query, key) * scale
    scores = jnp.where(keep, scores, -1e30)
    row_max = jnp.max(scores, -1, keepdims=True)
    terms = jnp.exp(scores - row_max)
    probs = terms / jnp.sum(terms, -1, keepdims=True)
    probs_low = probs.astype(BF)
    mixed = dot("ynkgts,ynskd->yntkgd", probs_low, value).astype(BF).reshape(2, 2 * slots, -1)
    attn_part = dot("ytc,ymc->tm", mixed, full_output).astype(BF)
    attn_out = lax.psum(attn_part, "core").astype(F32).reshape(2, slots, width)
    hidden = in_rows + attn_out
    unit_two, inverse_two = normalize(hidden)
    normed_two = (unit_two * gain_two).astype(BF).reshape(2 * slots, width)

    normed_pair_two = jnp.broadcast_to(normed_two, (2,) + normed_two.shape)
    gate = dot("ytm,ymc->ytc", normed_pair_two, full_gate)
    up = dot("ytm,ymc->ytc", normed_pair_two, full_up)
    sigma = jax.nn.sigmoid(gate)
    active = (gate * sigma * up).astype(BF)
    mlp_part = dot("ytc,ymc->tm", active, full_down).astype(BF).reshape(2, slots, width)
    mlp_out = lax.psum_scatter(mlp_part, "core", scatter_dimension=0, tiled=True)[0].astype(F32)
    own_hidden = lax.dynamic_index_in_dim(hidden, core, 0, False)
    result = (own_hidden + mlp_out).astype(BF).reshape(2, rows, width)
    result = lax.all_to_all(result, "yl", 0, 0, tiled=True)

    cotangent = grad_out.astype(BF).reshape(2 * slots, width)
    cotangent_pair = jnp.broadcast_to(cotangent, (2,) + cotangent.shape)
    down_part = dot("ytm,ytc->ymc", cotangent_pair, active, BF)
    grad_active = dot("ytm,ymc->ytc", cotangent_pair, full_down)
    grad_gate = (grad_active * up * sigma * (1.0 + gate * (1.0 - sigma))).astype(BF)
    grad_up = (grad_active * gate * sigma).astype(BF)
    gate_part = dot("ytm,ytc->ymc", normed_pair_two, grad_gate, BF)
    up_part = dot("ytm,ytc->ymc", normed_pair_two, grad_up, BF)
    grad_two = dot("ytc,ymc->tm", grad_gate, full_gate) + dot("ytc,ymc->tm", grad_up, full_up)
    grad_two = lax.psum(grad_two.astype(BF), "core").astype(F32).reshape(2, slots, width)
    gain_two_part = jnp.sum(grad_two * unit_two, (0, 1))
    grad_hidden = grad_out + norm_back(grad_two, unit_two, inverse_two, gain_two)

    branch = grad_hidden.astype(BF).reshape(2 * slots, width)
    branch_pair = jnp.broadcast_to(branch, (2,) + branch.shape)
    output_part = dot("ytm,ytc->ymc", branch_pair, mixed, BF)
    grad_mixed = dot("ytm,ymc->ytc", branch_pair, full_output).astype(BF)
    grad_mixed = grad_mixed.reshape(2, 2, slots, heads_kv, -1, HEAD)
    grad_probs = dot("yntkgd,ynskd->ynkgts", grad_mixed, value)
    grad_scores = (probs * (grad_probs - jnp.sum(grad_probs * probs, -1, keepdims=True))).astype(BF)
    grad_query = dot("ynkgts,ynskd->yntkgd", grad_scores, key) * scale
    grad_key = dot("ynkgts,yntkgd->ynskd", grad_scores, query) * scale
    grad_value = dot("ynkgts,yntkgd->ynskd", probs_low, grad_mixed)
    query_back = rotary_back(grad_query.reshape(2, 2, slots, -1, HEAD), cosine, sine).astype(BF)
    query_back = query_back.reshape(2, 2 * slots, -1)
    key_back = rotary_back(grad_key, cosine, sine).astype(BF).reshape(2, 2 * slots, -1)
    kv_back = jnp.concatenate([key_back, grad_value.astype(BF).reshape(2, 2 * slots, -1)], -1)
    query_part = dot("ytm,ytc->ymc", normed_pair, query_back, BF)
    kv_part = dot("ytm,ytc->ymc", normed_pair, kv_back, BF)
    grad_one = dot("ytc,ymc->tm", query_back, full_query) + dot("ytc,ymc->tm", kv_back, full_kv)
    grad_one = lax.psum_scatter(
        grad_one.astype(BF).reshape(2, slots, width), "core", scatter_dimension=0, tiled=True
    )[0].astype(F32)
    own_unit = lax.dynamic_index_in_dim(unit_one, core, 0, False)
    own_inverse = lax.dynamic_index_in_dim(inverse_one, core, 0, False)
    own_grad_hidden = lax.dynamic_index_in_dim(grad_hidden, core, 0, False)
    own_grad_two = lax.dynamic_index_in_dim(grad_two, core, 0, False)
    own_unit_two = lax.dynamic_index_in_dim(unit_two, core, 0, False)
    gain_one_part = jnp.sum(grad_one * own_unit, 0)
    gain_two_part = jnp.sum(own_grad_two * own_unit_two, 0)
    in_grad = own_grad_hidden + norm_back(grad_one, own_unit, own_inverse, gain_one)
    in_grad = lax.all_to_all(in_grad.reshape(2, rows, width), "yl", 0, 0, tiled=True)

    def blocked(part):
        parts = part.reshape(2, 2, 4, 4, 48, -1)
        return parts[0], parts[1]

    pieces = []
    for wide_part, thin_part in ((gate_part, query_part), (up_part, kv_part), (down_part, output_part)):
        wide_parts, thin_parts = blocked(wide_part), blocked(thin_part)
        pieces.append([[wide_parts[0], thin_parts[0]], [wide_parts[1], thin_parts[1]]])
    sums = reduced(pieces, (wide, third), 3, "reduce_grads")
    mine = jnp.concatenate(
        [sums[0][:, wide:], sums[1][:, wide:], sums[2][:, wide:], sums[0][:, :wide], sums[1][:, :wide], sums[2][:, :wide]],
        -1,
    )
    mine = lax.all_to_all(mine.reshape(2, 24, -1), "core", 0, 0, tiled=True)
    shards, start = [], 0
    for size in sizes:
        shards.append(jnp.concatenate([mine[0, :, start : start + size], mine[1, :, start : start + size]], -1))
        start += size
    gain_sums = lax.psum_scatter(
        lax.psum(jnp.stack([gain_one_part, gain_two_part], 1), "yl"), DP, scatter_dimension=0, tiled=True
    )
    return (
        result,
        in_grad,
        shards[0],
        shards[1],
        shards[2],
        shards[3].T,
        shards[4],
        shards[5],
        shards[6].T,
        gain_sums[:, 0],
        gain_sums[:, 1],
    )


def solution(mesh):
    fine = Mesh(mesh.devices.reshape(2, 4, 4, 2, 2), AXES)
    rows = P(None, AXES, None)
    into, out = P(DP, "yl"), P("yl", DP)
    return jax.shard_map(
        body,
        mesh=fine,
        in_specs=(rows, rows, P(None, DP), into, into, into, out, into, into, out, P(DP), P(DP)),
        out_specs=(rows, rows, into, into, into, out, into, into, out, P(DP), P(DP)),
        check_vma=False,
    )
```

time: 1340 us -> 973 us (0.73)
  waiting for transfers between devices: 839 us -> 6.59 us
  blocking collectives: 145 us -> 455 us
  Pallas kernels: 0 us -> 228 us
  matrix products: 157 us -> 88.3 us
  other arithmetic: 35.7 us -> 58.8 us
  local copies, waits for them, and re-layouts: 111 us -> 89.2 us
    unnamed x8 -> x5, waiting for transfers between devices: 758 us -> 0.08 us
    unnamed x0 -> x2, blocking collectives: none -> 322 us
    pallas_call x0 -> x3, Pallas kernels: none -> 228 us  [the longest x2 115 us: gathered(): pl.pallas_call(gather_kernel, out_shape=[jax.ShapeDtypeStruct((4, 4, 4) +...]
    all_gather x2 -> x1, waiting for transfers between devices: 73.4 us -> 0.01 us  [body(): both = lax.all_gather(both, 'core', axis=0, tiled=True)]
    dot_general x54 -> x24, matrix products: 157 us -> 88.3 us  [dot(): return jnp.einsum(spec, left, right, preferred_element_type=kind)]
    concatenate x2 -> x3, local copies, waits for them, and re-layouts: 58.6 us -> 5.03 us  [the longest x1 3.48 us: rotary_back(): turned = jnp.concatenate([shifted[..., half:], -shifted[..., :half]], -1)]
    all_gather x8 -> x1, blocking collectives: 141 us -> 96.7 us  [body(): lax.all_gather(jnp.stack([attn_gain, mlp_gain], 1), DP, axis=0, tiled=True)]
    all_to_all x0 -> x2, blocking collectives: none -> 32.9 us  [the longest x1 21.5 us: body(): both = lax.all_to_all(both, 'yl', 0, 2, tiled=True)]
  transfers between devices with their start and end apart: 11 -> 8, of which waited for: 5 -> 1; matrix products, arithmetic and copies ran while one was open for 12% -> 14% of each run, Pallas kernels for 0% -> 24%
where the time goes in v1:
time: 973 us; the launch traced here: 955 us
  blocking collectives  455 us (47%)
  Pallas kernels  228 us (23%)
  local copies, waits for them, and re-layouts  89.2 us (9%)
  matrix products  88.3 us (9%)
  other arithmetic  58.8 us (6%)
  between operations  15.6 us (2%)
  starting transfers between devices  12.9 us (1%)
    unnamed x2, blocking collectives  322 us
    pallas_call x2, Pallas kernels, gathered(): pl.pallas_call(gather_kernel, out_shape=[jax.ShapeDtypeStruct((4, 4, 4) +...  115 us
    pallas_call x1, Pallas kernels, reduced(): pl.pallas_call(lambda *refs: reduce_kernel(widths, *refs), out_shape=[jax...  113 us
    all_gather x1, blocking collectives, body(): lax.all_gather(jnp.stack([attn_gain, mlp_gain], 1), DP, axis=0, tiled=True)  96.7 us
    dot_general x24, matrix products, dot(): return jnp.einsum(spec, left, right, preferred_element_type=kind)  88.3 us
    all_to_all x1, blocking collectives, body(): both = lax.all_to_all(both, 'yl', 0, 2, tiled=True)  21.5 us
    slice x6, local copies, waits for them, and re-layouts, blocked(): return (parts[0], parts[1])  21.3 us
  transfers between devices with their start and end apart: 8, of which 1 were waited for; matrix products, arithmetic and copies ran while one was open for 14% of the time, Pallas kernels for 24%

profile of v1, /device:TPU:1, one launch (start us, length us, event | category | flops | bytes accessed | tf_op | source)
XLA Modules:
  0.0 955.0 jit_solution(1836450942192353873)
XLA Ops:
  8.7 21.5 %all_to_all.38 = bf16[2,2,128,1536]{3,2,1,0:T(8,128)(2,1)S(1)} all-to-all(bf16[2,2,128,1536]{3,2,1,0:T(8,128)(2,1)S(1)} %pad_maximum_fusion), channel_id=1, replica_groups=mesh['yh'=2,'x'=4,'z'=4,'core'=2,'yl'=2] {'yl'}, dimensions={0} | all-to-all | bytes 3145728 | tf_op jit(solution)/shard_map/all_to_all | solution.py:379
  34.2 5.3 all-to-all-start.1
  39.5 1.8 all-reduce
  41.3 96.7 %all-gather = bf16[64,24,2]{1,2,0:T(2,128)(2,1)S(1)} all-gather(bf16[1,24,2]{1,2,0:T(2,128)(2,1)S(1)} %maximum_bitcast_fusion.2), channel_id=1, replica_groups=mesh['yh'=2,'x'=4,'z'=4,'core'=2,'yl'=2] {'yh','x','z','core'}, dimensions={0}, use_global_device_ids=true | all-gather | bytes 6240 | tf_op jit(solution)/shard_map/all_gather | solution.py:371
  139.1 34.8 %gather_attn.1 = (bf16[4,4,4,48,384]{4,3,2,1,0:T(8,128)(2,1)}, bf16[4,4,4,48,384]{4,3,2,1,0:T(8,128)(2,1)}, bf16[4,4,4,48,384]{4,3,2,1,0:T(8,128)(2,1)}) custom-call(bf16[48,384]{1,0:T(8,128)(2,1)} %get-tuple-element.90.refs_0_, bf16[48,384]{1,0:T(8,128)(2,1)} %get-tuple-element.89.refs_1_, bf16[48,384]{1,0:T(8,128)(2,1)} %get-tuple-element.88.refs_2_), custom_call_target="tpu_custom_call" | custom-call | bytes 14155776 | tf_op jit(solution)/shard_map/gather_attn/pallas_call | solution.py:139
  176.4 1.8 multiply_reduce_fusion.2
  178.8 1.8 fusion.8
  180.7 2.1 copy.251
  182.8 3.6 fusion.43
  187.4 2.1 reshape.366
  189.5 3.6 fusion.45
  198.6 2.0 fusion.20
  207.1 4.5 fusion.11
  211.9 1.9 fusion.82
  217.7 80.5 %gather_mlp.1 = (bf16[4,4,4,48,1024]{4,3,2,1,0:T(8,128)(2,1)}, bf16[4,4,4,48,1024]{4,3,2,1,0:T(8,128)(2,1)}, bf16[4,4,4,48,1024]{4,3,2,1,0:T(8,128)(2,1)}) custom-call(bf16[48,1024]{1,0:T(8,128)(2,1)} %get-tuple-element.26.refs_0_, bf16[48,1024]{1,0:T(8,128)(2,1)} %get-tuple-element.27.refs_1_, bf16[48,1024]{1,0:T(8,128)(2,1)} %get-tuple-element.28.refs_2_), custom_call_target="tpu_custom_call" | custom-call | bytes 37748736 | tf_op jit(solution)/shard_map/gather_mlp/pallas_call | solution.py:139
  300.8 3.5 convert_bitcast_fusion
  304.3 2.0 multiply_reduce_fusion.1
  306.9 3.9 fusion.13
  310.8 2.6 copy.272
  313.4 2.6 copy.275
  316.0 6.2 fusion.35
  322.3 8.0 fusion.29
  330.3 8.6 multiply_convert_fusion.1
  338.9 3.4 convolution_bitcast_fusion.2
  342.4 5.4 fusion.31
  347.8 5.5 fusion.33
  353.3 4.6 fusion.12
  358.5 6.1 fusion.76
  364.7 6.9 fusion.75
  371.5 3.6 fusion.27
  375.2 3.4 fusion.74
  378.6 4.6 fusion.10
  383.3 4.6 broadcast_multiply_fusion
  387.9 2.9 multiply_reduce_fusion
  390.9 3.0 add_convert_fusion
  393.9 1.7 copy.277
  395.6 4.4 fusion.47
  400.0 3.7 reshape.415
  403.7 1.9 copy.281
  405.6 5.3 fusion.1
  412.6 3.2 fusion.23
  415.8 3.0 fusion.3
  421.8 1.9 pad_maximum_fusion.1
  423.7 3.5 concatenate.63
  427.2 3.8 copy.283
  431.0 3.4 reshape.377
  436.5 2.2 reshape.410
  438.7 2.0 copy.322
  440.7 2.1 reshape.411
  442.8 1.7 add_convert_fusion.1
  445.4 1.8 fusion.41
  447.3 1.9 fusion.39
  455.0 112.9 %reduce_grads.1 = (f32[48,1408]{1,0:T(8,128)}, f32[48,1408]{1,0:T(8,128)}, f32[48,1408]{1,0:T(8,128)}) custom-call(bf16[2,4,4,48,1024]{4,3,2,1,0:T(8,128)(2,1)} %bitcast.300, bf16[2,4,4,48,384]{4,3,2,1,0:T(8,128)(2,1)} %bitcast.313, bf16[2,4,4,48,1024]{4,3,2,1,0:T(8,128)(2,1)} %bitcast.299, bf16[2,4,4,48,384]{4,3,2,1,0:T(8,128)(2,1)} %bitcast.312, ...), custom_call_target="tpu_custom_call" | custom-call | tf_op jit(solution)/shard_map/reduce_grads/pallas_call | solution.py:278
  569.5 3.3 convolution_bitcast_fusion
  572.7 2.7 fusion.9
  578.7 3.2 multiply_reduce_fusion.3
  585.4 11.4 %all_to_all.39 = f32[2,24,4224]{2,1,0:T(8,128)S(1)} all-to-all(f32[2,24,4224]{2,1,0:T(8,128)} %bitcast.73), channel_id=1, replica_groups=mesh['yh'=2,'x'=4,'z'=4,'core'=2,'yl'=2] {'core'}, dimensions={0} | all-to-all | bytes 1622016 | tf_op jit(solution)/shard_map/all_to_all | solution.py:490
  601.1 2.2 add_convert_fusion.2
  603.3 3.5 all-to-all-start.2
  606.9 2.4 fusion.22
  610.9 6.5 all-to-all-done.2
  617.3 3.7 all-to-all-start.3
  621.7 320.2 %all-reduce.1 = f32[1536,2]{0,1:T(2,128)S(1)} all-reduce(f32[1536,2]{0,1:T(2,128)S(1)} %pad_maximum_fusion.12), channel_id=4, replica_groups=mesh['yh'=2,'x'=4,'z'=4,'core'=2,'yl'=2] {'yh','x','z','core'}, use_global_device_ids=true, to_apply=%region_14.15.clone | all-reduce | flops 3072 | bytes 24576
  942.0 3.8 psum.24
  (250 shorter events, 60.7 us)
Async XLA Ops:
  7.2 169.3 %all-gather.3.cloned.1.call-start = ((), (), s32[]{:S(2)}) async-start(), calls=%async_computation.7 | async-start | bytes 4718592 | tf_op jit(solution)/shard_map/all_gather | solution.py:380
  30.2 2.2 copy-start.57
  30.3 3.0 copy-start.45
  30.3 3.0 copy-start.46
  30.3 3.0 copy-start.43
  30.3 3.0 copy-start.44
  31.6 9.8 %copy-start.59 = (bf16[24]{0:T(256)(128)(2,1)S(1)}, bf16[24]{0:T(256)(128)(2,1)}, u32[]{:S(2)}) copy-start(bf16[24]{0:T(256)(128)(2,1)} %param.23) | copy-start | bytes 148
  31.6 9.8 %copy-start.60 = (bf16[24]{0:T(256)(128)(2,1)S(1)}, bf16[24]{0:T(256)(128)(2,1)}, u32[]{:S(2)}) copy-start(bf16[24]{0:T(256)(128)(2,1)} %param.22) | copy-start | bytes 148
  34.2 104.2 %all-to-all-start.1 = ((bf16[2,24,4224]{2,1,0:T(8,128)(2,1)}), bf16[2,24,4224]{2,1,0:T(8,128)(2,1)S(1)}, u32[]{:S(2)}, u32[]{:S(2)}) async-start(bf16[2,24,4224]{2,1,0:T(8,128)(2,1)} %bitcast.12), calls=%async_computation.1 | async-start | bytes 811008 | tf_op jit(solution)/shard_map/all_to_all | solution.py:370
  39.5 264.8 %all-reduce.5.cloned.1.call-start = ((), (), s32[]{:S(2)}) async-start(), calls=%async_computation.8 | async-start | bytes 3145728 | tf_op jit(solution)/shard_map/psum | solution.py:418
  138.4 40.5 %copy-start.19 = (bf16[2,24,4224]{2,1,0:T(8,128)(2,1)}, bf16[2,24,4224]{2,1,0:T(8,128)(2,1)S(1)}, u32[]{:S(2)}) copy-start(bf16[2,24,4224]{2,1,0:T(8,128)(2,1)S(1)} %all-to-all-done.1) | copy-start | bytes 1216516
  174.0 6.7 copy-start.39
  195.4 3.2 copy-start.11
  203.8 2.0 copy-start.13
  203.8 2.0 copy-start.51
  207.1 4.5 copy-start.29
  211.7 89.1 %copy-start = (bf16[2,2,256,1536]{3,2,1,0:T(8,128)(2,1)S(1)}, bf16[2,2,256,1536]{3,2,1,0:T(8,128)(2,1)}, u32[]{:S(2)}) copy-start(bf16[2,2,256,1536]{3,2,1,0:T(8,128)(2,1)} %all-gather.3.cloned.1.call-done) | copy-start | bytes 9437188
  211.7 176.2 %all-reduce.7.cloned.1.call-start = ((), (), s32[]{:S(2)}) async-start(), calls=%async_computation.10 | async-start | bytes 3145728 | tf_op jit(solution)/shard_map/psum | solution.py:443
  211.9 95.0 %copy-start.49 = (f32[1,2,2,128]{3,1,2,0:T(2,128)}, f32[1,2,2,128]{3,1,2,0:T(2,128)S(1)}, u32[]{:S(2)}) copy-start(f32[1,2,2,128]{3,1,2,0:T(2,128)S(1)} %copy.336) | copy-start | bytes 6148
  316.0 6.2 copy-start.22
  316.0 14.3 %slice-start.2 = ((s8[6291456]{0:T(1024)(128)(4,1)}), s8[4194304]{0:T(1024)(128)(4,1)S(1)}, s32[]{:S(2)}) async-start(s8[6291456]{0:T(1024)(128)(4,1)} %bitcast.342), calls=%async_computation.14 | async-start | bytes 8388608
  322.2 8.1 copy-start.24
  322.2 8.1 slice-start.3
  322.3 16.7 %slice-start.4 = ((s8[6291456]{0:T(1024)(128)(4,1)}), s8[4194304]{0:T(1024)(128)(4,1)S(1)}, s32[]{:S(2)}) async-start(s8[6291456]{0:T(1024)(128)(4,1)} %bitcast.347), calls=%async_computation.16 | async-start | bytes 8388608
  330.3 8.6 slice-start.5
  342.4 5.4 copy-start.62
  353.3 4.7 copy-start.53
  357.9 243.2 %reduce-scatter.4.cloned.1.call-start = ((), (), s32[]{:S(2)}) async-start(), calls=%async_computation.9 | async-start | bytes 2359296 | tf_op jit(solution)/shard_map/reduce_scatter | solution.py:429
  364.6 6.9 copy-start.23
  364.6 6.9 copy-start.63
  364.6 13.9 %slice-start = ((s8[6291456]{0:T(1024)(128)(4,1)}), s8[4194304]{0:T(1024)(128)(4,1)S(1)}, s32[]{:S(2)}) async-start(s8[6291456]{0:T(1024)(128)(4,1)} %bitcast.339), calls=%async_computation.12 | async-start | bytes 8388608
  371.5 7.1 slice-start.1
  383.2 223.6 %reduce-scatter.6.cloned.1.call-start = ((), (), s32[]{:S(2)}) async-start(), calls=%async_computation.11 | async-start | bytes 2359296 | tf_op jit(solution)/shard_map/reduce_scatter | solution.py:464
  387.9 3.0 copy-start.1
  387.9 3.0 copy-start.3
  387.9 3.0 copy-start.50
  400.0 5.6 copy-start.35
  400.0 5.6 copy-start.52
  405.6 5.4 copy-start.14
  405.6 5.4 copy-start.28
  412.6 3.2 copy-start.15
  419.3 2.5 copy-start.2
  430.9 3.4 copy-start.8
  430.9 3.4 copy-start.25
  435.4 7.4 copy-start.9
  435.4 7.4 copy-start.10
  442.8 2.6 copy-start.21
  445.4 1.8 copy-start.32
  449.1 2.5 copy-start.18
  569.5 3.3 copy-start.27
  569.5 3.3 copy-start.58
  576.8 1.9 copy-start.6
  576.8 1.9 copy-start.55
  576.8 1.9 copy-start.56
  578.7 3.3 copy-start.37
  578.7 3.9 copy-start.36
  578.7 4.6 copy-start.38
  585.4 15.6 %copy-start.5 = (f32[2,256,1536]{2,1,0:T(8,128)S(1)}, f32[2,256,1536]{2,1,0:T(8,128)}, u32[]{:S(2)}) copy-start(f32[2,256,1536]{2,1,0:T(8,128)} %get-tuple-element.41) | copy-start | bytes 9437188
  601.1 5.8 copy-start.40
  601.1 5.8 copy-start.54
  603.3 14.1 %all-to-all-start.2 = ((bf16[2,128,1536]{2,1,0:T(8,128)(2,1)}), bf16[2,128,1536]{2,1,0:T(8,128)(2,1)S(1)}, u32[]{:S(2)}, u32[]{:S(2)}) async-start(bf16[2,128,1536]{2,1,0:T(8,128)(2,1)} %bitcast.317), calls=%async_computation.3 | async-start | bytes 1572864 | tf_op jit(solution)/shard_map/all_to_all | solution.py:432
  606.8 2.5 copy-start.12
  606.9 2.4 copy-start.16
  617.3 328.9 %all-to-all-start.3 = ((f32[2,128,1536]{2,1,0:T(8,128)}), f32[2,128,1536]{2,1,0:T(8,128)S(1)}, u32[]{:S(2)}, u32[]{:S(2)}) async-start(f32[2,128,1536]{2,1,0:T(8,128)} %multiply_add_fusion), calls=%async_computation.5 | async-start | bytes 3145728 | tf_op jit(solution)/shard_map/all_to_all | solution.py:475
  (14 other events, 17.9 us)
Sparse Core Ops, SparseCore 0:
  31.7 18.9 all-gather.2
  211.8 25.7 all-reduce.4
  358.0 28.0 all-reduce.6
  388.3 13.0 reduce-scatter.3
  575.5 16.5 reduce-scatter.5

commit v2 on v0

v2 whole, which is shorter than its diff:
```python
import math

import jax
import jax.numpy as jnp
import numpy as np
from jax import lax
from jax.experimental import pallas as pl
from jax.experimental.pallas import tpu as pltpu
from jax.sharding import Mesh
from jax.sharding import PartitionSpec as P

HEAD = 96
EPS = 1e-05
ROPE_BASE = 100000.0
AXES = ("yh", "x", "z", "core", "yl")
DP = ("yh", "x", "z", "core")
MESH = pl.DeviceIdType.MESH
BF = jnp.bfloat16
F32 = jnp.float32
ORDERS = (("x", "y", "z"), ("y", "z", "x"), ("z", "x", "y"))
SEQ = 256
ROWS = 512
STEP = 128
VMEM_LIMIT = 62 * 1024 * 1024


def coordinates():
    x, z, yh, yl = (lax.axis_index(a) for a in ("x", "z", "yh", "yl"))
    return {"x": x, "z": z, "y": yh * 2 + yl}


def around(value, by):
    return lax.rem(value + (by + 4), 4)


def peer(at, axis, by):
    moved = around(at[axis], by)
    if axis == "y":
        return {"yh": moved // 2, "yl": lax.rem(moved, 2)}
    return {axis: moved}


def sibling():
    return {"core": 1 - lax.axis_index("core")}


def partner():
    return {"yl": 1 - lax.axis_index("yl")}


def place(at, whole=(), half=None, moved=None):
    out = []
    for axis in ("y", "x", "z"):
        if axis in whole:
            if half is not None and half[0] == axis:
                out.append(pl.ds(2 * half[1], 2))
            else:
                out.append(pl.ds(0, 4))
        else:
            value = at[axis] if moved is None or moved[0] != axis else around(at[axis], moved[1])
            out.append(lax.rem(value, 2) * 2 + value // 2 if axis == "y" else value)
    return tuple(out)


def greet(at):
    barrier = pltpu.get_barrier_semaphore()
    for axis in ("x", "y", "z"):
        for by in (1, -1, 2):
            pl.semaphore_signal(barrier, inc=1, device_id=peer(at, axis, by), device_id_type=MESH)
    pl.semaphore_signal(barrier, inc=1, device_id=sibling(), device_id_type=MESH)
    pl.semaphore_wait(barrier, 10)


def pair_greet():
    barrier = pltpu.get_barrier_semaphore()
    pl.semaphore_signal(barrier, inc=1, device_id=sibling(), device_id_type=MESH)
    pl.semaphore_wait(barrier, 1)


def sent(src, dst, send, recv, device):
    copy = pltpu.make_async_remote_copy(
        src_ref=src, dst_ref=dst, send_sem=send, recv_sem=recv, device_id=device, device_id_type=MESH
    )
    copy.start()
    return copy


def moved(src, dst, sem):
    copy = pltpu.make_async_copy(src, dst, sem)
    copy.start()
    return copy


def halved(order):
    return "x" if order[2] == "y" else "y"


class Gather:
    semaphores = (
        pltpu.SemaphoreType.DMA((3,)),
        pltpu.SemaphoreType.DMA((3, 2, 3)),
        pltpu.SemaphoreType.DMA((3, 2, 3)),
        pltpu.SemaphoreType.DMA((3, 2, 3)),
        pltpu.SemaphoreType.DMA((3, 2, 3)),
    )

    def __init__(self, at, srcs, outs, semaphores):
        self.at, self.srcs, self.outs = at, srcs, outs
        self.local, self.send, self.recv, self.last_send, self.last_recv = semaphores
        self.own, self.started, self.final = [], {}, {}

    def stage(self, stage):
        at = self.at
        for p, order in enumerate(ORDERS):
            if stage:
                self.own[p].wait()
                for copy in self.started[p, 0]:
                    copy.wait()
            else:
                self.own.append(moved(self.srcs[p], self.outs[p].at[place(at)], self.local.at[p]))
            group = self.outs[p].at[place(at, order[:stage])]
            self.started[p, stage] = [
                sent(
                    group if stage else self.srcs[p],
                    group,
                    self.send.at[p, stage, d],
                    self.recv.at[p, stage, d],
                    peer(at, order[stage], by),
                )
                for d, by in enumerate((1, -1, 2))
            ]

    def spread(self):
        at = self.at
        for p, order in enumerate(ORDERS):
            for copy in self.started[p, 1]:
                copy.wait()
            for t in range(2):
                for d, by in enumerate((1, -1)):
                    h = t if by == 1 else 1 - t
                    block = self.outs[p].at[place(at, order[:2], (halved(order), h))]
                    self.final[p, d, h] = sent(
                        block, block, self.last_send.at[p, d, h], self.last_recv.at[p, d, h], peer(at, order[2], by)
                    )

    def forward(self):
        at = self.at
        for p, order in enumerate(ORDERS):
            for d, by in enumerate((1, -1)):
                self.final[p, d, d].wait_recv()
                block = self.outs[p].at[place(at, order[:2], (halved(order), d), (order[2], -by))]
                self.final[p, d, 2] = sent(
                    block, block, self.last_send.at[p, d, 2], self.last_recv.at[p, d, 2], peer(at, order[2], by)
                )

    def finish(self):
        for p in range(3):
            for d in range(2):
                self.final[p, d, 0].wait_send()
                self.final[p, d, 1].wait_send()
                self.final[p, d, 1 - d].wait_recv()
                self.final[p, d, 2].wait()


class Reduce:
    semaphores = (
        pltpu.SemaphoreType.DMA((3, 3)),
        pltpu.SemaphoreType.DMA((3, 2, 3)),
        pltpu.SemaphoreType.DMA((3, 2, 3)),
        pltpu.SemaphoreType.DMA((3, 2, 3)),
        pltpu.SemaphoreType.DMA((3, 2, 3)),
        pltpu.SemaphoreType.DMA((3, 2)),
        pltpu.SemaphoreType.DMA((3, 2)),
    )

    @staticmethod
    def buffers(columns):
        def per_piece(*shape):
            return [pltpu.VMEM(shape + (48, columns), BF) for _ in range(3)]

        return [
            *per_piece(2, 2, 4),
            *per_piece(4, 4),
            *per_piece(2, 2, 4),
            *per_piece(2, 4, 4),
            *per_piece(3, 4),
            *per_piece(3),
            *[pltpu.VMEM((48, columns), F32) for _ in range(3)],
        ]

    def __init__(self, at, data, buffers, semaphores):
        self.at, self.data = at, data
        self.side, self.kept, self.far, self.near, self.second, self.third, self.sums = (
            buffers[3 * k : 3 * k + 3] for k in range(7)
        )
        self.load, self.first_send, self.first_recv, self.send, self.recv, self.end_send, self.end_recv = semaphores
        self.loads, self.copies = {}, {}

    def start(self):
        at, s, r = self.at, self.first_send, self.first_recv
        for p, order in enumerate(ORDERS):
            axis = order[2]
            for d, by in enumerate((1, -1)):
                block = self.data[p].at[place(at, order[:2], (halved(order), d), (axis, 2))]
                self.copies[p, d, 0] = sent(block, self.far[p].at[d], s.at[p, d, 0], r.at[p, d, 0], peer(at, axis, by))
            for d, by in enumerate((1, -1)):
                h = 1 - d
                block = self.data[p].at[place(at, order[:2], (halved(order), h), (axis, by))]
                self.copies[p, d, 1] = sent(
                    block, self.near[p].at[d, pl.ds(2 * h, 2)], s.at[p, d, 1], r.at[p, d, 1], peer(at, axis, by)
                )
                block = self.data[p].at[place(at, order[:2], (halved(order), d), (axis, by))]
                self.loads[p, d] = moved(block, self.side[p].at[d], self.load.at[p, d])
            self.loads[p, 2] = moved(self.data[p].at[place(at, order[:2])], self.kept[p], self.load.at[p, 2])

    def relay(self):
        for p, order in enumerate(ORDERS):
            for d, by in enumerate((1, -1)):
                self.loads[p, d].wait()
                self.copies[p, d, 0].wait_recv()
                side, far = self.side[p], self.far[p]

                @pl.loop(0, 8)
                def _(i, d=d, side=side, far=far):
                    a, b = i // 4, lax.rem(i, 4)
                    side[d, a, b] = (side[d, a, b].astype(F32) + far[d, a, b].astype(F32)).astype(BF)

                self.copies[p, d, 2] = sent(
                    side.at[d],
                    self.near[p].at[d, pl.ds(2 * d, 2)],
                    self.first_send.at[p, d, 2],
                    self.first_recv.at[p, d, 2],
                    peer(self.at, order[2], by),
                )

    def inner(self, p, by):
        order = ORDERS[p]
        left = [a for a in ("y", "x", "z") if a != order[2]]
        value = around(self.at[order[1]], by)
        if order[1] == "y":
            value = lax.rem(value, 2) * 2 + value // 2
        return value, left[0] == order[1]

    def spread(self):
        for p, order in enumerate(ORDERS):
            self.loads[p, 2].wait()
            for d in range(2):
                self.copies[p, d, 1].wait_recv()
                self.copies[p, d, 2].wait_recv()
            kept, near = self.kept[p], self.near[p]

            @pl.loop(0, 16)
            def _(i, kept=kept, near=near):
                a, b = i // 4, lax.rem(i, 4)
                total = kept[a, b].astype(F32) + near[0, a, b].astype(F32) + near[1, a, b].astype(F32)
                kept[a, b] = total.astype(BF)

            for d, by in enumerate((1, -1, 2)):
                value, first = self.inner(p, by)
                block = kept.at[value] if first else kept.at[:, value]
                self.copies[p, "b", d] = sent(
                    block, self.second[p].at[d], self.send.at[p, 0, d], self.recv.at[p, 0, d], peer(self.at, order[1], by)
                )

    def narrow(self):
        for p, order in enumerate(ORDERS):
            for d in range(3):
                self.copies[p, "b", d].wait_recv()
            kept, second = self.kept[p], self.second[p]
            value, first = self.inner(p, 0)

            @pl.loop(0, 4)
            def _(i, kept=kept, second=second, value=value, first=first):
                where = (value, i) if first else (i, value)
                total = kept[where].astype(F32)
                for d in range(3):
                    total = total + second[d, i].astype(F32)
                kept[where] = total.astype(BF)

            for d, by in enumerate((1, -1, 2)):
                index = around(self.at[order[0]], by)
                if order[0] == "y":
                    index = lax.rem(index, 2) * 2 + index // 2
                block = kept.at[(value, index) if first else (index, value)]
                self.copies[p, "c", d] = sent(
                    block, self.third[p].at[d], self.send.at[p, 1, d], self.recv.at[p, 1, d], peer(self.at, order[0], by)
                )

    def finish(self, outs):
        core = lax.axis_index("core")
        ends = []
        for p, order in enumerate(ORDERS):
            for d in range(3):
                self.copies[p, "c", d].wait_recv()
            value, first = self.inner(p, 0)
            index = self.at[order[0]]
            if order[0] == "y":
                index = lax.rem(index, 2) * 2 + index // 2
            total = self.kept[p][(value, index) if first else (index, value)].astype(F32)
            for d in range(3):
                total = total + self.third[p][d].astype(F32)
            self.sums[p][...] = total
            theirs = self.sums[p].at[pl.ds(pl.multiple_of(24 * (1 - core), 8), 24)]
            mine = self.sums[p].at[pl.ds(pl.multiple_of(24 * core, 8), 24)]
            ends.append(sent(theirs, outs[p].at[core], self.end_send.at[p, 0], self.end_recv.at[p, 0], sibling()))
            ends.append(moved(mine, outs[p].at[core], self.end_send.at[p, 1]))
        for key, copy in self.copies.items():
            copy.wait_send()
        for copy in ends:
            copy.wait()


def nn(left, right):
    return lax.dot_general(left, right, (((1,), (0,)), ((), ())), preferred_element_type=F32)


def nt(left, right):
    return lax.dot_general(left, right, (((1,), (1,)), ((), ())), preferred_element_type=F32)


def tn(left, right):
    return lax.dot_general(left, right, (((0,), (0,)), ((), ())), preferred_element_type=F32)


def inverse_rms(values):
    return lax.rsqrt(jnp.mean(values * values, -1, keepdims=True) + EPS)


def swap(values, first):
    width = values.shape[-1]
    return jnp.where(first, pltpu.roll(values, width - HEAD // 2, 1), pltpu.roll(values, HEAD // 2, 1))


def first_half(shape):
    return lax.rem(lax.broadcasted_iota(jnp.int32, shape, 1), HEAD) < HEAD // 2


def rows_at(start, size):
    return pl.ds(pl.multiple_of(start, size), size)


ANY = pl.BlockSpec(memory_space=pl.ANY)
VMEM = pl.BlockSpec(memory_space=pltpu.VMEM)


def shaped(shape, kind=BF):
    return jax.ShapeDtypeStruct(shape, kind)


def call(kernel, operands, in_specs, results, out_specs, scratch, name, collective_id, **more):
    return pl.pallas_call(
        kernel,
        out_shape=results,
        in_specs=in_specs,
        out_specs=out_specs,
        scratch_shapes=scratch,
        compiler_params=pltpu.CompilerParams(
            collective_id=collective_id, has_side_effects=True, vmem_limit_bytes=VMEM_LIMIT
        ),
        name=name,
        **more,
    )(*operands)


def forward_kernel(third, wide, *refs):
    shard, xin, gin, tables = refs[:4]
    full_mlp, x_out, cot_out, cott_out, n1t_out, q_out, kv_out, probs_out, mixed_out, hidden_out, n2_out, n2t_out, valid_out = (
        refs[4:7],
        *refs[7:19],
    )
    attn_out = refs[19:22]
    (
        got_shard, packed, xs, gs, normed, q, kv, probs, mixed, hidden, normed_two, part, arrived, turned, valid,
    ) = refs[22:37]
    full_attn = refs[37:40]
    attn_sems, mlp_sems = refs[40:45], refs[45:50]
    pair_send, pair_recv, row_send, row_recv, out_sem = refs[50:]
    at = coordinates()
    core, yl = lax.axis_index("core"), lax.axis_index("yl")
    own_x = moved(xin.at[yl], xs.at[core, yl], out_sem.at[0])
    own_g = moved(gin.at[yl], gs.at[core, yl], out_sem.at[1])
    greet(at)
    swap_shard = sent(shard.at[1 - core], got_shard, pair_send.at[0], pair_recv.at[0], sibling())

    rows = {}
    for k, (src, dst) in enumerate(((xin, xs), (gin, gs))):
        rows[k, 0] = sent(src.at[1 - yl], dst.at[core, yl], row_send.at[k, 0], row_recv.at[k, 0], partner())
        rows[k, 1] = sent(src.at[yl], dst.at[core, yl], row_send.at[k, 1], row_recv.at[k, 1], sibling())

    swap_shard.wait()
    low, high = shard[core], got_shard[...]
    first, last = jnp.where(core == 0, low, high), jnp.where(core == 0, high, low)
    packed[...] = jnp.concatenate([first[:24], last[:24]], 0).astype(BF)
    for c, rows_of in enumerate((first, last)):
        valid[c] = jnp.where(yl == 0, rows_of[24:32, :SEQ], rows_of[24:32, SEQ : 2 * SEQ])

    def pieces(start, size):
        return [packed.at[:, pl.ds(start + k * size, size)] for k in range(3)]

    attn = Gather(at, pieces(0, third), full_attn, attn_sems)
    mlp_gather = Gather(at, pieces(3 * third, wide), full_mlp, mlp_sems)
    attn.stage(0)
    mlp_gather.stage(0)
    attn.stage(1)
    attn.spread()
    for k, dst in enumerate((xs, gs)):
        rows[k, 0].wait_recv()
        rows[k, 2] = sent(dst.at[core, 1 - yl], dst.at[core, 1 - yl], row_send.at[k, 2], row_recv.at[k, 2], sibling())
    attn.forward()
    mlp_gather.stage(1)
    own_x.wait()
    own_g.wait()
    for k in range(2):
        rows[k, 0].wait_send()
        rows[k, 1].wait()
        rows[k, 2].wait()
    outs = [moved(xs, x_out, out_sem.at[0])]

    @pl.loop(0, ROWS // STEP)
    def _(i):
        block = rows_at(i * STEP, STEP)
        values = xs[i // 2, lax.rem(i, 2)].astype(F32)
        normed[block] = (values * inverse_rms(values)).astype(BF)

    turned[0] = normed[...].T
    outs.append(moved(turned.at[0], n1t_out, out_sem.at[1]))
    outs.append(moved(valid, valid_out, out_sem.at[2]))
    attn.finish()
    outs.extend(moved(full_attn[p], attn_out[p], out_sem.at[12 + p]) for p in range(3))
    wq, wkv, wo = full_attn

    def weight(ref, y):
        return ref[pl.ds(2 * y, 2)].reshape(-1, third)

    @pl.loop(0, 2)
    def _(y):
        @pl.loop(0, ROWS // SEQ)
        def _(n):
            block = rows_at(n * SEQ, SEQ)
            left = normed[block]
            first = first_half((SEQ, third))
            for k, (w, result) in enumerate(((wq, q), (wkv, kv))):
                lin = nn(left, weight(w, y))
                result[y, block] = (lin * tables[2 * k] + swap(lin, first) * tables[2 * k + 1]).astype(BF)

    outs.append(moved(q, q_out, out_sem.at[3]))
    outs.append(moved(kv, kv_out, out_sem.at[4]))
    scale = 1.0 / math.sqrt(HEAD)

    @pl.loop(0, 4)
    def _(i):
        y, n = i // 2, lax.rem(i, 2)
        block = rows_at(n * SEQ, SEQ)
        t = lax.broadcasted_iota(jnp.int32, (SEQ, SEQ), 0)
        s = lax.broadcasted_iota(jnp.int32, (SEQ, SEQ), 1)
        keep = (s <= t) & (valid[n, 0:1, :] > 0.5)
        queries, keys = q[y, block], kv[y, block]
        results = []
        for h in range(4):
            g = h // 2
            scores = nt(queries[:, h * HEAD : (h + 1) * HEAD], keys[:, g * HEAD : (g + 1) * HEAD]) * scale
            scores = jnp.where(keep, scores, -1e30)
            terms = jnp.exp(scores - jnp.max(scores, -1, keepdims=True))
            low = (terms / jnp.sum(terms, -1, keepdims=True)).astype(BF)
            probs[i, h] = low
            results.append(nn(low, keys[:, (2 + g) * HEAD : (3 + g) * HEAD]))
        mixed[y, block] = jnp.concatenate(results, -1).astype(BF)

    outs.append(moved(probs, probs_out, out_sem.at[5]))
    outs.append(moved(mixed, mixed_out, out_sem.at[6]))
    mlp_gather.spread()
    copies = []
    for i in range(ROWS // STEP):
        block = pl.ds(i * STEP, STEP)
        part[block] = (nt(mixed[0, block], weight(wo, 0)) + nt(mixed[1, block], weight(wo, 1))).astype(BF)
        copies.append(sent(part.at[block], arrived.at[block], pair_send.at[1 + i], pair_recv.at[1 + i], sibling()))
    for i in range(ROWS // STEP):
        block = pl.ds(i * STEP, STEP)
        copies[i].wait()
        values = xs[i // 2, i % 2].astype(F32) + (part[block].astype(F32) + arrived[block].astype(F32))
        hidden[block] = values
        normed_two[block] = (values * inverse_rms(values)).astype(BF)
    outs.append(moved(hidden, hidden_out, out_sem.at[7]))
    outs.append(moved(normed_two, n2_out, out_sem.at[8]))
    mlp_gather.forward()
    turned[1] = normed_two[...].T
    outs.append(moved(turned.at[1], n2t_out, out_sem.at[9]))

    for c in range(2):
        for half in range(2):
            block = pl.ds((2 * c + half) * STEP, STEP)
            mask = valid[c][:, half * STEP : (half + 1) * STEP].T[:, 0:1]
            part[block] = (gs[c, half].astype(F32) * mask).astype(BF)
    turned[2] = part[...].T
    outs.append(moved(part, cot_out, out_sem.at[10]))
    outs.append(moved(turned.at[2], cott_out, out_sem.at[11]))
    mlp_gather.finish()
    for copy in outs:
        copy.wait()


def forward(shard, xin, gin, tables, third, wide):
    width = xin.shape[2]
    rows = (ROWS, width)
    heads = (2, ROWS, third)
    square = (4, 4, SEQ, SEQ)
    return call(
        lambda *refs: forward_kernel(third, wide, *refs),
        (shard, xin, gin, tables),
        [VMEM, ANY, ANY, VMEM],
        [shaped((4, 4, 4, 48, wide))] * 3
        + [
            shaped((2, 2, 128, width)),
            shaped(rows),
            shaped(rows[::-1]),
            shaped(rows[::-1]),
            shaped(heads),
            shaped(heads),
            shaped(square),
            shaped(heads),
            shaped(rows, F32),
            shaped(rows),
            shaped(rows[::-1]),
            shaped((2, 8, SEQ), F32),
        ]
        + [shaped((4, 4, 4, 48, third))] * 3,
        [ANY] * 18,
        [
            pltpu.VMEM(shard.shape[1:], F32),
            pltpu.VMEM((48, shard.shape[2]), BF),
            pltpu.VMEM((2, 2, 128, width), BF),
            pltpu.VMEM((2, 2, 128, width), BF),
            pltpu.VMEM(rows, BF),
            pltpu.VMEM(heads, BF),
            pltpu.VMEM(heads, BF),
            pltpu.VMEM(square, BF),
            pltpu.VMEM(heads, BF),
            pltpu.VMEM(rows, F32),
            pltpu.VMEM(rows, BF),
            pltpu.VMEM(rows, BF),
            pltpu.VMEM(rows, BF),
            pltpu.VMEM((3,) + rows[::-1], BF),
            pltpu.VMEM((2, 8, SEQ), F32),
            *[pltpu.VMEM((4, 4, 4, 48, third), BF) for _ in range(3)],
            *Gather.semaphores,
            *Gather.semaphores,
            pltpu.SemaphoreType.DMA((5,)),
            pltpu.SemaphoreType.DMA((5,)),
            pltpu.SemaphoreType.DMA((2, 3)),
            pltpu.SemaphoreType.DMA((2, 3)),
            pltpu.SemaphoreType.DMA((15,)),
        ],
        "gather_attn_forward",
        1,
    )


def mlp_kernel(
    n2, cot, hidden, n2t, cott, wg, wu, wd, dg, du, dd, result, branch, grad_hidden,
    out_acc, grad_acc, out_part, out_in, grad_part, grad_in, send, recv
):
    step = pl.program_id(0)
    core = lax.axis_index("core")

    @pl.when(step == 0)
    def _():
        pair_greet()
        out_acc[...] = jnp.zeros_like(out_acc)
        grad_acc[...] = jnp.zeros_like(grad_acc)

    gate_w, up_w, down_w = wg[0], wu[0], wd[0]
    gate = nn(n2[...], gate_w)
    up = nn(n2[...], up_w)
    sigma = jax.nn.sigmoid(gate)
    silu = gate * sigma
    active = (silu * up).astype(BF)
    grad_active = nn(cot[...], down_w)
    grad_gate = (grad_active * up * (sigma + silu * (1.0 - sigma))).astype(BF)
    grad_up = (grad_active * silu).astype(BF)
    dd[0] = nn(cott[...], active).astype(BF)
    dg[0] = nn(n2t[...], grad_gate).astype(BF)
    du[0] = nn(n2t[...], grad_up).astype(BF)
    out_acc[...] += nt(active, down_w)
    grad_acc[...] += nt(grad_gate, gate_w) + nt(grad_up, up_w)

    @pl.when(step == pl.num_programs(0) - 1)
    def _():
        own = rows_at(core * SEQ, SEQ)
        other = rows_at((1 - core) * SEQ, SEQ)
        grad_part[...] = grad_acc[...].astype(BF)
        copies = [sent(grad_part, grad_in, send.at[0], recv.at[0], sibling())]
        out_part[...] = out_acc[other].astype(BF)
        copies.append(sent(out_part, out_in, send.at[1], recv.at[1], sibling()))
        copies[0].wait()

        @pl.loop(0, ROWS // STEP)
        def _(i):
            rows = rows_at(i * STEP, STEP)
            grad = grad_part[rows].astype(F32) + grad_in[rows].astype(F32)
            values = hidden[rows]
            inverse = inverse_rms(values)
            unit = values * inverse
            back = inverse * (grad - unit * jnp.mean(grad * unit, -1, keepdims=True))
            grad_acc[rows] = cot[rows].astype(F32) + back
            branch[rows] = grad_acc[rows].astype(BF)

        grad_hidden[...] = grad_acc[own]
        copies[1].wait()
        result[...] = (hidden[own] + (out_acc[own] + out_in[...].astype(F32))).astype(BF)


def mlp(n2, cot, hidden, n2t, cott, wg, wu, wd):
    rows, width = n2.shape
    chunk = 256
    per = wg.shape[2] // chunk
    block = pl.BlockSpec((1, width, chunk), lambda i: (i // per, 0, lax.rem(i, per)))
    return call(
        mlp_kernel,
        (n2, cot, hidden, n2t, cott, wg, wu, wd),
        [VMEM] * 5 + [block] * 3,
        [shaped(wg.shape)] * 3 + [shaped((SEQ, width)), shaped((rows, width)), shaped((SEQ, width), F32)],
        [block] * 3 + [VMEM] * 3,
        [
            pltpu.VMEM((rows, width), F32),
            pltpu.VMEM((rows, width), F32),
            pltpu.VMEM((SEQ, width), BF),
            pltpu.VMEM((SEQ, width), BF),
            pltpu.VMEM((rows, width), BF),
            pltpu.VMEM((rows, width), BF),
            pltpu.SemaphoreType.DMA((2,)),
            pltpu.SemaphoreType.DMA((2,)),
        ],
        "mlp",
        2,
        grid=(2 * per,),
    )


def backward_kernel(*refs):
    xall, grad_hidden_in, branch_in, n1t_in, q_in, kv_in, probs_in, mixed_in, wq_in, wkv_in, wo_in, tables = refs[:12]
    data, result = refs[12:15], refs[15]
    mlp_outs, result_out, dq_out, dkv_out, do_out, in_grad_out = refs[16:19], *refs[19:24]
    (
        xs, gh, branch, branch_t, normed_t, q, kv, probs, mixed, wq, wkv, wo,
        grad_mixed, dq, dkv, part, keep_part, arrived, in_grad, stage,
    ) = refs[24:44]
    buffers = refs[44:65]
    reduce_sems = refs[65:72]
    load, put, send, recv = refs[72:]
    at = coordinates()
    core, yl = lax.axis_index("core"), lax.axis_index("yl")
    loads = [
        moved(src, dst, load.at[k])
        for k, (src, dst) in enumerate(
            (
                (branch_in, branch),
                (wo_in, wo),
                (mixed_in, mixed),
                (q_in, q),
                (kv_in, kv),
                (probs_in, probs),
                (wq_in, wq),
                (wkv_in, wkv),
                (n1t_in, normed_t),
                (grad_hidden_in, gh),
                (xall.at[core], xs),
            )
        )
    ]
    greet(at)
    mlp_sum = Reduce(at, data, buffers, reduce_sems)
    mlp_sum.start()
    halves = [
        moved(result.at[yl], result_out.at[yl], put.at[0]),
        sent(result.at[1 - yl], result_out.at[yl], send.at[0], recv.at[0], partner()),
    ]
    for k in range(3):
        loads[k].wait()
    branch_t[...] = branch[...].T
    third = wq.shape[2]
    outs = {}

    def put_out(k, y, value):
        slot = (2 * k + y) % 2
        if (k, y) != (0, 0) and (k, y) != (0, 1):
            outs.pop(slot).wait()
        stage[slot] = value.astype(BF)
        outs[slot] = moved(stage.at[slot], (do_out, dq_out, dkv_out)[k].at[y], put.at[1 + slot])

    for y in range(2):
        grad_mixed[y] = nn(branch[...], wo[y]).astype(BF)
        put_out(0, y, nn(branch_t[...], mixed[y]))
    for k in range(3, 6):
        loads[k].wait()
    scale = 1.0 / math.sqrt(HEAD)

    @pl.loop(0, 4)
    def _(i):
        y, n = i // 2, lax.rem(i, 2)
        rows = rows_at(n * SEQ, SEQ)
        queries, keys, grads = q[y, rows], kv[y, rows], grad_mixed[y, rows]
        grad_q, grad_k, grad_v = [], [None, None], [None, None]
        for h in range(4):
            g = h // 2
            key = keys[:, g * HEAD : (g + 1) * HEAD]
            value = keys[:, (2 + g) * HEAD : (3 + g) * HEAD]
            query = queries[:, h * HEAD : (h + 1) * HEAD]
            grad = grads[:, h * HEAD : (h + 1) * HEAD]
            low = probs[i, h]
            prob = low.astype(F32)
            grad_probs = nt(grad, value)
            grad_scores = (prob * (grad_probs - jnp.sum(grad_probs * prob, -1, keepdims=True))).astype(BF)
            grad_q.append(nn(grad_scores, key) * scale)
            back_k = tn(grad_scores, query) * scale
            back_v = tn(low, grad)
            grad_k[g] = back_k if grad_k[g] is None else grad_k[g] + back_k
            grad_v[g] = back_v if grad_v[g] is None else grad_v[g] + back_v
        first = first_half((SEQ, 4 * HEAD))
        for k, (pieces, target) in enumerate(((grad_q, dq), (grad_k + grad_v, dkv))):
            values = jnp.concatenate(pieces, -1)
            target[y, rows] = (values * tables[2 * k] - swap(values, first) * tables[2 * k + 1]).astype(BF)

    for k in range(6, 11):
        loads[k].wait()

    def back(start):
        rows = rows_at(start, SEQ)
        return (nt(dq[0, rows], wq[0]) + nt(dq[1, rows], wq[1])) + (nt(dkv[0, rows], wkv[0]) + nt(dkv[1, rows], wkv[1]))

    part[...] = back((1 - core) * SEQ).astype(BF)
    pair = sent(part, arrived, send.at[1], recv.at[1], sibling())
    mlp_sum.relay()
    keep_part[...] = back(core * SEQ)
    pair.wait()

    @pl.loop(0, SEQ // STEP)
    def _(i):
        rows = rows_at(i * STEP, STEP)
        grad = keep_part[rows] + arrived[rows].astype(F32)
        values = xs[i].astype(F32)
        inverse = inverse_rms(values)
        unit = values * inverse
        change = inverse * (grad - unit * jnp.mean(grad * unit, -1, keepdims=True))
        in_grad[i] = gh[rows] + change

    halves.append(moved(in_grad.at[yl], in_grad_out.at[yl], put.at[3]))
    halves.append(sent(in_grad.at[1 - yl], in_grad_out.at[yl], send.at[2], recv.at[2], partner()))
    for k, source in ((1, dq), (2, dkv)):
        for y in range(2):
            put_out(k, y, nn(normed_t[...], source[y]))
    mlp_sum.spread()
    mlp_sum.narrow()
    mlp_sum.finish(mlp_outs)
    for copy in (*halves, *outs.values()):
        copy.wait()


def backward(x, grad_hidden, branch, n1t, q, kv, probs, mixed, wq, wkv, wo, tables, data, result):
    rows, width = branch.shape
    third, wide = wq.shape[2], data[0].shape[-1]
    heads = (2, rows, third)
    weights = (2, width, third)
    half = (2, 128, width)
    return call(
        backward_kernel,
        (x, grad_hidden, branch, n1t, q, kv, probs, mixed, wq, wkv, wo, tables, *data, result),
        [ANY] * 11 + [VMEM] + [ANY] * 4,
        [shaped((2, 24, wide), F32)] * 3 + [shaped(half)] + [shaped(weights)] * 3 + [shaped(half, F32)],
        [ANY] * 8,
        [
            pltpu.VMEM(half, BF),
            pltpu.VMEM((SEQ, width), F32),
            pltpu.VMEM((rows, width), BF),
            pltpu.VMEM((width, rows), BF),
            pltpu.VMEM((width, rows), BF),
            pltpu.VMEM(heads, BF),
            pltpu.VMEM(heads, BF),
            pltpu.VMEM((4, 4, SEQ, SEQ), BF),
            pltpu.VMEM(heads, BF),
            pltpu.VMEM(weights, BF),
            pltpu.VMEM(weights, BF),
            pltpu.VMEM(weights, BF),
            pltpu.VMEM(heads, BF),
            pltpu.VMEM(heads, BF),
            pltpu.VMEM(heads, BF),
            pltpu.VMEM((SEQ, width), BF),
            pltpu.VMEM((SEQ, width), F32),
            pltpu.VMEM((SEQ, width), BF),
            pltpu.VMEM(half, F32),
            pltpu.VMEM(weights, BF),
            *Reduce.buffers(wide),
            *Reduce.semaphores,
            pltpu.SemaphoreType.DMA((11,)),
            pltpu.SemaphoreType.DMA((4,)),
            pltpu.SemaphoreType.DMA((3,)),
            pltpu.SemaphoreType.DMA((3,)),
        ],
        "reduce_mlp_attn_backward",
        3,
    )


def last_kernel(*refs):
    data, outs = refs[:3], refs[3:6]
    at = coordinates()
    greet(at)
    total = Reduce(at, data, refs[6:27], refs[27:])
    total.start()
    total.relay()
    total.spread()
    total.narrow()
    total.finish(outs)


def last_sums(data):
    columns = data[0].shape[-1]
    return call(
        last_kernel,
        data,
        [ANY] * 3,
        [shaped((2, 24, columns), F32)] * 3,
        [ANY] * 3,
        [*Reduce.buffers(columns), *Reduce.semaphores],
        "reduce_attn",
        4,
    )


def tables_for(count, heads, plain):
    half = HEAD // 2
    inverse = np.float32(ROPE_BASE) ** (-(np.arange(half, dtype=np.float32) * np.float32(2.0)) / np.float32(HEAD))
    angle = np.arange(count, dtype=np.float32)[:, None] * inverse.astype(np.float32)[None, :]
    cosine, sine = np.cos(angle), np.sin(angle)
    cosine = np.tile(np.concatenate([cosine, cosine], -1), (1, heads))
    sine = np.tile(np.concatenate([-sine, sine], -1), (1, heads))
    cosine = np.concatenate([cosine, np.ones((count, plain), np.float32)], -1)
    sine = np.concatenate([sine, np.zeros((count, plain), np.float32)], -1)
    return np.stack([cosine, sine]).astype(np.float32)


def body(
    inputs,
    out_grad,
    lengths,
    query_weight,
    key_matrix,
    value_matrix,
    output_weight,
    gate_weight,
    up_weight,
    down_weight,
    attn_gain,
    mlp_gain,
):
    width = inputs.shape[2]
    gain_one = attn_gain.astype(F32)[:, None]
    gain_two = mlp_gain.astype(F32)[:, None]

    def halves(weight):
        return weight.reshape(weight.shape[0], 2, -1)

    query32, key32, value32, gate32, up32 = (
        w.astype(F32) for w in (query_weight, key_matrix, value_matrix, gate_weight, up_weight)
    )
    blocks = [
        halves(query32 * gain_one),
        halves(key32 * gain_one),
        halves(value32 * gain_one),
        halves(output_weight.astype(F32).T),
        halves(gate32 * gain_two),
        halves(up32 * gain_two),
        halves(down_weight.astype(F32).T),
    ]
    sizes = [b.shape[2] for b in blocks]
    third, wide = sizes[0], sizes[4]
    shard = jnp.moveaxis(jnp.concatenate(blocks, -1), 1, 0)
    valid = (jnp.arange(SEQ)[None, :] < lengths).astype(F32).reshape(1, 1, 2 * SEQ)
    valid = jnp.broadcast_to(valid, (2, 8, 2 * SEQ))
    valid = jnp.pad(valid, ((0, 0), (0, 0), (0, shard.shape[2] - 2 * SEQ)))
    shard = jnp.concatenate([shard, valid], 1)
    tables = jnp.asarray(np.concatenate([tables_for(SEQ, 4, 0), tables_for(SEQ, 2, 2 * HEAD)]))

    wg, wu, wd, x, cot, cott, n1t, q, kv, probs, mixed, hidden, n2, n2t, _, wq, wkv, wo = forward(
        shard, inputs, out_grad, tables, third, wide
    )

    def joined(w):
        return w.reshape(2, width, -1)

    def blocked(w):
        return w.reshape(4, 4, 4, 48, -1)

    dg, du, dd, result, branch, grad_hidden = mlp(n2, cot, hidden, n2t, cott, joined(wg), joined(wu), joined(wd))
    *mlp_sums, result, dq, dkv, do, in_grad = backward(
        x,
        grad_hidden,
        branch,
        n1t,
        q,
        kv,
        probs,
        mixed,
        joined(wq),
        joined(wkv),
        joined(wo),
        tables,
        [blocked(w) for w in (dg, du, dd)],
        result.reshape(2, 128, width),
    )
    attn_sums = last_sums([blocked(w) for w in (dq, dkv, do)])

    def whole(part):
        return jnp.moveaxis(part, 0, 1).reshape(24, -1)

    key_size = sizes[1]
    dquery, doutput = whole(attn_sums[0]), whole(attn_sums[2])
    dkey, dvalue = whole(attn_sums[1][..., :key_size]), whole(attn_sums[1][..., key_size:])
    dgate, dup, ddown = (whole(part) for part in mlp_sums)
    gain_grads = jnp.stack(
        [
            sum(jnp.sum(w * g, -1) for w, g in ((query32, dquery), (key32, dkey), (value32, dvalue))),
            sum(jnp.sum(w * g, -1) for w, g in ((gate32, dgate), (up32, dup))),
        ]
    )
    gain_grads = lax.psum(gain_grads, "yl")
    return (
        result,
        in_grad,
        dquery * gain_one,
        dkey * gain_one,
        dvalue * gain_one,
        doutput.T,
        dgate * gain_two,
        dup * gain_two,
        ddown.T,
        gain_grads[0],
        gain_grads[1],
    )


def solution(mesh):
    fine = Mesh(mesh.devices.reshape(2, 4, 4, 2, 2), AXES)
    rows = P(None, AXES, None)
    into, out = P(DP, "yl"), P("yl", DP)
    return jax.shard_map(
        body,
        mesh=fine,
        in_specs=(rows, rows, P(None, DP), into, into, into, out, into, into, out, P(DP), P(DP)),
        out_specs=(rows, rows, into, into, into, out, into, into, out, P(DP), P(DP)),
        check_vma=False,
    )
```

time: 1340 us -> 349 us (0.26); the launches traced: 1320 us -> 348 us
  waiting for transfers between devices: 839 us -> 0 us
  Pallas kernels: 0 us -> 325 us
  matrix products: 157 us -> 0 us
  blocking collectives: 145 us -> 3.79 us
  local copies, waits for them, and re-layouts: 111 us -> 9.3 us
  other arithmetic: 35.7 us -> 9.18 us
  starting transfers between devices: 18 us -> 0 us
  between operations: 16.4 us -> 0.87 us
    unnamed x8 -> x0, waiting for transfers between devices: 758 us -> none
    pallas_call x0 -> x4, Pallas kernels: none -> 325 us  [call(): pl.pallas_call(kernel, out_shape=results, in_specs=in_specs, out_specs=ou...]
    dot_general x54 -> x0, matrix products: 157 us -> none  [the longest x14 60.3 us: outer_sum(): lax.dot_general(left, right, (((0,), (0,)), ((), ())), preferred_element_...]
    all_gather x8 -> x0, blocking collectives: 141 us -> none  [the longest x2 63.5 us: body(): lax.all_gather(grad_out.astype(jnp.bfloat16), 'tensor', axis=0, tiled=True)]
    all_gather x2 -> x0, waiting for transfers between devices: 73.4 us -> none  [turned_gather(): out, at, finished = (lax.all_gather(both, axis, axis=0, tiled=True), 0, [])]
    concatenate x2 -> x1, local copies, waits for them, and re-layouts: 58.6 us -> 0.09 us  [body(): shard = jnp.moveaxis(jnp.concatenate(blocks, -1), 1, 0)]
    add x6 -> x0, local copies, waits for them, and re-layouts: 20.7 us -> none  [body(): a_part + b_part]
    all_to_all x4 -> x0, starting transfers between devices: 16.6 us -> none  [the longest x2 8.64 us: sum_at_owner(): tiles = lax.all_to_all(in_blocks(array, dim, peers), axis, 0, 0, tiled=True)]
  transfers between devices with their start and end apart: 11 -> 0, of which waited for: 5 -> 0; matrix products, arithmetic and copies ran while one was open for 12% -> 0% of each run, Pallas kernels for 0% -> 0%
where the time goes in v2:
time: 349 us; the launch traced here: 348 us
  Pallas kernels  325 us (93%)
  local copies, waits for them, and re-layouts  9.3 us (3%)
  other arithmetic  9.18 us (3%)
  blocking collectives  3.79 us (1%)
    pallas_call x4, Pallas kernels, call(): pl.pallas_call(kernel, out_shape=results, in_specs=in_specs, out_specs=ou...  325 us

profile of v2, /device:TPU:1, one launch (start us, length us, event | category | flops | bytes accessed | tf_op | source)
XLA Modules:
  0.0 348.0 jit_solution(16617060538878764665)
XLA Ops:
  0.6 0.0 copy-start.2
  0.7 0.0 copy-start.3
  0.7 0.7 convert_element_type.34
  1.4 0.7 convert_element_type.38
  2.0 0.7 iota_compare_fusion
  2.8 0.8 convert_multiply_fusion.5
  3.6 0.8 reshape.194
  4.4 0.8 convert_multiply_fusion.7
  5.2 0.1 reshape.163
  5.3 0.1 reshape.162
  5.5 0.9 reshape.195
  6.4 0.0 copy-done.2
  6.4 0.0 copy-done.3
  6.4 0.1 convert_multiply_fusion.1
  6.6 0.1 concatenate.6
  6.7 1.1 pad_maximum_fusion.refs_0_
  7.7 128.9 %gather_attn_forward.1 = (bf16[4,4,4,48,1024]{4,3,2,1,0:T(8,128)(2,1)}, bf16[4,4,4,48,1024]{4,3,2,1,0:T(8,128)(2,1)}, bf16[4,4,4,48,1024]{4,3,2,1,0:T(8,128)(2,1...) custom-call(f32[2,32,4224]{2,1,0:T(8,128)} %pad_maximum_fusion.refs_, ...), custom_call_target="tpu_custom_call" | custom-call | tf_op jit(solution)/shard_map/gather_attn_forward/pallas_call | solution.py:351
  136.7 48.1 %mlp.1 = (bf16[2,1536,1024]{2,1,0:T(8,128)(2,1)}, bf16[2,1536,1024]{2,1,0:T(8,128)(2,1)}, bf16[2,1536,1024]{2,1,0:T(8,128)(2,1)}, bf16[256,1536]{1,0:T(8,128)(2,...) custom-call(bf16[512,1536]{1,0:T(8,128)(2,1)} %get-tuple-element.46.n2, bf16[512,1536]{1,0:T(8,128)(2,1)} %get-tuple-element.47.cot, ...), custom_call_target="tpu_custom_call" | custom-call | tf_op jit(solution)/shard_map/mlp/pallas_call | solution.py:351
  184.8 108.5 %reduce_mlp_attn_backward.1 = (f32[2,24,1024]{2,1,0:T(8,128)}, f32[2,24,1024]{2,1,0:T(8,128)}, f32[2,24,1024]{2,1,0:T(8,128)}, bf16[2,128,1536]{2,1,0:T(8,128)(2...) custom-call(bf16[2,2,128,1536]{3,2,1,0:T(8,128)(2,1)} %get-tuple-ele, ...), custom_call_target="tpu_custom_call" | custom-call | tf_op jit(solution)/shard_map/reduce_mlp_attn_backward/pallas_call | solution.py:351
  293.3 0.0 copy-start.4
  293.3 1.0 copy.45
  294.3 0.9 copy.46
  295.2 0.9 fusion
  296.2 0.0 copy-done.4
  296.2 0.7 copy.47
  296.9 0.0 copy-start.5
  296.9 0.0 copy-start.6
  296.9 0.0 copy-start.7
  296.9 0.0 copy-start.1
  296.9 39.3 %reduce_attn.1 = (f32[2,24,384]{2,1,0:T(8,128)}, f32[2,24,384]{2,1,0:T(8,128)}, f32[2,24,384]{2,1,0:T(8,128)}) custom-call(bf16[4,4,4,48,384]{4,3,2,1,0:T(8,128)(2,1)} %bitcast.78, bf16[4,4,4,48,384]{4,3,2,1,0:T(8,128)(2,1)} %bitcast.79, bf16[4,4,4,48,384]{4,3,2,1,0:T(8,128)(2,1)} %bitcast.80), custom_call_target="tpu_custom_call" | custom-call | tf_op jit(solution)/shard_map/reduce_attn/pallas_call | solution.py:351
  336.2 0.0 copy-start
  336.2 1.0 copy.43
  337.2 0.0 copy-done.5
  337.2 0.8 fusion.2
  338.0 1.5 copy.44
  339.6 0.9 slice_bitcast_fusion
  340.6 0.1 reshape.185
  340.7 0.1 reshape.184
  340.8 0.0 copy-done.6
  340.8 0.0 copy-done.7
  340.8 0.8 fusion.3
  341.6 3.8 %psum.7 = f32[2,24]{1,0:T(2,128)S(1)} all-reduce(f32[2,24]{1,0:T(2,128)S(1)} %pad_maximum_fusion.1), channel_id=1, replica_groups=mesh['yh'=2,'x'=4,'z'=4,'core'=2,'yl'=2] {'yl'}, use_global_device_ids=true, to_apply=%region_5.6 | all-reduce | flops 48 | bytes 384 | tf_op jit(solution)/shard_map/psum | solution.py:925
  345.4 0.5 slice_bitcast_fusion.2
  346.0 0.0 copy-done.1
  346.0 0.9 copy.60
  346.8 0.0 copy-done
  346.8 1.1 copy.61
  (15 shorter events, 0.2 us)
Async XLA Ops:
  0.6 5.8 %copy-start.2 = (bf16[24,2048]{1,0:T(8,128)(2,1)S(1)}, bf16[24,2048]{1,0:T(8,128)(2,1)}, u32[]{:S(2)}) copy-start(bf16[24,2048]{1,0:T(8,128)(2,1)} %param.21) | copy-start | bytes 294916
  0.7 5.8 %copy-start.3 = (bf16[24,2048]{1,0:T(8,128)(2,1)S(1)}, bf16[24,2048]{1,0:T(8,128)(2,1)}, u32[]{:S(2)}) copy-start(bf16[24,2048]{1,0:T(8,128)(2,1)} %param.20) | copy-start | bytes 294916
  293.3 2.9 copy-start.4
  296.9 40.4 %copy-start.5 = (bf16[24,768]{1,0:T(8,128)(2,1)S(1)}, bf16[24,768]{1,0:T(8,128)(2,1)}, u32[]{:S(2)}) copy-start(bf16[24,768]{1,0:T(8,128)(2,1)} %param.16) | copy-start | bytes 110596
  296.9 43.9 %copy-start.6 = (bf16[24,384]{1,0:T(8,128)(2,1)S(1)}, bf16[24,384]{1,0:T(8,128)(2,1)}, u32[]{:S(2)}) copy-start(bf16[24,384]{1,0:T(8,128)(2,1)} %param.18) | copy-start | bytes 55300
  296.9 43.9 %copy-start.7 = (bf16[24,384]{1,0:T(8,128)(2,1)S(1)}, bf16[24,384]{1,0:T(8,128)(2,1)}, u32[]{:S(2)}) copy-start(bf16[24,384]{1,0:T(8,128)(2,1)} %param.17) | copy-start | bytes 55300
  296.9 49.1 %copy-start.1 = (bf16[2,128,1536]{2,1,0:T(8,128)(2,1)S(1)}, bf16[2,128,1536]{2,1,0:T(8,128)(2,1)}, u32[]{:S(2)}) copy-start(bf16[2,128,1536]{2,1,0:T(8,128)(2,1)} %get-tuple-element.112) | copy-start | bytes 2359300
  336.2 10.6 %copy-start = (f32[2,128,1536]{2,1,0:T(8,128)S(1)}, f32[2,128,1536]{2,1,0:T(8,128)}, u32[]{:S(2)}) copy-start(f32[2,128,1536]{2,1,0:T(8,128)} %get-tuple-element.113) | copy-start | bytes 4718596

commit v3 on v2

--- a/solution.py
+++ b/solution.py
@@ -21,6 +21,7 @@
 SEQ = 256
 ROWS = 512
 STEP = 128
+CHUNK = 256
 VMEM_LIMIT = 62 * 1024 * 1024
 
 
@@ -362,19 +363,51 @@
     )(*operands)
 
 
+def mlp_step(n2, cot, n2t, cott, gate_w, up_w, down_w, out_acc, grad_acc):
+    gate = nn(n2[...], gate_w)
+    up = nn(n2[...], up_w)
+    sigma = jax.nn.sigmoid(gate)
+    silu = gate * sigma
+    active = (silu * up).astype(BF)
+    grad_active = nn(cot[...], down_w)
+    grad_gate = (grad_active * up * (sigma + silu * (1.0 - sigma))).astype(BF)
+    grad_up = (grad_active * silu).astype(BF)
+    out_acc[...] += nt(active, down_w)
+    grad_acc[...] += nt(grad_gate, gate_w) + nt(grad_up, up_w)
+    return (
+        nn(n2t[...], grad_gate).astype(BF),
+        nn(n2t[...], grad_up).astype(BF),
+        nn(cott[...], active).astype(BF),
+    )
+
+
+def mlp_chunk(step, acts, weights, accs, staging, outs, sems, waits):
+    y, sub = step // 2, step % 2
+    columns = pl.ds(sub * CHUNK, CHUNK)
+    values = mlp_step(*acts, *(w[pl.ds(2 * y, 2), :, :, :, columns].reshape(-1, CHUNK) for w in weights), *accs)
+    slot = step % 2
+    for p in range(3):
+        if (p, slot) in waits:
+            waits[p, slot].wait()
+        staging[slot, p] = values[p]
+        waits[p, slot] = moved(staging.at[slot, p], outs[p].at[y, :, columns], sems.at[p, slot])
+
+
 def forward_kernel(third, wide, *refs):
     shard, xin, gin, tables = refs[:4]
-    full_mlp, x_out, cot_out, cott_out, n1t_out, q_out, kv_out, probs_out, mixed_out, hidden_out, n2_out, n2t_out, valid_out = (
-        refs[4:7],
-        *refs[7:19],
-    )
-    attn_out = refs[19:22]
+    full_two = refs[4:7]
+    (
+        x_out, cot_out, cott_out, n1t_out, q_out, kv_out, probs_out, mixed_out, hidden_out, n2_out, n2t_out,
+        out_acc_out, grad_acc_out,
+    ) = refs[7:20]
+    attn_out, grads_out = refs[20:23], refs[23:26]
     (
         got_shard, packed, xs, gs, normed, q, kv, probs, mixed, hidden, normed_two, part, arrived, turned, valid,
-    ) = refs[22:37]
-    full_attn = refs[37:40]
-    attn_sems, mlp_sems = refs[40:45], refs[45:50]
-    pair_send, pair_recv, row_send, row_recv, out_sem = refs[50:]
+        out_acc, grad_acc, staging,
+    ) = refs[26:44]
+    full_attn, weights = refs[44:47], refs[47:50]
+    attn_sems, one_sems, two_sems = refs[50:55], refs[55:60], refs[60:65]
+    pair_send, pair_recv, row_send, row_recv, out_sem, put_sem = refs[65:]
     at = coordinates()
     core, yl = lax.axis_index("core"), lax.axis_index("yl")
     own_x = moved(xin.at[yl], xs.at[core, yl], out_sem.at[0])
@@ -394,20 +427,24 @@
     for c, rows_of in enumerate((first, last)):
         valid[c] = jnp.where(yl == 0, rows_of[24:32, :SEQ], rows_of[24:32, SEQ : 2 * SEQ])
 
-    def pieces(start, size):
-        return [packed.at[:, pl.ds(start + k * size, size)] for k in range(3)]
-
-    attn = Gather(at, pieces(0, third), full_attn, attn_sems)
-    mlp_gather = Gather(at, pieces(3 * third, wide), full_mlp, mlp_sems)
+    def pieces(start, size, step):
+        return [packed.at[:, pl.ds(start + k * step, size)] for k in range(3)]
+
+    half = wide // 2
+    attn = Gather(at, pieces(0, third, third), full_attn, attn_sems)
+    one = Gather(at, pieces(3 * third, half, wide), weights, one_sems)
+    two = Gather(at, pieces(3 * third + half, half, wide), full_two, two_sems)
     attn.stage(0)
-    mlp_gather.stage(0)
+    one.stage(0)
+    two.stage(0)
     attn.stage(1)
+    one.stage(1)
     attn.spread()
     for k, dst in enumerate((xs, gs)):
         rows[k, 0].wait_recv()
         rows[k, 2] = sent(dst.at[core, 1 - yl], dst.at[core, 1 - yl], row_send.at[k, 2], row_recv.at[k, 2], sibling())
     attn.forward()
-    mlp_gather.stage(1)
+    one.spread()
     own_x.wait()
     own_g.wait()
     for k in range(2):
@@ -424,8 +461,17 @@
 
     turned[0] = normed[...].T
     outs.append(moved(turned.at[0], n1t_out, out_sem.at[1]))
-    outs.append(moved(valid, valid_out, out_sem.at[2]))
+
+    cot = arrived
+    for c in range(2):
+        for h in range(2):
+            block = pl.ds((2 * c + h) * STEP, STEP)
+            mask = valid[c][:, h * STEP : (h + 1) * STEP].T[:, 0:1]
+            gs[c, h] = (gs[c, h].astype(F32) * mask).astype(BF)
+    out_acc[...] = jnp.zeros_like(out_acc)
+    grad_acc[...] = jnp.zeros_like(grad_acc)
     attn.finish()
+    two.stage(1)
     outs.extend(moved(full_attn[p], attn_out[p], out_sem.at[12 + p]) for p in range(3))
     wq, wkv, wo = full_attn
 
@@ -438,13 +484,14 @@
         def _(n):
             block = rows_at(n * SEQ, SEQ)
             left = normed[block]
-            first = first_half((SEQ, third))
+            is_first = first_half((SEQ, third))
             for k, (w, result) in enumerate(((wq, q), (wkv, kv))):
                 lin = nn(left, weight(w, y))
-                result[y, block] = (lin * tables[2 * k] + swap(lin, first) * tables[2 * k + 1]).astype(BF)
+                result[y, block] = (lin * tables[2 * k] + swap(lin, is_first) * tables[2 * k + 1]).astype(BF)
 
     outs.append(moved(q, q_out, out_sem.at[3]))
     outs.append(moved(kv, kv_out, out_sem.at[4]))
+    one.forward()
     scale = 1.0 / math.sqrt(HEAD)
 
     @pl.loop(0, 4)
@@ -468,12 +515,12 @@
 
     outs.append(moved(probs, probs_out, out_sem.at[5]))
     outs.append(moved(mixed, mixed_out, out_sem.at[6]))
-    mlp_gather.spread()
     copies = []
     for i in range(ROWS // STEP):
         block = pl.ds(i * STEP, STEP)
         part[block] = (nt(mixed[0, block], weight(wo, 0)) + nt(mixed[1, block], weight(wo, 1))).astype(BF)
         copies.append(sent(part.at[block], arrived.at[block], pair_send.at[1 + i], pair_recv.at[1 + i], sibling()))
+    two.spread()
     for i in range(ROWS // STEP):
         block = pl.ds(i * STEP, STEP)
         copies[i].wait()
@@ -482,20 +529,23 @@
         normed_two[block] = (values * inverse_rms(values)).astype(BF)
     outs.append(moved(hidden, hidden_out, out_sem.at[7]))
     outs.append(moved(normed_two, n2_out, out_sem.at[8]))
-    mlp_gather.forward()
     turned[1] = normed_two[...].T
     outs.append(moved(turned.at[1], n2t_out, out_sem.at[9]))
-
-    for c in range(2):
-        for half in range(2):
-            block = pl.ds((2 * c + half) * STEP, STEP)
-            mask = valid[c][:, half * STEP : (half + 1) * STEP].T[:, 0:1]
-            part[block] = (gs[c, half].astype(F32) * mask).astype(BF)
-    turned[2] = part[...].T
-    outs.append(moved(part, cot_out, out_sem.at[10]))
+    for i in range(ROWS // STEP):
+        cot[pl.ds(i * STEP, STEP)] = gs[i // 2, i % 2]
+    turned[2] = cot[...].T
+    outs.append(moved(cot, cot_out, out_sem.at[10]))
     outs.append(moved(turned.at[2], cott_out, out_sem.at[11]))
-    mlp_gather.finish()
-    for copy in outs:
+    one.finish()
+    acts, accs, waits = (normed_two, cot, turned.at[1], turned.at[2]), (out_acc, grad_acc), {}
+    for step in range(4):
+        mlp_chunk(step, acts, weights, accs, staging, grads_out, put_sem, waits)
+        if step == 1:
+            two.forward()
+    outs.append(moved(out_acc, out_acc_out, out_sem.at[2]))
+    outs.append(moved(grad_acc, grad_acc_out, out_sem.at[15]))
+    two.finish()
+    for copy in (*outs, *waits.values()):
         copy.wait()
 
 
@@ -504,11 +554,12 @@
     rows = (ROWS, width)
     heads = (2, ROWS, third)
     square = (4, 4, SEQ, SEQ)
+    half = wide // 2
     return call(
         lambda *refs: forward_kernel(third, wide, *refs),
         (shard, xin, gin, tables),
         [VMEM, ANY, ANY, VMEM],
-        [shaped((4, 4, 4, 48, wide))] * 3
+        [shaped((4, 4, 4, 48, half))] * 3
         + [
             shaped((2, 2, 128, width)),
             shaped(rows),
@@ -521,10 +572,12 @@
             shaped(rows, F32),
             shaped(rows),
             shaped(rows[::-1]),
-            shaped((2, 8, SEQ), F32),
+            shaped(rows, F32),
+            shaped(rows, F32),
         ]
-        + [shaped((4, 4, 4, 48, third))] * 3,
-        [ANY] * 18,
+        + [shaped((4, 4, 4, 48, third))] * 3
+        + [shaped((2, width, half))] * 3,
+        [ANY] * 22,
         [
             pltpu.VMEM(shard.shape[1:], F32),
             pltpu.VMEM((48, shard.shape[2]), BF),
@@ -541,112 +594,148 @@
             pltpu.VMEM(rows, BF),
             pltpu.VMEM((3,) + rows[::-1], BF),
             pltpu.VMEM((2, 8, SEQ), F32),
+            pltpu.VMEM(rows, F32),
+            pltpu.VMEM(rows, F32),
+            pltpu.VMEM((2, 3, width, CHUNK), BF),
             *[pltpu.VMEM((4, 4, 4, 48, third), BF) for _ in range(3)],
+            *[pltpu.VMEM((4, 4, 4, 48, half), BF) for _ in range(3)],
+            *Gather.semaphores,
             *Gather.semaphores,
             *Gather.semaphores,
             pltpu.SemaphoreType.DMA((5,)),
             pltpu.SemaphoreType.DMA((5,)),
             pltpu.SemaphoreType.DMA((2, 3)),
             pltpu.SemaphoreType.DMA((2, 3)),
-            pltpu.SemaphoreType.DMA((15,)),
+            pltpu.SemaphoreType.DMA((16,)),
+            pltpu.SemaphoreType.DMA((3, 2)),
         ],
-        "gather_attn_forward",
+        "gather_attn_forward_mlp",
         1,
     )
 
 
-def mlp_kernel(
-    n2, cot, hidden, n2t, cott, wg, wu, wd, dg, du, dd, result, branch, grad_hidden,
-    out_acc, grad_acc, out_part, out_in, grad_part, grad_in, send, recv
-):
-    step = pl.program_id(0)
+def middle_kernel(*refs):
+    n2_in, cot_in, hidden_in, n2t_in, cott_in, out_acc_in, grad_acc_in = refs[:7]
+    weights_in, data = refs[7:10], refs[10:13]
+    sums_out, grads_out = refs[13:16], refs[16:19]
+    result_out, branch_out, grad_hidden_out = refs[19:22]
+    (
+        n2, cot, hidden, n2t, cott, out_acc, grad_acc, staging, out_part, out_in, grad_part, grad_in, result, branch,
+    ) = refs[22:36]
+    weights, buffers = refs[36:39], refs[39:60]
+    reduce_sems = refs[60:67]
+    load, put, put_sem, send, recv = refs[67:]
     core = lax.axis_index("core")
-
-    @pl.when(step == 0)
-    def _():
-        pair_greet()
-        out_acc[...] = jnp.zeros_like(out_acc)
-        grad_acc[...] = jnp.zeros_like(grad_acc)
-
-    gate_w, up_w, down_w = wg[0], wu[0], wd[0]
-    gate = nn(n2[...], gate_w)
-    up = nn(n2[...], up_w)
-    sigma = jax.nn.sigmoid(gate)
-    silu = gate * sigma
-    active = (silu * up).astype(BF)
-    grad_active = nn(cot[...], down_w)
-    grad_gate = (grad_active * up * (sigma + silu * (1.0 - sigma))).astype(BF)
-    grad_up = (grad_active * silu).astype(BF)
-    dd[0] = nn(cott[...], active).astype(BF)
-    dg[0] = nn(n2t[...], grad_gate).astype(BF)
-    du[0] = nn(n2t[...], grad_up).astype(BF)
-    out_acc[...] += nt(active, down_w)
-    grad_acc[...] += nt(grad_gate, gate_w) + nt(grad_up, up_w)
-
-    @pl.when(step == pl.num_programs(0) - 1)
-    def _():
-        own = rows_at(core * SEQ, SEQ)
-        other = rows_at((1 - core) * SEQ, SEQ)
-        grad_part[...] = grad_acc[...].astype(BF)
-        copies = [sent(grad_part, grad_in, send.at[0], recv.at[0], sibling())]
-        out_part[...] = out_acc[other].astype(BF)
-        copies.append(sent(out_part, out_in, send.at[1], recv.at[1], sibling()))
-        copies[0].wait()
-
-        @pl.loop(0, ROWS // STEP)
-        def _(i):
-            rows = rows_at(i * STEP, STEP)
-            grad = grad_part[rows].astype(F32) + grad_in[rows].astype(F32)
-            values = hidden[rows]
-            inverse = inverse_rms(values)
-            unit = values * inverse
-            back = inverse * (grad - unit * jnp.mean(grad * unit, -1, keepdims=True))
-            grad_acc[rows] = cot[rows].astype(F32) + back
-            branch[rows] = grad_acc[rows].astype(BF)
-
-        grad_hidden[...] = grad_acc[own]
-        copies[1].wait()
-        result[...] = (hidden[own] + (out_acc[own] + out_in[...].astype(F32))).astype(BF)
-
-
-def mlp(n2, cot, hidden, n2t, cott, wg, wu, wd):
+    at = coordinates()
+    loads = [
+        moved(src, dst, load.at[k])
+        for k, (src, dst) in enumerate(
+            (
+                (n2_in, n2),
+                (weights_in[0], weights[0]),
+                (weights_in[1], weights[1]),
+                (cot_in, cot),
+                (weights_in[2], weights[2]),
+                (n2t_in, n2t),
+                (cott_in, cott),
+                (out_acc_in, out_acc),
+                (grad_acc_in, grad_acc),
+                (hidden_in, hidden),
+            )
+        )
+    ]
+    greet(at)
+    total = Reduce(at, data, buffers, reduce_sems)
+    total.start()
+    for k in range(9):
+        loads[k].wait()
+    acts, accs, waits = (n2, cot, n2t, cott), (out_acc, grad_acc), {}
+    for step in range(4):
+        mlp_chunk(step, acts, weights, accs, staging, grads_out, put_sem, waits)
+        if step == 2:
+            total.relay()
+    own = rows_at(core * SEQ, SEQ)
+    other = rows_at((1 - core) * SEQ, SEQ)
+    grad_part[...] = grad_acc[...].astype(BF)
+    copies = [sent(grad_part, grad_in, send.at[0], recv.at[0], sibling())]
+    out_part[...] = out_acc[other].astype(BF)
+    copies.append(sent(out_part, out_in, send.at[1], recv.at[1], sibling()))
+    loads[9].wait()
+    total.spread()
+    copies[0].wait()
+
+    @pl.loop(0, ROWS // STEP)
+    def _(i):
+        rows = rows_at(i * STEP, STEP)
+        grad = grad_part[rows].astype(F32) + grad_in[rows].astype(F32)
+        values = hidden[rows]
+        inverse = inverse_rms(values)
+        unit = values * inverse
+        back = inverse * (grad - unit * jnp.mean(grad * unit, -1, keepdims=True))
+        grad_acc[rows] = cot[rows].astype(F32) + back
+        branch[rows] = grad_acc[rows].astype(BF)
+
+    outs = [moved(branch, branch_out, put.at[0]), moved(grad_acc.at[own], grad_hidden_out, put.at[1])]
+    copies[1].wait()
+    result[...] = (hidden[own] + (out_acc[own] + out_in[...].astype(F32))).astype(BF)
+    outs.append(moved(result, result_out, put.at[2]))
+    total.narrow()
+    total.finish(sums_out)
+    for copy in (*outs, *waits.values()):
+        copy.wait()
+
+
+def middle(n2, cot, hidden, n2t, cott, out_acc, grad_acc, weights, data):
     rows, width = n2.shape
-    chunk = 256
-    per = wg.shape[2] // chunk
-    block = pl.BlockSpec((1, width, chunk), lambda i: (i // per, 0, lax.rem(i, per)))
+    half = weights[0].shape[-1]
     return call(
-        mlp_kernel,
-        (n2, cot, hidden, n2t, cott, wg, wu, wd),
-        [VMEM] * 5 + [block] * 3,
-        [shaped(wg.shape)] * 3 + [shaped((SEQ, width)), shaped((rows, width)), shaped((SEQ, width), F32)],
-        [block] * 3 + [VMEM] * 3,
+        middle_kernel,
+        (n2, cot, hidden, n2t, cott, out_acc, grad_acc, *weights, *data),
+        [ANY] * 13,
+        [shaped((2, 24, half), F32)] * 3
+        + [shaped((2, width, half))] * 3
+        + [shaped((SEQ, width)), shaped((rows, width)), shaped((SEQ, width), F32)],
+        [ANY] * 9,
         [
+            pltpu.VMEM((rows, width), BF),
+            pltpu.VMEM((rows, width), BF),
+            pltpu.VMEM((rows, width), F32),
+            pltpu.VMEM((width, rows), BF),
+            pltpu.VMEM((width, rows), BF),
             pltpu.VMEM((rows, width), F32),
             pltpu.VMEM((rows, width), F32),
+            pltpu.VMEM((2, 3, width, CHUNK), BF),
             pltpu.VMEM((SEQ, width), BF),
             pltpu.VMEM((SEQ, width), BF),
             pltpu.VMEM((rows, width), BF),
             pltpu.VMEM((rows, width), BF),
+            pltpu.VMEM((SEQ, width), BF),
+            pltpu.VMEM((rows, width), BF),
+            *[pltpu.VMEM((4, 4, 4, 48, half), BF) for _ in range(3)],
+            *Reduce.buffers(half),
+            *Reduce.semaphores,
+            pltpu.SemaphoreType.DMA((10,)),
+            pltpu.SemaphoreType.DMA((3,)),
+            pltpu.SemaphoreType.DMA((3, 2)),
             pltpu.SemaphoreType.DMA((2,)),
             pltpu.SemaphoreType.DMA((2,)),
         ],
-        "mlp",
+        "mlp_reduce",
         2,
-        grid=(2 * per,),
     )
 
 
 def backward_kernel(*refs):
     xall, grad_hidden_in, branch_in, n1t_in, q_in, kv_in, probs_in, mixed_in, wq_in, wkv_in, wo_in, tables = refs[:12]
     data, result = refs[12:15], refs[15]
-    mlp_outs, result_out, dq_out, dkv_out, do_out, in_grad_out = refs[16:19], *refs[19:24]
+    mlp_outs, attn_outs, attn_grads, result_out, in_grad_out = refs[16:19], refs[19:22], refs[22:25], *refs[25:27]
     (
         xs, gh, branch, branch_t, normed_t, q, kv, probs, mixed, wq, wkv, wo,
         grad_mixed, dq, dkv, part, keep_part, arrived, in_grad, stage,
-    ) = refs[24:44]
-    buffers = refs[44:65]
-    reduce_sems = refs[65:72]
-    load, put, send, recv = refs[72:]
+    ) = refs[27:47]
+    mlp_buffers, attn_buffers = refs[47:68], refs[68:89]
+    mlp_sems, attn_sems = refs[89:96], refs[96:103]
+    load, put, send, recv = refs[103:]
     at = coordinates()
     core, yl = lax.axis_index("core"), lax.axis_index("yl")
     loads = [
@@ -668,7 +757,8 @@
         )
     ]
     greet(at)
-    mlp_sum = Reduce(at, data, buffers, reduce_sems)
+    mlp_sum = Reduce(at, data, mlp_buffers, mlp_sems)
+    attn_sum = Reduce(at, attn_grads, attn_buffers, attn_sems)
     mlp_sum.start()
     halves = [
         moved(result.at[yl], result_out.at[yl], put.at[0]),
@@ -684,8 +774,9 @@
         slot = (2 * k + y) % 2
         if (k, y) != (0, 0) and (k, y) != (0, 1):
             outs.pop(slot).wait()
-        stage[slot] = value.astype(BF)
-        outs[slot] = moved(stage.at[slot], (do_out, dq_out, dkv_out)[k].at[y], put.at[1 + slot])
+        stage[slot] = value.astype(BF).reshape(stage.shape[1:])
+        target = (attn_grads[2], attn_grads[0], attn_grads[1])[k]
+        outs[slot] = moved(stage.at[slot], target.at[pl.ds(2 * y, 2)], put.at[1 + slot])
 
     for y in range(2):
         grad_mixed[y] = nn(branch[...], wo[y]).astype(BF)
@@ -720,8 +811,12 @@
             values = jnp.concatenate(pieces, -1)
             target[y, rows] = (values * tables[2 * k] - swap(values, first) * tables[2 * k + 1]).astype(BF)
 
+    mlp_sum.relay()
     for k in range(6, 11):
         loads[k].wait()
+    for k, source in ((1, dq), (2, dkv)):
+        for y in range(2):
+            put_out(k, y, nn(normed_t[...], source[y]))
 
     def back(start):
         rows = rows_at(start, SEQ)
@@ -729,7 +824,10 @@
 
     part[...] = back((1 - core) * SEQ).astype(BF)
     pair = sent(part, arrived, send.at[1], recv.at[1], sibling())
-    mlp_sum.relay()
+    for copy in outs.values():
+        copy.wait()
+    attn_sum.start()
+    mlp_sum.spread()
     keep_part[...] = back(core * SEQ)
     pair.wait()
 
@@ -745,13 +843,13 @@
 
     halves.append(moved(in_grad.at[yl], in_grad_out.at[yl], put.at[3]))
     halves.append(sent(in_grad.at[1 - yl], in_grad_out.at[yl], send.at[2], recv.at[2], partner()))
-    for k, source in ((1, dq), (2, dkv)):
-        for y in range(2):
-            put_out(k, y, nn(normed_t[...], source[y]))
-    mlp_sum.spread()
+    attn_sum.relay()
     mlp_sum.narrow()
+    attn_sum.spread()
     mlp_sum.finish(mlp_outs)
-    for copy in (*halves, *outs.values()):
+    attn_sum.narrow()
+    attn_sum.finish(attn_outs)
+    for copy in halves:
         copy.wait()
 
 
@@ -765,8 +863,11 @@
         backward_kernel,
         (x, grad_hidden, branch, n1t, q, kv, probs, mixed, wq, wkv, wo, tables, *data, result),
         [ANY] * 11 + [VMEM] + [ANY] * 4,
-        [shaped((2, 24, wide), F32)] * 3 + [shaped(half)] + [shaped(weights)] * 3 + [shaped(half, F32)],
-        [ANY] * 8,
+        [shaped((2, 24, wide), F32)] * 3
+        + [shaped((2, 24, third), F32)] * 3
+        + [shaped((4, 4, 4, 48, third))] * 3
+        + [shaped(half), shaped(half, F32)],
+        [ANY] * 11,
         [
             pltpu.VMEM(half, BF),
             pltpu.VMEM((SEQ, width), F32),
@@ -787,42 +888,18 @@
             pltpu.VMEM((SEQ, width), F32),
             pltpu.VMEM((SEQ, width), BF),
             pltpu.VMEM(half, F32),
-            pltpu.VMEM(weights, BF),
+            pltpu.VMEM((2, 2, 4, 4, 48, third), BF),
             *Reduce.buffers(wide),
+            *Reduce.buffers(third),
+            *Reduce.semaphores,
             *Reduce.semaphores,
             pltpu.SemaphoreType.DMA((11,)),
             pltpu.SemaphoreType.DMA((4,)),
             pltpu.SemaphoreType.DMA((3,)),
             pltpu.SemaphoreType.DMA((3,)),
         ],
-        "reduce_mlp_attn_backward",
+        "attn_backward_reduce",
         3,
-    )
-
-
-def last_kernel(*refs):
-    data, outs = refs[:3], refs[3:6]
-    at = coordinates()
-    greet(at)
-    total = Reduce(at, data, refs[6:27], refs[27:])
-    total.start()
-    total.relay()
-    total.spread()
-    total.narrow()
-    total.finish(outs)
-
-
-def last_sums(data):
-    columns = data[0].shape[-1]
-    return call(
-        last_kernel,
-        data,
-        [ANY] * 3,
-        [shaped((2, 24, columns), F32)] * 3,
-        [ANY] * 3,
-        [*Reduce.buffers(columns), *Reduce.semaphores],
-        "reduce_attn",
-        4,
     )
 
 
@@ -880,7 +957,7 @@
     shard = jnp.concatenate([shard, valid], 1)
     tables = jnp.asarray(np.concatenate([tables_for(SEQ, 4, 0), tables_for(SEQ, 2, 2 * HEAD)]))
 
-    wg, wu, wd, x, cot, cott, n1t, q, kv, probs, mixed, hidden, n2, n2t, _, wq, wkv, wo = forward(
+    *two, x, cot, cott, n1t, q, kv, probs, mixed, hidden, n2, n2t, out_acc, grad_acc, wq, wkv, wo, dg, du, dd = forward(
         shard, inputs, out_grad, tables, third, wide
     )
 
@@ -890,8 +967,10 @@
     def blocked(w):
         return w.reshape(4, 4, 4, 48, -1)
 
-    dg, du, dd, result, branch, grad_hidden = mlp(n2, cot, hidden, n2t, cott, joined(wg), joined(wu), joined(wd))
-    *mlp_sums, result, dq, dkv, do, in_grad = backward(
+    *one_sums, dg, du, dd, result, branch, grad_hidden = middle(
+        n2, cot, hidden, n2t, cott, out_acc, grad_acc, two, [blocked(w) for w in (dg, du, dd)]
+    )
+    *sums, _, _, _, result, in_grad = backward(
         x,
         grad_hidden,
         branch,
@@ -907,7 +986,8 @@
         [blocked(w) for w in (dg, du, dd)],
         result.reshape(2, 128, width),
     )
-    attn_sums = last_sums([blocked(w) for w in (dq, dkv, do)])
+    mlp_sums = [jnp.concatenate(parts, -1) for parts in zip(one_sums, sums[:3])]
+    attn_sums = sums[3:]
 
     def whole(part):
         return jnp.moveaxis(part, 0, 1).reshape(24, -1)

time: 349 us -> 307 us (0.88); the launches traced: 348 us -> 302 us
  Pallas kernels: 325 us -> 278 us
    pallas_call x4 -> x3, Pallas kernels: 325 us -> 278 us  [call(): pl.pallas_call(kernel, out_shape=results, in_specs=in_specs, out_specs=ou...]
where the time goes in v3:
time: 307 us; the launch traced here: 302 us
  Pallas kernels  278 us (91%)
  other arithmetic  11.9 us (4%)
  local copies, waits for them, and re-layouts  6.55 us (2%)
  blocking collectives  3.79 us (1%)
    pallas_call x3, Pallas kernels, call(): pl.pallas_call(kernel, out_shape=results, in_specs=in_specs, out_specs=ou...  278 us

profile of v3, /device:TPU:1, one launch (start us, length us, event | category | flops | bytes accessed | tf_op | source)
XLA Modules:
  0.0 301.9 jit_solution(16150104469941817768)
XLA Ops:
  0.6 0.7 convert_element_type.34
  1.3 0.7 convert_element_type.38
  2.0 0.7 iota_compare_fusion
  2.7 0.8 convert_multiply_fusion.5
  3.6 0.8 reshape.182
  4.4 0.8 convert_multiply_fusion.7
  5.2 0.1 reshape.154
  5.3 0.1 reshape.153
  5.4 0.9 reshape.183
  6.4 1.0 convert_multiply_fusion.1
  7.5 0.1 concatenate.15
  7.5 1.1 pad_maximum_fusion.refs_0_
  8.6 125.9 %gather_attn_forward_mlp.1 = (bf16[4,4,4,48,512]{4,3,2,1,0:T(8,128)(2,1)}, bf16[4,4,4,48,512]{4,3,2,1,0:T(8,128)(2,1)}, bf16[4,4,4,48,512]{4,3,2,1,0:T(8,128)(2,...) custom-call(f32[2,32,4224]{2,1,0:T(8,128)} %pad_maximum_fusion.refs_, ...), custom_call_target="tpu_custom_call" | custom-call | tf_op jit(solution)/shard_map/gather_attn_forward_mlp/pallas_call | solution.py:352
  134.5 51.4 %mlp_reduce.1 = (f32[2,24,512]{2,1,0:T(8,128)}, f32[2,24,512]{2,1,0:T(8,128)}, f32[2,24,512]{2,1,0:T(8,128)}, bf16[2,1536,512]{2,1,0:T(8,128)(2,1)}, bf16[2,1536...) custom-call(bf16[512,1536]{1,0:T(8,128)(2,1)} %get-tuple-element.51., ...), custom_call_target="tpu_custom_call" | custom-call | tf_op jit(solution)/shard_map/mlp_reduce/pallas_call | solution.py:352
  185.9 0.0 copy-start.4
  185.9 0.0 copy-start.8
  185.9 0.0 copy-start.7
  185.9 0.0 copy-start.2
  185.9 0.0 copy-start.3
  186.0 101.0 %attn_backward_reduce.1 = (f32[2,24,512]{2,1,0:T(8,128)}, f32[2,24,512]{2,1,0:T(8,128)}, f32[2,24,512]{2,1,0:T(8,128)}, f32[2,24,384]{2,1,0:T(8,128)}, f32[2,24,...) custom-call(bf16[2,2,128,1536]{3,2,1,0:T(8,128)(2,1)} %get-tuple-ele, ...), custom_call_target="tpu_custom_call" | custom-call | tf_op jit(solution)/shard_map/attn_backward_reduce/pallas_call | solution.py:352
  287.0 0.0 copy-start.6
  287.0 0.0 copy-start.9
  287.0 0.0 copy-start.5
  287.0 0.0 copy-start.10
  287.0 0.0 copy-start.11
  287.0 0.0 copy-start.1
  287.0 1.0 copy.43
  288.0 0.0 copy-done.4
  288.0 0.8 fusion.2
  288.8 1.5 copy.44
  290.4 0.0 copy-done.8
  290.4 0.9 maximum_bitcast_fusion
  291.3 0.0 copy-done.7
  291.3 0.9 maximum_bitcast_fusion.1
  292.2 0.0 copy-start
  292.2 0.0 copy-done.2
  292.3 0.0 copy-done.3
  292.3 0.9 fusion
  293.2 0.0 copy-done.6
  293.2 0.0 copy-done.9
  293.3 0.7 copy.47
  294.0 0.0 copy-done.5
  294.0 0.1 slice_bitcast_fusion
  294.1 0.1 reshape.173
  294.2 0.1 reshape.172
  294.3 0.0 copy-done.10
  294.3 0.0 copy-done.11
  294.3 0.8 fusion.3
  295.1 3.8 %psum.7 = f32[2,24]{1,0:T(2,128)S(1)} all-reduce(f32[2,24]{1,0:T(2,128)S(1)} %pad_maximum_fusion.1), channel_id=1, replica_groups=mesh['yh'=2,'x'=4,'z'=4,'core'=2,'yl'=2] {'yl'}, use_global_device_ids=true, to_apply=%region_5.6 | all-reduce | flops 48 | bytes 384 | tf_op jit(solution)/shard_map/psum | solution.py:1005
  298.9 0.5 slice_bitcast_fusion.2
  299.5 0.0 copy-done.1
  299.5 0.9 copy.60
  300.3 0.0 copy-done
  300.3 1.1 copy.61
  (18 shorter events, 0.3 us)
Async XLA Ops:
  185.9 102.1 %copy-start.4 = (bf16[24,768]{1,0:T(8,128)(2,1)S(1)}, bf16[24,768]{1,0:T(8,128)(2,1)}, u32[]{:S(2)}) copy-start(bf16[24,768]{1,0:T(8,128)(2,1)} %param.16) | copy-start | bytes 110596
  185.9 104.4 %copy-start.8 = (f32[2,24,512]{2,1,0:T(8,128)S(1)}, f32[2,24,512]{2,1,0:T(8,128)}, u32[]{:S(2)}) copy-start(f32[2,24,512]{2,1,0:T(8,128)} %get-tuple-element.83) | copy-start | bytes 294916
  185.9 105.4 %copy-start.7 = (f32[2,24,512]{2,1,0:T(8,128)S(1)}, f32[2,24,512]{2,1,0:T(8,128)}, u32[]{:S(2)}) copy-start(f32[2,24,512]{2,1,0:T(8,128)} %get-tuple-element.85) | copy-start | bytes 294916
  185.9 106.3 %copy-start.2 = (bf16[24,2048]{1,0:T(8,128)(2,1)S(1)}, bf16[24,2048]{1,0:T(8,128)(2,1)}, u32[]{:S(2)}) copy-start(bf16[24,2048]{1,0:T(8,128)(2,1)} %param.21) | copy-start | bytes 294916
  185.9 106.3 %copy-start.3 = (bf16[24,2048]{1,0:T(8,128)(2,1)S(1)}, bf16[24,2048]{1,0:T(8,128)(2,1)}, u32[]{:S(2)}) copy-start(bf16[24,2048]{1,0:T(8,128)(2,1)} %param.20) | copy-start | bytes 294916
  287.0 6.3 %copy-start.6 = (f32[2,24,512]{2,1,0:T(8,128)S(1)}, f32[2,24,512]{2,1,0:T(8,128)}, u32[]{:S(2)}) copy-start(f32[2,24,512]{2,1,0:T(8,128)} %get-tuple-element.87) | copy-start | bytes 294916
  287.0 6.3 %copy-start.9 = (f32[2,24,512]{2,1,0:T(8,128)S(1)}, f32[2,24,512]{2,1,0:T(8,128)}, u32[]{:S(2)}) copy-start(f32[2,24,512]{2,1,0:T(8,128)} %get-tuple-element.88) | copy-start | bytes 294916
  287.0 7.0 %copy-start.5 = (f32[2,24,384]{2,1,0:T(8,128)S(1)}, f32[2,24,384]{2,1,0:T(8,128)}, u32[]{:S(2)}) copy-start(f32[2,24,384]{2,1,0:T(8,128)} %get-tuple-element.81) | copy-start | bytes 221188
  287.0 7.3 %copy-start.10 = (bf16[24,384]{1,0:T(8,128)(2,1)S(1)}, bf16[24,384]{1,0:T(8,128)(2,1)}, u32[]{:S(2)}) copy-start(bf16[24,384]{1,0:T(8,128)(2,1)} %param.18) | copy-start | bytes 55300
  287.0 7.3 %copy-start.11 = (bf16[24,384]{1,0:T(8,128)(2,1)S(1)}, bf16[24,384]{1,0:T(8,128)(2,1)}, u32[]{:S(2)}) copy-start(bf16[24,384]{1,0:T(8,128)(2,1)} %param.17) | copy-start | bytes 55300
  287.0 12.5 %copy-start.1 = (bf16[2,128,1536]{2,1,0:T(8,128)(2,1)S(1)}, bf16[2,128,1536]{2,1,0:T(8,128)(2,1)}, u32[]{:S(2)}) copy-start(bf16[2,128,1536]{2,1,0:T(8,128)(2,1)} %get-tuple-element.122) | copy-start | bytes 2359300
  292.2 8.1 %copy-start = (f32[2,128,1536]{2,1,0:T(8,128)S(1)}, f32[2,128,1536]{2,1,0:T(8,128)}, u32[]{:S(2)}) copy-start(f32[2,128,1536]{2,1,0:T(8,128)} %get-tuple-element.123) | copy-start | bytes 4718596

commit v4 on v3

--- a/solution.py
+++ b/solution.py
@@ -17,7 +17,9 @@
 MESH = pl.DeviceIdType.MESH
 BF = jnp.bfloat16
 F32 = jnp.float32
-ORDERS = (("x", "y", "z"), ("y", "z", "x"), ("z", "x", "y"))
+EVEN = (("x", "y", "z"), ("y", "z", "x"), ("z", "x", "y"))
+SPARE_Y = (("x", "z", "y"), ("y", "x", "z"), ("y", "z", "x"))
+SPARE_Y_TOO = (("y", "x", "z"), ("y", "z", "x"), ("z", "x", "y"))
 SEQ = 256
 ROWS = 512
 STEP = 128
@@ -101,26 +103,33 @@
         pltpu.SemaphoreType.DMA((3,)),
         pltpu.SemaphoreType.DMA((3, 2, 3)),
         pltpu.SemaphoreType.DMA((3, 2, 3)),
-        pltpu.SemaphoreType.DMA((3, 2, 3)),
-        pltpu.SemaphoreType.DMA((3, 2, 3)),
-    )
-
-    def __init__(self, at, srcs, outs, semaphores):
-        self.at, self.srcs, self.outs = at, srcs, outs
-        self.local, self.send, self.recv, self.last_send, self.last_recv = semaphores
-        self.own, self.started, self.final = [], {}, {}
-
-    def stage(self, stage):
+        pltpu.SemaphoreType.DMA((3, 2, 2, 3)),
+        pltpu.SemaphoreType.DMA((3, 2, 2, 3)),
+    )
+
+    def __init__(self, at, srcs, outs, semaphores, orders):
+        self.at, self.srcs, self.outs, self.orders = at, srcs, outs, orders
+        self.local, self.send, self.recv, self.ring_send, self.ring_recv = semaphores
+        self.own, self.direct, self.ring = [], {}, {}
+
+    def arrive(self, p, stage):
+        for copy in self.direct.get((p, stage), ()):
+            copy.wait_recv()
+        if (p, stage, 0, 0) in self.ring:
+            for d in range(2):
+                self.ring[p, stage, d, 1 - d].wait_recv()
+                self.ring[p, stage, d, 2].wait_recv()
+
+    def to_all(self, stage):
         at = self.at
-        for p, order in enumerate(ORDERS):
+        for p, order in enumerate(self.orders):
             if stage:
                 self.own[p].wait()
-                for copy in self.started[p, 0]:
-                    copy.wait()
+                self.arrive(p, 0)
             else:
                 self.own.append(moved(self.srcs[p], self.outs[p].at[place(at)], self.local.at[p]))
             group = self.outs[p].at[place(at, order[:stage])]
-            self.started[p, stage] = [
+            self.direct[p, stage] = [
                 sent(
                     group if stage else self.srcs[p],
                     group,
@@ -131,36 +140,42 @@
                 for d, by in enumerate((1, -1, 2))
             ]
 
-    def spread(self):
-        at = self.at
-        for p, order in enumerate(ORDERS):
-            for copy in self.started[p, 1]:
-                copy.wait()
+    def pass_on(self, p, stage, d, k, block):
+        self.ring[p, stage, d, k] = sent(
+            block,
+            block,
+            self.ring_send.at[p, stage - 1, d, k],
+            self.ring_recv.at[p, stage - 1, d, k],
+            peer(self.at, self.orders[p][stage], 1 - 2 * d),
+        )
+
+    def spread(self, stage):
+        for p, order in enumerate(self.orders):
+            if stage == 1:
+                self.own[p].wait()
+            self.arrive(p, stage - 1)
             for t in range(2):
-                for d, by in enumerate((1, -1)):
-                    h = t if by == 1 else 1 - t
-                    block = self.outs[p].at[place(at, order[:2], (halved(order), h))]
-                    self.final[p, d, h] = sent(
-                        block, block, self.last_send.at[p, d, h], self.last_recv.at[p, d, h], peer(at, order[2], by)
+                for d in range(2):
+                    h = t if d == 0 else 1 - t
+                    self.pass_on(
+                        p, stage, d, h, self.outs[p].at[place(self.at, order[:stage], (order[0], h))]
                     )
 
-    def forward(self):
-        at = self.at
-        for p, order in enumerate(ORDERS):
+    def forward(self, stage):
+        for p, order in enumerate(self.orders):
             for d, by in enumerate((1, -1)):
-                self.final[p, d, d].wait_recv()
-                block = self.outs[p].at[place(at, order[:2], (halved(order), d), (order[2], -by))]
-                self.final[p, d, 2] = sent(
-                    block, block, self.last_send.at[p, d, 2], self.last_recv.at[p, d, 2], peer(at, order[2], by)
-                )
+                self.ring[p, stage, d, d].wait_recv()
+                where = place(self.at, order[:stage], (order[0], d), (order[stage], -by))
+                self.pass_on(p, stage, d, 2, self.outs[p].at[where])
 
     def finish(self):
         for p in range(3):
-            for d in range(2):
-                self.final[p, d, 0].wait_send()
-                self.final[p, d, 1].wait_send()
-                self.final[p, d, 1 - d].wait_recv()
-                self.final[p, d, 2].wait()
+            self.arrive(p, 2)
+        for copies in self.direct.values():
+            for copy in copies:
+                copy.wait_send()
+        for copy in self.ring.values():
+            copy.wait_send()
 
 
 class Reduce:
@@ -189,8 +204,8 @@
             *[pltpu.VMEM((48, columns), F32) for _ in range(3)],
         ]
 
-    def __init__(self, at, data, buffers, semaphores):
-        self.at, self.data = at, data
+    def __init__(self, at, data, buffers, semaphores, orders):
+        self.at, self.data, self.orders = at, data, orders
         self.side, self.kept, self.far, self.near, self.second, self.third, self.sums = (
             buffers[3 * k : 3 * k + 3] for k in range(7)
         )
@@ -199,7 +214,7 @@
 
     def start(self):
         at, s, r = self.at, self.first_send, self.first_recv
-        for p, order in enumerate(ORDERS):
+        for p, order in enumerate(self.orders):
             axis = order[2]
             for d, by in enumerate((1, -1)):
                 block = self.data[p].at[place(at, order[:2], (halved(order), d), (axis, 2))]
@@ -215,7 +230,7 @@
             self.loads[p, 2] = moved(self.data[p].at[place(at, order[:2])], self.kept[p], self.load.at[p, 2])
 
     def relay(self):
-        for p, order in enumerate(ORDERS):
+        for p, order in enumerate(self.orders):
             for d, by in enumerate((1, -1)):
                 self.loads[p, d].wait()
                 self.copies[p, d, 0].wait_recv()
@@ -235,7 +250,7 @@
                 )
 
     def inner(self, p, by):
-        order = ORDERS[p]
+        order = self.orders[p]
         left = [a for a in ("y", "x", "z") if a != order[2]]
         value = around(self.at[order[1]], by)
         if order[1] == "y":
@@ -243,7 +258,7 @@
         return value, left[0] == order[1]
 
     def spread(self):
-        for p, order in enumerate(ORDERS):
+        for p, order in enumerate(self.orders):
             self.loads[p, 2].wait()
             for d in range(2):
                 self.copies[p, d, 1].wait_recv()
@@ -264,7 +279,7 @@
                 )
 
     def narrow(self):
-        for p, order in enumerate(ORDERS):
+        for p, order in enumerate(self.orders):
             for d in range(3):
                 self.copies[p, "b", d].wait_recv()
             kept, second = self.kept[p], self.second[p]
@@ -290,7 +305,7 @@
     def finish(self, outs):
         core = lax.axis_index("core")
         ends = []
-        for p, order in enumerate(ORDERS):
+        for p, order in enumerate(self.orders):
             for d in range(3):
                 self.copies[p, "c", d].wait_recv()
             value, first = self.inner(p, 0)
@@ -394,7 +409,8 @@
 
 
 def forward_kernel(third, wide, *refs):
-    shard, xin, gin, tables = refs[:4]
+    own_weights, gains, lengths, xin, gin, tables = refs[:7], *refs[7:12]
+    refs = refs[8:]
     full_two = refs[4:7]
     (
         x_out, cot_out, cott_out, n1t_out, q_out, kv_out, probs_out, mixed_out, hidden_out, n2_out, n2t_out,
@@ -402,16 +418,39 @@
     ) = refs[7:20]
     attn_out, grads_out = refs[20:23], refs[23:26]
     (
-        got_shard, packed, xs, gs, normed, q, kv, probs, mixed, hidden, normed_two, part, arrived, turned, valid,
+        shard, got_shard, packed, xs, gs, normed, q, kv, probs, mixed, hidden, normed_two, part, arrived, turned, valid,
         out_acc, grad_acc, staging,
-    ) = refs[26:44]
-    full_attn, weights = refs[44:47], refs[47:50]
-    attn_sems, one_sems, two_sems = refs[50:55], refs[55:60], refs[60:65]
-    pair_send, pair_recv, row_send, row_recv, out_sem, put_sem = refs[65:]
+    ) = refs[26:45]
+    full_attn, weights = refs[45:48], refs[48:51]
+    attn_sems, one_sems, two_sems = refs[51:56], refs[56:61], refs[61:66]
+    pair_send, pair_recv, row_send, row_recv, out_sem, put_sem = refs[66:]
     at = coordinates()
     core, yl = lax.axis_index("core"), lax.axis_index("yl")
     own_x = moved(xin.at[yl], xs.at[core, yl], out_sem.at[0])
     own_g = moved(gin.at[yl], gs.at[core, yl], out_sem.at[1])
+
+    column = 0
+    query, key, value, output, *mlp_weights = (ref[...].astype(F32) for ref in own_weights)
+    gain_one, gain_two = gains[:, 0:1].astype(F32), gains[:, 1:2].astype(F32)
+    small = key.shape[1] // 2
+    for c in range(2):
+        thin = slice(c * small, (c + 1) * small)
+        parts = [
+            query[:, c * third : (c + 1) * third] * gain_one,
+            jnp.concatenate([key[:, thin] * gain_one, value[:, thin] * gain_one], -1),
+            output[:, c * third : (c + 1) * third],
+            *(
+                w[:, c * wide : (c + 1) * wide] * g
+                for w, g in zip(mlp_weights, (gain_two, gain_two, jnp.ones_like(gain_two)))
+            ),
+        ]
+        column = 0
+        for part_value in parts:
+            shard[c, :24, column : column + part_value.shape[1]] = part_value
+            column += part_value.shape[1]
+        lane = lax.broadcasted_iota(jnp.int32, (8, 2 * SEQ), 1)
+        ends = jnp.where(lane < SEQ, lengths[0, 0], lengths[1, 0] + SEQ)
+        shard[c, 24:, : 2 * SEQ] = jnp.where(lane < ends, 1.0, 0.0)
     greet(at)
     swap_shard = sent(shard.at[1 - core], got_shard, pair_send.at[0], pair_recv.at[0], sibling())
 
@@ -431,20 +470,22 @@
         return [packed.at[:, pl.ds(start + k * step, size)] for k in range(3)]
 
     half = wide // 2
-    attn = Gather(at, pieces(0, third, third), full_attn, attn_sems)
-    one = Gather(at, pieces(3 * third, half, wide), weights, one_sems)
-    two = Gather(at, pieces(3 * third + half, half, wide), full_two, two_sems)
-    attn.stage(0)
-    one.stage(0)
-    two.stage(0)
-    attn.stage(1)
-    one.stage(1)
-    attn.spread()
+    attn = Gather(at, pieces(0, third, third), full_attn, attn_sems, EVEN)
+    one = Gather(at, pieces(3 * third, half, wide), weights, one_sems, SPARE_Y)
+    two = Gather(at, pieces(3 * third + half, half, wide), full_two, two_sems, SPARE_Y_TOO)
+    attn.to_all(0)
+    one.to_all(0)
+    two.to_all(0)
+    attn.to_all(1)
+    one.spread(1)
+    attn.spread(2)
+    one.forward(1)
     for k, dst in enumerate((xs, gs)):
         rows[k, 0].wait_recv()
         rows[k, 2] = sent(dst.at[core, 1 - yl], dst.at[core, 1 - yl], row_send.at[k, 2], row_recv.at[k, 2], sibling())
-    attn.forward()
-    one.spread()
+    attn.forward(2)
+    one.spread(2)
+    two.spread(1)
     own_x.wait()
     own_g.wait()
     for k in range(2):
@@ -471,7 +512,7 @@
     out_acc[...] = jnp.zeros_like(out_acc)
     grad_acc[...] = jnp.zeros_like(grad_acc)
     attn.finish()
-    two.stage(1)
+    two.forward(1)
     outs.extend(moved(full_attn[p], attn_out[p], out_sem.at[12 + p]) for p in range(3))
     wq, wkv, wo = full_attn
 
@@ -491,7 +532,7 @@
 
     outs.append(moved(q, q_out, out_sem.at[3]))
     outs.append(moved(kv, kv_out, out_sem.at[4]))
-    one.forward()
+    one.forward(2)
     scale = 1.0 / math.sqrt(HEAD)
 
     @pl.loop(0, 4)
@@ -520,7 +561,7 @@
         block = pl.ds(i * STEP, STEP)
         part[block] = (nt(mixed[0, block], weight(wo, 0)) + nt(mixed[1, block], weight(wo, 1))).astype(BF)
         copies.append(sent(part.at[block], arrived.at[block], pair_send.at[1 + i], pair_recv.at[1 + i], sibling()))
-    two.spread()
+    two.spread(2)
     for i in range(ROWS // STEP):
         block = pl.ds(i * STEP, STEP)
         copies[i].wait()
@@ -541,7 +582,7 @@
     for step in range(4):
         mlp_chunk(step, acts, weights, accs, staging, grads_out, put_sem, waits)
         if step == 1:
-            two.forward()
+            two.forward(2)
     outs.append(moved(out_acc, out_acc_out, out_sem.at[2]))
     outs.append(moved(grad_acc, grad_acc_out, out_sem.at[15]))
     two.finish()
@@ -549,7 +590,7 @@
         copy.wait()
 
 
-def forward(shard, xin, gin, tables, third, wide):
+def forward(own_weights, gains, lengths, xin, gin, tables, third, wide):
     width = xin.shape[2]
     rows = (ROWS, width)
     heads = (2, ROWS, third)
@@ -557,8 +598,8 @@
     half = wide // 2
     return call(
         lambda *refs: forward_kernel(third, wide, *refs),
-        (shard, xin, gin, tables),
-        [VMEM, ANY, ANY, VMEM],
+        (*own_weights, gains, lengths, xin, gin, tables),
+        [VMEM] * 8 + [pl.BlockSpec(memory_space=pltpu.SMEM), ANY, ANY, VMEM],
         [shaped((4, 4, 4, 48, half))] * 3
         + [
             shaped((2, 2, 128, width)),
@@ -579,8 +620,9 @@
         + [shaped((2, width, half))] * 3,
         [ANY] * 22,
         [
-            pltpu.VMEM(shard.shape[1:], F32),
-            pltpu.VMEM((48, shard.shape[2]), BF),
+            pltpu.VMEM((2, 32, 3 * third + 3 * wide), F32),
+            pltpu.VMEM((32, 3 * third + 3 * wide), F32),
+            pltpu.VMEM((48, 3 * third + 3 * wide), BF),
             pltpu.VMEM((2, 2, 128, width), BF),
             pltpu.VMEM((2, 2, 128, width), BF),
             pltpu.VMEM(rows, BF),
@@ -645,7 +687,7 @@
         )
     ]
     greet(at)
-    total = Reduce(at, data, buffers, reduce_sems)
+    total = Reduce(at, data, buffers, reduce_sems, EVEN)
     total.start()
     for k in range(9):
         loads[k].wait()
@@ -728,14 +770,15 @@
 def backward_kernel(*refs):
     xall, grad_hidden_in, branch_in, n1t_in, q_in, kv_in, probs_in, mixed_in, wq_in, wkv_in, wo_in, tables = refs[:12]
     data, result = refs[12:15], refs[15]
-    mlp_outs, attn_outs, attn_grads, result_out, in_grad_out = refs[16:19], refs[19:22], refs[22:25], *refs[25:27]
+    mlp_outs, attn_outs, attn_grads = refs[16:19], refs[19:22], refs[22:25]
+    result_out, in_grad_out, from_partner = refs[25:28]
     (
         xs, gh, branch, branch_t, normed_t, q, kv, probs, mixed, wq, wkv, wo,
-        grad_mixed, dq, dkv, part, keep_part, arrived, in_grad, stage,
-    ) = refs[27:47]
-    mlp_buffers, attn_buffers = refs[47:68], refs[68:89]
-    mlp_sems, attn_sems = refs[89:96], refs[96:103]
-    load, put, send, recv = refs[103:]
+        grad_mixed, dq, dkv, part, keep_part, arrived, in_grad, for_partner, stage,
+    ) = refs[28:49]
+    mlp_buffers, attn_buffers = refs[49:70], refs[70:91]
+    mlp_sems, attn_sems = refs[91:98], refs[98:105]
+    load, put, send, recv = refs[105:]
     at = coordinates()
     core, yl = lax.axis_index("core"), lax.axis_index("yl")
     loads = [
@@ -757,8 +800,8 @@
         )
     ]
     greet(at)
-    mlp_sum = Reduce(at, data, mlp_buffers, mlp_sems)
-    attn_sum = Reduce(at, attn_grads, attn_buffers, attn_sems)
+    mlp_sum = Reduce(at, data, mlp_buffers, mlp_sems, SPARE_Y_TOO)
+    attn_sum = Reduce(at, attn_grads, attn_buffers, attn_sems, SPARE_Y)
     mlp_sum.start()
     halves = [
         moved(result.at[yl], result_out.at[yl], put.at[0]),
@@ -841,8 +884,9 @@
         change = inverse * (grad - unit * jnp.mean(grad * unit, -1, keepdims=True))
         in_grad[i] = gh[rows] + change
 
-    halves.append(moved(in_grad.at[yl], in_grad_out.at[yl], put.at[3]))
-    halves.append(sent(in_grad.at[1 - yl], in_grad_out.at[yl], send.at[2], recv.at[2], partner()))
+    for_partner[...] = in_grad[1 - yl].astype(BF)
+    halves.append(moved(in_grad.at[yl], in_grad_out, put.at[3]))
+    halves.append(sent(for_partner, from_partner, send.at[2], recv.at[2], partner()))
     attn_sum.relay()
     mlp_sum.narrow()
     attn_sum.spread()
@@ -866,8 +910,8 @@
         [shaped((2, 24, wide), F32)] * 3
         + [shaped((2, 24, third), F32)] * 3
         + [shaped((4, 4, 4, 48, third))] * 3
-        + [shaped(half), shaped(half, F32)],
-        [ANY] * 11,
+        + [shaped(half), shaped(half[1:], F32), shaped(half[1:])],
+        [ANY] * 12,
         [
             pltpu.VMEM(half, BF),
             pltpu.VMEM((SEQ, width), F32),
@@ -888,6 +932,7 @@
             pltpu.VMEM((SEQ, width), F32),
             pltpu.VMEM((SEQ, width), BF),
             pltpu.VMEM(half, F32),
+            pltpu.VMEM(half[1:], BF),
             pltpu.VMEM((2, 2, 4, 4, 48, third), BF),
             *Reduce.buffers(wide),
             *Reduce.buffers(third),
@@ -933,32 +978,23 @@
     gain_one = attn_gain.astype(F32)[:, None]
     gain_two = mlp_gain.astype(F32)[:, None]
 
-    def halves(weight):
-        return weight.reshape(weight.shape[0], 2, -1)
-
+    own_weights = (
+        query_weight,
+        key_matrix,
+        value_matrix,
+        output_weight.T,
+        gate_weight,
+        up_weight,
+        down_weight.T,
+    )
     query32, key32, value32, gate32, up32 = (
         w.astype(F32) for w in (query_weight, key_matrix, value_matrix, gate_weight, up_weight)
     )
-    blocks = [
-        halves(query32 * gain_one),
-        halves(key32 * gain_one),
-        halves(value32 * gain_one),
-        halves(output_weight.astype(F32).T),
-        halves(gate32 * gain_two),
-        halves(up32 * gain_two),
-        halves(down_weight.astype(F32).T),
-    ]
-    sizes = [b.shape[2] for b in blocks]
-    third, wide = sizes[0], sizes[4]
-    shard = jnp.moveaxis(jnp.concatenate(blocks, -1), 1, 0)
-    valid = (jnp.arange(SEQ)[None, :] < lengths).astype(F32).reshape(1, 1, 2 * SEQ)
-    valid = jnp.broadcast_to(valid, (2, 8, 2 * SEQ))
-    valid = jnp.pad(valid, ((0, 0), (0, 0), (0, shard.shape[2] - 2 * SEQ)))
-    shard = jnp.concatenate([shard, valid], 1)
+    third, wide = query_weight.shape[1] // 2, gate_weight.shape[1] // 2
     tables = jnp.asarray(np.concatenate([tables_for(SEQ, 4, 0), tables_for(SEQ, 2, 2 * HEAD)]))
 
     *two, x, cot, cott, n1t, q, kv, probs, mixed, hidden, n2, n2t, out_acc, grad_acc, wq, wkv, wo, dg, du, dd = forward(
-        shard, inputs, out_grad, tables, third, wide
+        own_weights, jnp.stack([attn_gain, mlp_gain], 1), lengths, inputs, out_grad, tables, third, wide
     )
 
     def joined(w):
@@ -970,7 +1006,7 @@
     *one_sums, dg, du, dd, result, branch, grad_hidden = middle(
         n2, cot, hidden, n2t, cott, out_acc, grad_acc, two, [blocked(w) for w in (dg, du, dd)]
     )
-    *sums, _, _, _, result, in_grad = backward(
+    *sums, _, _, _, result, in_grad, in_grad_theirs = backward(
         x,
         grad_hidden,
         branch,
@@ -986,13 +1022,15 @@
         [blocked(w) for w in (dg, du, dd)],
         result.reshape(2, 128, width),
     )
+    mine = jnp.arange(2)[:, None, None] == lax.axis_index("yl")
+    in_grad = jnp.where(mine, in_grad[None], in_grad_theirs[None].astype(F32))
     mlp_sums = [jnp.concatenate(parts, -1) for parts in zip(one_sums, sums[:3])]
     attn_sums = sums[3:]
 
     def whole(part):
         return jnp.moveaxis(part, 0, 1).reshape(24, -1)
 
-    key_size = sizes[1]
+    key_size = key_matrix.shape[1] // 2
     dquery, doutput = whole(attn_sums[0]), whole(attn_sums[2])
     dkey, dvalue = whole(attn_sums[1][..., :key_size]), whole(attn_sums[1][..., key_size:])
     dgate, dup, ddown = (whole(part) for part in mlp_sums)

time: 307 us -> 296 us (0.964)
  other arithmetic: 11.9 us -> 6.54 us
  Pallas kernels: 278 us -> 273 us
    pallas_call x3, Pallas kernels: 278 us -> 273 us  [call(): pl.pallas_call(kernel, out_shape=results, in_specs=in_specs, out_specs=ou...]
where the time goes in v4:
time: 296 us; the launch traced here: 291 us
  Pallas kernels  273 us (92%)
  local copies, waits for them, and re-layouts  6.93 us (2%)
  other arithmetic  6.54 us (2%)
  blocking collectives  3.79 us (1%)
    pallas_call x3, Pallas kernels, call(): pl.pallas_call(kernel, out_shape=results, in_specs=in_specs, out_specs=ou...  273 us

profile of v4, /device:TPU:1, one launch (start us, length us, event | category | flops | bytes accessed | tf_op | source)
XLA Modules:
  0.0 291.5 jit_solution(12211466388308793589)
XLA Ops:
  0.6 0.7 pad_maximum_fusion.1
  1.3 0.7 copy.37.refs_7_
  2.0 1.3 copy.38.refs_8_
  3.3 133.7 %gather_attn_forward_mlp.1 = (bf16[4,4,4,48,512]{4,3,2,1,0:T(8,128)(2,1)}, bf16[4,4,4,48,512]{4,3,2,1,0:T(8,128)(2,1)}, bf16[4,4,4,48,512]{4,3,2,1,0:T(8,128)(2,...) custom-call(bf16[24,768]{1,0:T(8,128)(2,1)} %refs_0_.1, ...), custom_call_target="tpu_custom_call" | custom-call | tf_op jit(solution)/shard_map/gather_attn_forward_mlp/pallas_call | solution.py:367
  137.0 49.9 %mlp_reduce.1 = (f32[2,24,512]{2,1,0:T(8,128)}, f32[2,24,512]{2,1,0:T(8,128)}, f32[2,24,512]{2,1,0:T(8,128)}, bf16[2,1536,512]{2,1,0:T(8,128)(2,1)}, bf16[2,1536...) custom-call(bf16[512,1536]{1,0:T(8,128)(2,1)} %get-tuple-element.52., ...), custom_call_target="tpu_custom_call" | custom-call | tf_op jit(solution)/shard_map/mlp_reduce/pallas_call | solution.py:367
  186.9 0.0 copy-start.13
  187.0 0.0 copy-start.10
  187.0 0.0 copy-start.11
  187.0 0.0 copy-start.5
  187.0 0.0 copy-start.6
  187.0 0.0 copy-start.7
  187.0 0.0 copy-start.14
  187.0 89.2 %attn_backward_reduce.1 = (f32[2,24,512]{2,1,0:T(8,128)}, f32[2,24,512]{2,1,0:T(8,128)}, f32[2,24,512]{2,1,0:T(8,128)}, f32[2,24,384]{2,1,0:T(8,128)}, f32[2,24,...) custom-call(bf16[2,2,128,1536]{3,2,1,0:T(8,128)(2,1)} %get-tuple-ele, ...), custom_call_target="tpu_custom_call" | custom-call | tf_op jit(solution)/shard_map/attn_backward_reduce/pallas_call | solution.py:367
  276.2 0.0 copy-start.2
  276.2 0.0 copy-start.3
  276.3 0.0 copy-start.8
  276.3 0.0 copy-start.9
  276.3 0.0 copy-start.4
  276.3 1.0 slice_bitcast_fusion
  277.3 0.1 reshape.126
  277.4 0.1 reshape.127
  277.5 0.0 copy-done.13
  277.5 0.0 copy-done.10
  277.6 0.0 copy-done.11
  277.6 0.8 multiply_reduce_fusion.3
  278.4 0.9 copy.46
  279.3 0.0 copy-done.5
  279.3 0.0 copy-start.1
  279.3 0.8 multiply_reduce_fusion.2
  280.1 0.0 copy-done.6
  280.1 0.0 copy-done.7
  280.1 1.0 maximum_bitcast_fusion
  281.1 0.0 copy-done.14
  281.1 0.0 copy-done.2
  281.1 0.9 multiply_reduce_fusion
  282.0 0.0 copy-done.3
  282.0 0.9 multiply_reduce_fusion.1
  282.9 3.8 %psum.7 = f32[2,24]{1,0:T(2,128)S(1)} all-reduce(f32[2,24]{1,0:T(2,128)S(1)} %pad_maximum_fusion), channel_id=1, replica_groups=mesh['yh'=2,'x'=4,'z'=4,'core'=2,'yl'=2] {'yl'}, use_global_device_ids=true, to_apply=%region_5.6 | all-reduce | flops 48 | bytes 384 | tf_op jit(solution)/shard_map/psum | solution.py:1043
  286.7 0.5 slice_bitcast_fusion.2
  287.3 0.0 copy-done.8
  287.3 0.0 copy-done.9
  287.3 0.0 copy-start.12
  287.3 0.0 copy-start
  287.3 0.7 copy.50
  288.0 0.0 copy-done.4
  288.0 0.1 convert_element_type.25
  288.1 0.0 copy-done.1
  288.1 1.4 broadcast_select_fusion
  289.5 0.0 copy-done.12
  289.5 0.6 copy.47
  290.1 0.0 copy-done
  290.1 0.9 copy.52
  (11 shorter events, 0.1 us)
Async XLA Ops:
  186.9 90.6 %copy-start.13 = (bf16[24]{0:T(256)(128)(2,1)S(1)}, bf16[24]{0:T(256)(128)(2,1)}, u32[]{:S(2)}) copy-start(bf16[24]{0:T(256)(128)(2,1)} %param.23) | copy-start | bytes 148
  187.0 90.6 %copy-start.10 = (bf16[24,384]{1,0:T(8,128)(2,1)S(1)}, bf16[24,384]{1,0:T(8,128)(2,1)}, u32[]{:S(2)}) copy-start(bf16[24,384]{1,0:T(8,128)(2,1)} %refs_1_.1) | copy-start | bytes 55300
  187.0 90.6 %copy-start.11 = (bf16[24,384]{1,0:T(8,128)(2,1)S(1)}, bf16[24,384]{1,0:T(8,128)(2,1)}, u32[]{:S(2)}) copy-start(bf16[24,384]{1,0:T(8,128)(2,1)} %refs_2_.1) | copy-start | bytes 55300
  187.0 92.3 %copy-start.5 = (bf16[24,768]{1,0:T(8,128)(2,1)S(1)}, bf16[24,768]{1,0:T(8,128)(2,1)}, u32[]{:S(2)}) copy-start(bf16[24,768]{1,0:T(8,128)(2,1)} %refs_0_.1) | copy-start | bytes 110596
  187.0 93.1 %copy-start.6 = (f32[2,24,512]{2,1,0:T(8,128)S(1)}, f32[2,24,512]{2,1,0:T(8,128)}, u32[]{:S(2)}) copy-start(f32[2,24,512]{2,1,0:T(8,128)} %get-tuple-element.85) | copy-start | bytes 294916
  187.0 93.1 %copy-start.7 = (f32[2,24,512]{2,1,0:T(8,128)S(1)}, f32[2,24,512]{2,1,0:T(8,128)}, u32[]{:S(2)}) copy-start(f32[2,24,512]{2,1,0:T(8,128)} %get-tuple-element.87) | copy-start | bytes 294916
  187.0 94.1 %copy-start.14 = (bf16[24]{0:T(256)(128)(2,1)S(1)}, bf16[24]{0:T(256)(128)(2,1)}, u32[]{:S(2)}) copy-start(bf16[24]{0:T(256)(128)(2,1)} %param.24) | copy-start | bytes 148
  276.2 4.9 %copy-start.2 = (bf16[24,2048]{1,0:T(8,128)(2,1)S(1)}, bf16[24,2048]{1,0:T(8,128)(2,1)}, u32[]{:S(2)}) copy-start(bf16[24,2048]{1,0:T(8,128)(2,1)} %refs_5_.1) | copy-start | bytes 294916
  276.2 5.8 %copy-start.3 = (bf16[24,2048]{1,0:T(8,128)(2,1)S(1)}, bf16[24,2048]{1,0:T(8,128)(2,1)}, u32[]{:S(2)}) copy-start(bf16[24,2048]{1,0:T(8,128)(2,1)} %refs_4_.1) | copy-start | bytes 294916
  276.3 11.0 %copy-start.8 = (f32[2,24,512]{2,1,0:T(8,128)S(1)}, f32[2,24,512]{2,1,0:T(8,128)}, u32[]{:S(2)}) copy-start(f32[2,24,512]{2,1,0:T(8,128)} %get-tuple-element.89) | copy-start | bytes 294916
  276.3 11.0 %copy-start.9 = (f32[2,24,512]{2,1,0:T(8,128)S(1)}, f32[2,24,512]{2,1,0:T(8,128)}, u32[]{:S(2)}) copy-start(f32[2,24,512]{2,1,0:T(8,128)} %get-tuple-element.90) | copy-start | bytes 294916
  276.3 11.7 %copy-start.4 = (bf16[128,1536]{1,0:T(8,128)(2,1)S(1)}, bf16[128,1536]{1,0:T(8,128)(2,1)}, u32[]{:S(2)}) copy-start(bf16[128,1536]{1,0:T(8,128)(2,1)} %get-tuple-element.81) | copy-start | bytes 1179652
  279.3 8.8 %copy-start.1 = (f32[128,1536]{1,0:T(8,128)S(1)}, f32[128,1536]{1,0:T(8,128)}, u32[]{:S(2)}) copy-start(f32[128,1536]{1,0:T(8,128)} %get-tuple-element.80) | copy-start | bytes 2359300
  287.3 2.2 copy-start.12
  287.3 2.8 copy-start

commit v5 on v4

--- a/solution.py
+++ b/solution.py
@@ -18,8 +18,9 @@
 BF = jnp.bfloat16
 F32 = jnp.float32
 EVEN = (("x", "y", "z"), ("y", "z", "x"), ("z", "x", "y"))
-SPARE_Y = (("x", "z", "y"), ("y", "x", "z"), ("y", "z", "x"))
-SPARE_Y_TOO = (("y", "x", "z"), ("y", "z", "x"), ("z", "x", "y"))
+SPARE_X = (("y", "z", "x"), ("x", "y", "z"), ("x", "z", "y"))
+PLANE_Z = (("w", "x", "z"), ("w", "z", "x"), ("w", "x", "z"))
+PLANE_X = (("w", "z", "x"), ("w", "x", "z"), ("w", "z", "x"))
 SEQ = 256
 ROWS = 512
 STEP = 128
@@ -29,18 +30,26 @@
 
 def coordinates():
     x, z, yh, yl = (lax.axis_index(a) for a in ("x", "z", "yh", "yl"))
-    return {"x": x, "z": z, "y": yh * 2 + yl}
-
-
-def around(value, by):
-    return lax.rem(value + (by + 4), 4)
+    return {"x": x, "z": z, "y": yh * 2 + yl, "w": yh}
+
+
+def extent(axis):
+    return 2 if axis == "w" else 4
+
+
+def around(at, axis, by):
+    return lax.rem(at[axis] + (by + 4), extent(axis))
+
+
+def others(axis):
+    return (1,) if axis == "w" else (1, -1, 2)
 
 
 def peer(at, axis, by):
-    moved = around(at[axis], by)
+    value = around(at, axis, by)
     if axis == "y":
-        return {"yh": moved // 2, "yl": lax.rem(moved, 2)}
-    return {axis: moved}
+        return {"yh": value // 2, "yl": lax.rem(value, 2)}
+    return {"yh" if axis == "w" else axis: value}
 
 
 def sibling():
@@ -51,17 +60,26 @@
     return {"yl": 1 - lax.axis_index("yl")}
 
 
-def place(at, whole=(), half=None, moved=None):
+def slot(at, axis, by=0):
+    value = around(at, axis, by)
+    return lax.rem(value, 2) * 2 + value // 2 if axis == "y" else value
+
+
+def dimensions(order):
+    return ("w" if "w" in order else "y", "x", "z")
+
+
+def place(at, order, count, half=None, shifted=None):
     out = []
-    for axis in ("y", "x", "z"):
-        if axis in whole:
+    for axis in dimensions(order):
+        if axis in order[:count]:
+            size = extent(axis)
             if half is not None and half[0] == axis:
-                out.append(pl.ds(2 * half[1], 2))
+                out.append(pl.ds(size // 2 * half[1], size // 2))
             else:
-                out.append(pl.ds(0, 4))
+                out.append(pl.ds(0, size))
         else:
-            value = at[axis] if moved is None or moved[0] != axis else around(at[axis], moved[1])
-            out.append(lax.rem(value, 2) * 2 + value // 2 if axis == "y" else value)
+            out.append(slot(at, axis, shifted[1] if shifted is not None and shifted[0] == axis else 0))
     return tuple(out)
 
 
@@ -74,12 +92,6 @@
     pl.semaphore_wait(barrier, 10)
 
 
-def pair_greet():
-    barrier = pltpu.get_barrier_semaphore()
-    pl.semaphore_signal(barrier, inc=1, device_id=sibling(), device_id_type=MESH)
-    pl.semaphore_wait(barrier, 1)
-
-
 def sent(src, dst, send, recv, device):
     copy = pltpu.make_async_remote_copy(
         src_ref=src, dst_ref=dst, send_sem=send, recv_sem=recv, device_id=device, device_id_type=MESH
@@ -92,10 +104,6 @@
     copy = pltpu.make_async_copy(src, dst, sem)
     copy.start()
     return copy
-
-
-def halved(order):
-    return "x" if order[2] == "y" else "y"
 
 
 class Gather:
@@ -127,8 +135,8 @@
                 self.own[p].wait()
                 self.arrive(p, 0)
             else:
-                self.own.append(moved(self.srcs[p], self.outs[p].at[place(at)], self.local.at[p]))
-            group = self.outs[p].at[place(at, order[:stage])]
+                self.own.append(moved(self.srcs[p], self.outs[p].at[place(at, order, 0)], self.local.at[p]))
+            group = self.outs[p].at[place(at, order, stage)]
             self.direct[p, stage] = [
                 sent(
                     group if stage else self.srcs[p],
@@ -137,7 +145,7 @@
                     self.recv.at[p, stage, d],
                     peer(at, order[stage], by),
                 )
-                for d, by in enumerate((1, -1, 2))
+                for d, by in enumerate(others(order[stage]))
             ]
 
     def pass_on(self, p, stage, d, k, block):
@@ -157,15 +165,13 @@
             for t in range(2):
                 for d in range(2):
                     h = t if d == 0 else 1 - t
-                    self.pass_on(
-                        p, stage, d, h, self.outs[p].at[place(self.at, order[:stage], (order[0], h))]
-                    )
+                    self.pass_on(p, stage, d, h, self.outs[p].at[place(self.at, order, stage, (order[0], h))])
 
     def forward(self, stage):
         for p, order in enumerate(self.orders):
             for d, by in enumerate((1, -1)):
                 self.ring[p, stage, d, d].wait_recv()
-                where = place(self.at, order[:stage], (order[0], d), (order[stage], -by))
+                where = place(self.at, order, stage, (order[0], d), (order[stage], -by))
                 self.pass_on(p, stage, d, 2, self.outs[p].at[where])
 
     def finish(self):
@@ -190,16 +196,17 @@
     )
 
     @staticmethod
-    def buffers(columns):
+    def buffers(columns, orders):
         def per_piece(*shape):
             return [pltpu.VMEM(shape + (48, columns), BF) for _ in range(3)]
 
+        size = extent(dimensions(orders[0])[0])
         return [
-            *per_piece(2, 2, 4),
-            *per_piece(4, 4),
-            *per_piece(2, 2, 4),
-            *per_piece(2, 4, 4),
-            *per_piece(3, 4),
+            *per_piece(2, size // 2, 4),
+            *per_piece(size, 4),
+            *per_piece(2, size // 2, 4),
+            *per_piece(2, size, 4),
+            *per_piece(3, size),
             *per_piece(3),
             *[pltpu.VMEM((48, columns), F32) for _ in range(3)],
         ]
@@ -212,52 +219,55 @@
         self.load, self.first_send, self.first_recv, self.send, self.recv, self.end_send, self.end_recv = semaphores
         self.loads, self.copies = {}, {}
 
+    def left(self, p):
+        order = self.orders[p]
+        return [axis for axis in dimensions(order) if axis != order[2]]
+
+    def inside(self, p, first, second=None):
+        whole = slice(None) if second is None else second
+        return (first, whole) if self.left(p)[0] == self.orders[p][1] else (whole, first)
+
     def start(self):
         at, s, r = self.at, self.first_send, self.first_recv
         for p, order in enumerate(self.orders):
-            axis = order[2]
+            axis, cut = order[2], self.left(p)[0]
+            size = extent(cut) // 2
             for d, by in enumerate((1, -1)):
-                block = self.data[p].at[place(at, order[:2], (halved(order), d), (axis, 2))]
+                block = self.data[p].at[place(at, order, 2, (cut, d), (axis, 2))]
                 self.copies[p, d, 0] = sent(block, self.far[p].at[d], s.at[p, d, 0], r.at[p, d, 0], peer(at, axis, by))
             for d, by in enumerate((1, -1)):
                 h = 1 - d
-                block = self.data[p].at[place(at, order[:2], (halved(order), h), (axis, by))]
+                block = self.data[p].at[place(at, order, 2, (cut, h), (axis, by))]
                 self.copies[p, d, 1] = sent(
-                    block, self.near[p].at[d, pl.ds(2 * h, 2)], s.at[p, d, 1], r.at[p, d, 1], peer(at, axis, by)
+                    block, self.near[p].at[d, pl.ds(size * h, size)], s.at[p, d, 1], r.at[p, d, 1], peer(at, axis, by)
                 )
-                block = self.data[p].at[place(at, order[:2], (halved(order), d), (axis, by))]
+                block = self.data[p].at[place(at, order, 2, (cut, d), (axis, by))]
                 self.loads[p, d] = moved(block, self.side[p].at[d], self.load.at[p, d])
-            self.loads[p, 2] = moved(self.data[p].at[place(at, order[:2])], self.kept[p], self.load.at[p, 2])
+            self.loads[p, 2] = moved(self.data[p].at[place(at, order, 2)], self.kept[p], self.load.at[p, 2])
 
     def relay(self):
         for p, order in enumerate(self.orders):
+            size = extent(self.left(p)[0]) // 2
             for d, by in enumerate((1, -1)):
                 self.loads[p, d].wait()
                 self.copies[p, d, 0].wait_recv()
                 side, far = self.side[p], self.far[p]
 
-                @pl.loop(0, 8)
+                @pl.loop(0, 4 * size)
                 def _(i, d=d, side=side, far=far):
                     a, b = i // 4, lax.rem(i, 4)
                     side[d, a, b] = (side[d, a, b].astype(F32) + far[d, a, b].astype(F32)).astype(BF)
 
                 self.copies[p, d, 2] = sent(
                     side.at[d],
-                    self.near[p].at[d, pl.ds(2 * d, 2)],
+                    self.near[p].at[d, pl.ds(size * d, size)],
                     self.first_send.at[p, d, 2],
                     self.first_recv.at[p, d, 2],
                     peer(self.at, order[2], by),
                 )
 
-    def inner(self, p, by):
-        order = self.orders[p]
-        left = [a for a in ("y", "x", "z") if a != order[2]]
-        value = around(self.at[order[1]], by)
-        if order[1] == "y":
-            value = lax.rem(value, 2) * 2 + value // 2
-        return value, left[0] == order[1]
-
     def spread(self):
+        at = self.at
         for p, order in enumerate(self.orders):
             self.loads[p, 2].wait()
             for d in range(2):
@@ -265,62 +275,51 @@
                 self.copies[p, d, 2].wait_recv()
             kept, near = self.kept[p], self.near[p]
 
-            @pl.loop(0, 16)
+            @pl.loop(0, 4 * extent(self.left(p)[0]))
             def _(i, kept=kept, near=near):
                 a, b = i // 4, lax.rem(i, 4)
                 total = kept[a, b].astype(F32) + near[0, a, b].astype(F32) + near[1, a, b].astype(F32)
                 kept[a, b] = total.astype(BF)
 
-            for d, by in enumerate((1, -1, 2)):
-                value, first = self.inner(p, by)
-                block = kept.at[value] if first else kept.at[:, value]
+            for d, by in enumerate(others(order[1])):
+                block = kept.at[self.inside(p, slot(at, order[1], by))]
                 self.copies[p, "b", d] = sent(
-                    block, self.second[p].at[d], self.send.at[p, 0, d], self.recv.at[p, 0, d], peer(self.at, order[1], by)
+                    block, self.second[p].at[d], self.send.at[p, 0, d], self.recv.at[p, 0, d], peer(at, order[1], by)
                 )
 
     def narrow(self):
+        at = self.at
         for p, order in enumerate(self.orders):
-            for d in range(3):
+            for d in range(len(others(order[1]))):
                 self.copies[p, "b", d].wait_recv()
-            kept, second = self.kept[p], self.second[p]
-            value, first = self.inner(p, 0)
-
-            @pl.loop(0, 4)
-            def _(i, kept=kept, second=second, value=value, first=first):
-                where = (value, i) if first else (i, value)
-                total = kept[where].astype(F32)
+            kept, second, mine = self.kept[p], self.second[p], slot(at, order[1])
+
+            @pl.loop(0, extent(order[0]))
+            def _(i, p=p, kept=kept, second=second, mine=mine):
+                total = kept[self.inside(p, mine, i)].astype(F32)
                 for d in range(3):
                     total = total + second[d, i].astype(F32)
-                kept[where] = total.astype(BF)
-
-            for d, by in enumerate((1, -1, 2)):
-                index = around(self.at[order[0]], by)
-                if order[0] == "y":
-                    index = lax.rem(index, 2) * 2 + index // 2
-                block = kept.at[(value, index) if first else (index, value)]
+                kept[self.inside(p, mine, i)] = total.astype(BF)
+
+            for d, by in enumerate(others(order[0])):
+                block = kept.at[self.inside(p, mine, slot(at, order[0], by))]
                 self.copies[p, "c", d] = sent(
-                    block, self.third[p].at[d], self.send.at[p, 1, d], self.recv.at[p, 1, d], peer(self.at, order[0], by)
+                    block, self.third[p].at[d], self.send.at[p, 1, d], self.recv.at[p, 1, d], peer(at, order[0], by)
                 )
 
     def finish(self, outs):
-        core = lax.axis_index("core")
-        ends = []
+        at, core, ends = self.at, lax.axis_index("core"), []
         for p, order in enumerate(self.orders):
-            for d in range(3):
+            total = self.kept[p][self.inside(p, slot(at, order[1]), slot(at, order[0]))].astype(F32)
+            for d in range(len(others(order[0]))):
                 self.copies[p, "c", d].wait_recv()
-            value, first = self.inner(p, 0)
-            index = self.at[order[0]]
-            if order[0] == "y":
-                index = lax.rem(index, 2) * 2 + index // 2
-            total = self.kept[p][(value, index) if first else (index, value)].astype(F32)
-            for d in range(3):
                 total = total + self.third[p][d].astype(F32)
             self.sums[p][...] = total
             theirs = self.sums[p].at[pl.ds(pl.multiple_of(24 * (1 - core), 8), 24)]
             mine = self.sums[p].at[pl.ds(pl.multiple_of(24 * core, 8), 24)]
             ends.append(sent(theirs, outs[p].at[core], self.end_send.at[p, 0], self.end_recv.at[p, 0], sibling()))
             ends.append(moved(mine, outs[p].at[core], self.end_send.at[p, 1]))
-        for key, copy in self.copies.items():
+        for copy in self.copies.values():
             copy.wait_send()
         for copy in ends:
             copy.wait()
@@ -378,58 +377,52 @@
     )(*operands)
 
 
-def mlp_step(n2, cot, n2t, cott, gate_w, up_w, down_w, out_acc, grad_acc):
-    gate = nn(n2[...], gate_w)
-    up = nn(n2[...], up_w)
+def hidden_units(m, sub, n2, cot, weights, acts):
+    rows = rows_at(m * ROWS, ROWS)
+    columns = pl.ds(sub * CHUNK, CHUNK)
+    gate_w, up_w, down_w = (w[..., columns].reshape(-1, CHUNK) for w in weights)
+    gate = nn(n2[rows], gate_w)
+    up = nn(n2[rows], up_w)
     sigma = jax.nn.sigmoid(gate)
     silu = gate * sigma
-    active = (silu * up).astype(BF)
-    grad_active = nn(cot[...], down_w)
-    grad_gate = (grad_active * up * (sigma + silu * (1.0 - sigma))).astype(BF)
-    grad_up = (grad_active * silu).astype(BF)
-    out_acc[...] += nt(active, down_w)
-    grad_acc[...] += nt(grad_gate, gate_w) + nt(grad_up, up_w)
-    return (
-        nn(n2t[...], grad_gate).astype(BF),
-        nn(n2t[...], grad_up).astype(BF),
-        nn(cott[...], active).astype(BF),
-    )
-
-
-def mlp_chunk(step, acts, weights, accs, staging, outs, sems, waits):
-    y, sub = step // 2, step % 2
-    columns = pl.ds(sub * CHUNK, CHUNK)
-    values = mlp_step(*acts, *(w[pl.ds(2 * y, 2), :, :, :, columns].reshape(-1, CHUNK) for w in weights), *accs)
-    slot = step % 2
-    for p in range(3):
-        if (p, slot) in waits:
-            waits[p, slot].wait()
-        staging[slot, p] = values[p]
-        waits[p, slot] = moved(staging.at[slot, p], outs[p].at[y, :, columns], sems.at[p, slot])
+    grad_active = nn(cot[m].reshape(ROWS, -1), down_w)
+    acts[0][rows, columns] = (silu * up).astype(BF)
+    acts[1][rows, columns] = (grad_active * up * (sigma + silu * (1.0 - sigma))).astype(BF)
+    acts[2][rows, columns] = (grad_active * silu).astype(BF)
+
+
+def unit_gradients(n2t, cott, acts, staging, outs, sems):
+    waits = {}
+    for k, (left, right, target) in enumerate(((n2t, acts[1], 0), (n2t, acts[2], 1), (cott, acts[0], 2))):
+        for sub in range(2):
+            columns = pl.ds(sub * CHUNK, CHUNK)
+            place_in = (2 * k + sub) % 4
+            if place_in in waits:
+                waits[place_in].wait()
+            staging[place_in] = nn(left[...], right[:, columns]).astype(BF)
+            waits[place_in] = moved(staging.at[place_in], outs[target].at[:, columns], sems.at[place_in])
+    return list(waits.values())
 
 
 def forward_kernel(third, wide, *refs):
     own_weights, gains, lengths, xin, gin, tables = refs[:7], *refs[7:12]
-    refs = refs[8:]
-    full_two = refs[4:7]
+    full_two, full_one = refs[12:15], refs[15:18]
     (
-        x_out, cot_out, cott_out, n1t_out, q_out, kv_out, probs_out, mixed_out, hidden_out, n2_out, n2t_out,
-        out_acc_out, grad_acc_out,
-    ) = refs[7:20]
-    attn_out, grads_out = refs[20:23], refs[23:26]
+        x_out, n1t_out, q_out, kv_out, probs_out, mixed_out, hidden_out, n2_out, n2t_out, cot_out, cott_out,
+    ) = refs[18:29]
+    attn_out, grads_out, acts_out = refs[29:32], refs[32:35], refs[35:38]
     (
-        shard, got_shard, packed, xs, gs, normed, q, kv, probs, mixed, hidden, normed_two, part, arrived, turned, valid,
-        out_acc, grad_acc, staging,
-    ) = refs[26:45]
-    full_attn, weights = refs[45:48], refs[48:51]
-    attn_sems, one_sems, two_sems = refs[51:56], refs[56:61], refs[61:66]
-    pair_send, pair_recv, row_send, row_recv, out_sem, put_sem = refs[66:]
+        shard, got_shard, packed, xs, gs, normed, q, kv, probs, mixed, hidden, n2, n2t, cott, part, arrived, n1t,
+        valid, staging,
+    ) = refs[38:57]
+    full_attn, weights, acts = refs[57:60], refs[60:63], refs[63:66]
+    attn_sems, one_sems, two_sems = refs[66:71], refs[71:76], refs[76:81]
+    pair_send, pair_recv, row_send, row_recv, far_send, far_recv, own_sem, out_sem, put_sem = refs[81:]
     at = coordinates()
     core, yl = lax.axis_index("core"), lax.axis_index("yl")
-    own_x = moved(xin.at[yl], xs.at[core, yl], out_sem.at[0])
-    own_g = moved(gin.at[yl], gs.at[core, yl], out_sem.at[1])
-
-    column = 0
+    own_x = moved(xin.at[yl], xs.at[core, yl], own_sem.at[0])
+    own_g = moved(gin, gs.at[:, core, yl], own_sem.at[1])
+
     query, key, value, output, *mlp_weights = (ref[...].astype(F32) for ref in own_weights)
     gain_one, gain_two = gains[:, 0:1].astype(F32), gains[:, 1:2].astype(F32)
     small = key.shape[1] // 2
@@ -455,43 +448,56 @@
     swap_shard = sent(shard.at[1 - core], got_shard, pair_send.at[0], pair_recv.at[0], sibling())
 
     rows = {}
-    for k, (src, dst) in enumerate(((xin, xs), (gin, gs))):
-        rows[k, 0] = sent(src.at[1 - yl], dst.at[core, yl], row_send.at[k, 0], row_recv.at[k, 0], partner())
-        rows[k, 1] = sent(src.at[yl], dst.at[core, yl], row_send.at[k, 1], row_recv.at[k, 1], sibling())
+
+    def exchange(k):
+        ours, theirs, dst = (
+            (xin.at[yl], xin.at[1 - yl], xs.at[core, yl]),
+            (gin, gin, gs.at[:, core, yl]),
+        )[k]
+        rows[k, 0] = sent(theirs, dst, row_send.at[k, 0], row_recv.at[k, 0], partner())
+        rows[k, 1] = sent(ours, dst, row_send.at[k, 1], row_recv.at[k, 1], sibling())
+
+    def share(k):
+        block = (xs.at[core, 1 - yl], gs.at[:, core, 1 - yl])[k]
+        rows[k, 0].wait_recv()
+        rows[k, 2] = sent(block, block, row_send.at[k, 2], row_recv.at[k, 2], sibling())
+
+    def settle(k):
+        (own_x, own_g)[k].wait()
+        rows[k, 0].wait_send()
+        rows[k, 1].wait()
+        rows[k, 2].wait()
 
     swap_shard.wait()
     low, high = shard[core], got_shard[...]
     first, last = jnp.where(core == 0, low, high), jnp.where(core == 0, high, low)
     packed[...] = jnp.concatenate([first[:24], last[:24]], 0).astype(BF)
     for c, rows_of in enumerate((first, last)):
-        valid[c] = jnp.where(yl == 0, rows_of[24:32, :SEQ], rows_of[24:32, SEQ : 2 * SEQ])
+        for m in range(2):
+            valid[m, c] = rows_of[24:32, m * SEQ : (m + 1) * SEQ]
 
     def pieces(start, size, step):
         return [packed.at[:, pl.ds(start + k * step, size)] for k in range(3)]
 
     half = wide // 2
     attn = Gather(at, pieces(0, third, third), full_attn, attn_sems, EVEN)
-    one = Gather(at, pieces(3 * third, half, wide), weights, one_sems, SPARE_Y)
-    two = Gather(at, pieces(3 * third + half, half, wide), full_two, two_sems, SPARE_Y_TOO)
+    one = Gather(at, pieces(3 * third, half, wide), weights, one_sems, PLANE_Z)
+    two = Gather(at, pieces(3 * third + half, half, wide), full_two, two_sems, PLANE_X)
     attn.to_all(0)
     one.to_all(0)
     two.to_all(0)
     attn.to_all(1)
     one.spread(1)
+    exchange(0)
     attn.spread(2)
     one.forward(1)
-    for k, dst in enumerate((xs, gs)):
-        rows[k, 0].wait_recv()
-        rows[k, 2] = sent(dst.at[core, 1 - yl], dst.at[core, 1 - yl], row_send.at[k, 2], row_recv.at[k, 2], sibling())
+    two.spread(1)
     attn.forward(2)
+    two.forward(1)
     one.spread(2)
-    two.spread(1)
-    own_x.wait()
-    own_g.wait()
-    for k in range(2):
-        rows[k, 0].wait_send()
-        rows[k, 1].wait()
-        rows[k, 2].wait()
+    exchange(1)
+    share(0)
+    settle(0)
     outs = [moved(xs, x_out, out_sem.at[0])]
 
     @pl.loop(0, ROWS // STEP)
@@ -500,20 +506,10 @@
         values = xs[i // 2, lax.rem(i, 2)].astype(F32)
         normed[block] = (values * inverse_rms(values)).astype(BF)
 
-    turned[0] = normed[...].T
-    outs.append(moved(turned.at[0], n1t_out, out_sem.at[1]))
-
-    cot = arrived
-    for c in range(2):
-        for h in range(2):
-            block = pl.ds((2 * c + h) * STEP, STEP)
-            mask = valid[c][:, h * STEP : (h + 1) * STEP].T[:, 0:1]
-            gs[c, h] = (gs[c, h].astype(F32) * mask).astype(BF)
-    out_acc[...] = jnp.zeros_like(out_acc)
-    grad_acc[...] = jnp.zeros_like(grad_acc)
+    n1t[...] = normed[...].T
+    outs.append(moved(n1t, n1t_out, out_sem.at[1]))
     attn.finish()
-    two.forward(1)
-    outs.extend(moved(full_attn[p], attn_out[p], out_sem.at[12 + p]) for p in range(3))
+    outs.extend(moved(full_attn[p], attn_out[p], out_sem.at[2 + p]) for p in range(3))
     wq, wkv, wo = full_attn
 
     def weight(ref, y):
@@ -530,8 +526,8 @@
                 lin = nn(left, weight(w, y))
                 result[y, block] = (lin * tables[2 * k] + swap(lin, is_first) * tables[2 * k + 1]).astype(BF)
 
-    outs.append(moved(q, q_out, out_sem.at[3]))
-    outs.append(moved(kv, kv_out, out_sem.at[4]))
+    outs.append(moved(q, q_out, out_sem.at[5]))
+    outs.append(moved(kv, kv_out, out_sem.at[6]))
     one.forward(2)
     scale = 1.0 / math.sqrt(HEAD)
 
@@ -541,7 +537,7 @@
         block = rows_at(n * SEQ, SEQ)
         t = lax.broadcasted_iota(jnp.int32, (SEQ, SEQ), 0)
         s = lax.broadcasted_iota(jnp.int32, (SEQ, SEQ), 1)
-        keep = (s <= t) & (valid[n, 0:1, :] > 0.5)
+        keep = (s <= t) & (valid[yl, n, 0:1, :] > 0.5)
         queries, keys = q[y, block], kv[y, block]
         results = []
         for h in range(4):
@@ -549,98 +545,129 @@
             scores = nt(queries[:, h * HEAD : (h + 1) * HEAD], keys[:, g * HEAD : (g + 1) * HEAD]) * scale
             scores = jnp.where(keep, scores, -1e30)
             terms = jnp.exp(scores - jnp.max(scores, -1, keepdims=True))
-            low = (terms / jnp.sum(terms, -1, keepdims=True)).astype(BF)
-            probs[i, h] = low
-            results.append(nn(low, keys[:, (2 + g) * HEAD : (3 + g) * HEAD]))
+            low_probs = (terms / jnp.sum(terms, -1, keepdims=True)).astype(BF)
+            probs[i, h] = low_probs
+            results.append(nn(low_probs, keys[:, (2 + g) * HEAD : (3 + g) * HEAD]))
         mixed[y, block] = jnp.concatenate(results, -1).astype(BF)
 
-    outs.append(moved(probs, probs_out, out_sem.at[5]))
-    outs.append(moved(mixed, mixed_out, out_sem.at[6]))
+    outs.append(moved(probs, probs_out, out_sem.at[7]))
+    outs.append(moved(mixed, mixed_out, out_sem.at[8]))
+    two.spread(2)
+
     copies = []
     for i in range(ROWS // STEP):
-        block = pl.ds(i * STEP, STEP)
+        block = rows_at(lax.rem(2 * (1 - core) + i, 4) * STEP, STEP)
         part[block] = (nt(mixed[0, block], weight(wo, 0)) + nt(mixed[1, block], weight(wo, 1))).astype(BF)
         copies.append(sent(part.at[block], arrived.at[block], pair_send.at[1 + i], pair_recv.at[1 + i], sibling()))
-    two.spread(2)
+    second_rows = {}
+    mine, theirs = yl * ROWS, (1 - yl) * ROWS
     for i in range(ROWS // STEP):
-        block = pl.ds(i * STEP, STEP)
-        copies[i].wait()
-        values = xs[i // 2, i % 2].astype(F32) + (part[block].astype(F32) + arrived[block].astype(F32))
+        copies[(i + 2) % 4 if i < 2 else i - 2].wait_send()
+        copies[i].wait_recv()
+        number = lax.rem(2 * core + i, 4)
+        block = rows_at(number * STEP, STEP)
+        values = xs[number // 2, lax.rem(number, 2)].astype(F32) + (
+            part[block].astype(F32) + arrived[block].astype(F32)
+        )
         hidden[block] = values
-        normed_two[block] = (values * inverse_rms(values)).astype(BF)
-    outs.append(moved(hidden, hidden_out, out_sem.at[7]))
-    outs.append(moved(normed_two, n2_out, out_sem.at[8]))
-    turned[1] = normed_two[...].T
-    outs.append(moved(turned.at[1], n2t_out, out_sem.at[9]))
-    for i in range(ROWS // STEP):
-        cot[pl.ds(i * STEP, STEP)] = gs[i // 2, i % 2]
-    turned[2] = cot[...].T
-    outs.append(moved(cot, cot_out, out_sem.at[10]))
-    outs.append(moved(turned.at[2], cott_out, out_sem.at[11]))
+        target = rows_at(mine + number * STEP, STEP)
+        n2[target] = (values * inverse_rms(values)).astype(BF)
+        if i < 2:
+            second_rows[0, i] = sent(n2.at[target], n2.at[target], far_send.at[0, i], far_recv.at[0, i], partner())
+    outs.append(moved(hidden.at[rows_at(core * SEQ, SEQ)], hidden_out, out_sem.at[9]))
+    share(1)
+    settle(1)
+
+    for m in range(2):
+        for c in range(2):
+            for h in range(2):
+                mask = valid[m, c][:, h * STEP : (h + 1) * STEP].T[:, 0:1]
+                gs[m, c, h] = (gs[m, c, h].astype(F32) * mask).astype(BF)
+    outs.append(moved(gs, cot_out, out_sem.at[10]))
+
     one.finish()
-    acts, accs, waits = (normed_two, cot, turned.at[1], turned.at[2]), (out_acc, grad_acc), {}
-    for step in range(4):
-        mlp_chunk(step, acts, weights, accs, staging, grads_out, put_sem, waits)
-        if step == 1:
-            two.forward(2)
-    outs.append(moved(out_acc, out_acc_out, out_sem.at[2]))
-    outs.append(moved(grad_acc, grad_acc_out, out_sem.at[15]))
+    outs.extend(moved(weights[p], full_one[p], out_sem.at[11 + p]) for p in range(3))
+    for i in range(2):
+        second_rows[0, i].wait_recv()
+        block = rows_at(theirs + (2 * core + i) * STEP, STEP)
+        second_rows[1, i] = sent(n2.at[block], n2.at[block], far_send.at[1, i], far_recv.at[1, i], sibling())
+    for sub in range(2):
+        hidden_units(yl, sub, n2, gs, weights, acts)
+    for m in range(2):
+        for c in range(2):
+            for h in range(2):
+                cott[:, pl.ds(m * ROWS + (2 * c + h) * STEP, STEP)] = gs[m, c, h].T
+    outs.append(moved(cott, cott_out, out_sem.at[14]))
+    two.forward(2)
+    for i in range(2):
+        second_rows[0, i].wait_send()
+        second_rows[1, i].wait()
+    for sub in range(2):
+        hidden_units(1 - yl, sub, n2, gs, weights, acts)
+    outs.extend(moved(acts[p], acts_out[p], out_sem.at[15 + p]) for p in range(3))
+    outs.append(moved(n2, n2_out, out_sem.at[18]))
+    for i in range(2 * ROWS // STEP):
+        n2t[:, pl.ds(i * STEP, STEP)] = n2[pl.ds(i * STEP, STEP)].T
+    outs.append(moved(n2t, n2t_out, out_sem.at[19]))
+    outs.extend(unit_gradients(n2t, cott, acts, staging, grads_out, put_sem))
     two.finish()
-    for copy in (*outs, *waits.values()):
+    for copy in outs:
         copy.wait()
 
 
 def forward(own_weights, gains, lengths, xin, gin, tables, third, wide):
     width = xin.shape[2]
     rows = (ROWS, width)
+    both = (2 * ROWS, width)
     heads = (2, ROWS, third)
     square = (4, 4, SEQ, SEQ)
     half = wide // 2
+    piece = (2, 4, 4, 48, half)
     return call(
         lambda *refs: forward_kernel(third, wide, *refs),
         (*own_weights, gains, lengths, xin, gin, tables),
         [VMEM] * 8 + [pl.BlockSpec(memory_space=pltpu.SMEM), ANY, ANY, VMEM],
-        [shaped((4, 4, 4, 48, half))] * 3
+        [shaped(piece)] * 6
         + [
             shaped((2, 2, 128, width)),
-            shaped(rows),
-            shaped(rows[::-1]),
             shaped(rows[::-1]),
             shaped(heads),
             shaped(heads),
             shaped(square),
             shaped(heads),
-            shaped(rows, F32),
-            shaped(rows),
-            shaped(rows[::-1]),
-            shaped(rows, F32),
-            shaped(rows, F32),
+            shaped((SEQ, width), F32),
+            shaped(both),
+            shaped(both[::-1]),
+            shaped((2, 2, 2, 128, width)),
+            shaped(both[::-1]),
         ]
         + [shaped((4, 4, 4, 48, third))] * 3
-        + [shaped((2, width, half))] * 3,
-        [ANY] * 22,
+        + [shaped((width, half))] * 3
+        + [shaped((2 * ROWS, half))] * 3,
+        [ANY] * 26,
         [
             pltpu.VMEM((2, 32, 3 * third + 3 * wide), F32),
             pltpu.VMEM((32, 3 * third + 3 * wide), F32),
             pltpu.VMEM((48, 3 * third + 3 * wide), BF),
             pltpu.VMEM((2, 2, 128, width), BF),
-            pltpu.VMEM((2, 2, 128, width), BF),
+            pltpu.VMEM((2, 2, 2, 128, width), BF),
             pltpu.VMEM(rows, BF),
             pltpu.VMEM(heads, BF),
             pltpu.VMEM(heads, BF),
             pltpu.VMEM(square, BF),
             pltpu.VMEM(heads, BF),
             pltpu.VMEM(rows, F32),
+            pltpu.VMEM(both, BF),
+            pltpu.VMEM(both[::-1], BF),
+            pltpu.VMEM(both[::-1], BF),
             pltpu.VMEM(rows, BF),
             pltpu.VMEM(rows, BF),
-            pltpu.VMEM(rows, BF),
-            pltpu.VMEM((3,) + rows[::-1], BF),
-            pltpu.VMEM((2, 8, SEQ), F32),
-            pltpu.VMEM(rows, F32),
-            pltpu.VMEM(rows, F32),
-            pltpu.VMEM((2, 3, width, CHUNK), BF),
+            pltpu.VMEM(rows[::-1], BF),
+            pltpu.VMEM((2, 2, 8, SEQ), F32),
+            pltpu.VMEM((4, width, CHUNK), BF),
             *[pltpu.VMEM((4, 4, 4, 48, third), BF) for _ in range(3)],
-            *[pltpu.VMEM((4, 4, 4, 48, half), BF) for _ in range(3)],
+            *[pltpu.VMEM(piece, BF) for _ in range(3)],
+            *[pltpu.VMEM((2 * ROWS, half), BF) for _ in range(3)],
             *Gather.semaphores,
             *Gather.semaphores,
             *Gather.semaphores,
@@ -648,8 +675,11 @@
             pltpu.SemaphoreType.DMA((5,)),
             pltpu.SemaphoreType.DMA((2, 3)),
             pltpu.SemaphoreType.DMA((2, 3)),
-            pltpu.SemaphoreType.DMA((16,)),
-            pltpu.SemaphoreType.DMA((3, 2)),
+            pltpu.SemaphoreType.DMA((2, 2)),
+            pltpu.SemaphoreType.DMA((2, 2)),
+            pltpu.SemaphoreType.DMA((2,)),
+            pltpu.SemaphoreType.DMA((20,)),
+            pltpu.SemaphoreType.DMA((4,)),
         ],
         "gather_attn_forward_mlp",
         1,
@@ -657,108 +687,152 @@
 
 
 def middle_kernel(*refs):
-    n2_in, cot_in, hidden_in, n2t_in, cott_in, out_acc_in, grad_acc_in = refs[:7]
-    weights_in, data = refs[7:10], refs[10:13]
-    sums_out, grads_out = refs[13:16], refs[16:19]
-    result_out, branch_out, grad_hidden_out = refs[19:22]
-    (
-        n2, cot, hidden, n2t, cott, out_acc, grad_acc, staging, out_part, out_in, grad_part, grad_in, result, branch,
-    ) = refs[22:36]
-    weights, buffers = refs[36:39], refs[39:60]
-    reduce_sems = refs[60:67]
-    load, put, put_sem, send, recv = refs[67:]
-    core = lax.axis_index("core")
+    n2_in, cot_in, hidden_in, n2t_in, cott_in = refs[:5]
+    one_in, two_in, acts_in, data = refs[5:8], refs[8:11], refs[11:14], refs[14:17]
+    sums_out, grads_out = refs[17:20], refs[20:23]
+    result_out, branch_out, grad_hidden_out = refs[23:26]
+    n2, cot, hidden, n2t, cott, staging, to_pair, from_pair, to_far, from_far, keep, result, branch, gh = refs[26:40]
+    one, two, acts_one, acts_two = refs[40:43], refs[43:46], refs[46:49], refs[49:52]
+    buffers, reduce_sems = refs[52:73], refs[73:80]
+    load, put, put_sem, pair_send, pair_recv, far_send, far_recv = refs[80:]
+    core, yl = lax.axis_index("core"), lax.axis_index("yl")
     at = coordinates()
-    loads = [
-        moved(src, dst, load.at[k])
-        for k, (src, dst) in enumerate(
-            (
-                (n2_in, n2),
-                (weights_in[0], weights[0]),
-                (weights_in[1], weights[1]),
-                (cot_in, cot),
-                (weights_in[2], weights[2]),
-                (n2t_in, n2t),
-                (cott_in, cott),
-                (out_acc_in, out_acc),
-                (grad_acc_in, grad_acc),
-                (hidden_in, hidden),
-            )
+    order = (
+        (n2_in, n2),
+        (two_in[0], two[0]),
+        (two_in[1], two[1]),
+        (cot_in, cot),
+        (two_in[2], two[2]),
+        *zip(acts_in[1:], acts_one[1:]),
+        *zip(one_in[:2], one[:2]),
+        (acts_in[0], acts_one[0]),
+        (one_in[2], one[2]),
+        (n2t_in, n2t),
+        (cott_in, cott),
+        (hidden_in, hidden),
+    )
+    loads = [moved(src, dst, load.at[k]) for k, (src, dst) in enumerate(order)]
+    greet(at)
+    total = Reduce(at, data, buffers, reduce_sems, PLANE_Z)
+    total.start()
+    for k in range(5):
+        loads[k].wait()
+    for sub in range(2):
+        hidden_units(1 - yl, sub, n2, cot, two, acts_two)
+    for k in range(5, 11):
+        loads[k].wait()
+
+    def weight(ref):
+        return ref[...].reshape(n2.shape[1], -1)
+
+    def grad_rows(m, c):
+        rows = rows_at(m * ROWS + c * SEQ, SEQ)
+        return (nt(acts_one[1][rows], weight(one[0])) + nt(acts_one[2][rows], weight(one[1]))) + (
+            nt(acts_two[1][rows], weight(two[0])) + nt(acts_two[2][rows], weight(two[1]))
         )
-    ]
-    greet(at)
-    total = Reduce(at, data, buffers, reduce_sems, EVEN)
-    total.start()
-    for k in range(9):
+
+    def out_rows(m, c):
+        rows = rows_at(m * ROWS + c * SEQ, SEQ)
+        return nt(acts_one[0][rows], weight(one[2])) + nt(acts_two[0][rows], weight(two[2]))
+
+    pair, far = {}, {}
+
+    def to_sibling(k, value):
+        to_pair[k] = value.astype(BF)
+        pair[k] = sent(to_pair.at[k], from_pair.at[k], pair_send.at[k], pair_recv.at[k], sibling())
+
+    def to_partner(k, value):
+        pair[k].wait_recv()
+        to_far[k] = (value + from_pair[k].astype(F32)).astype(BF)
+        far[k] = sent(to_far.at[k], from_far.at[k], far_send.at[k], far_recv.at[k], partner())
+
+    to_sibling(0, grad_rows(1 - yl, 1 - core))
+    to_partner(0, grad_rows(1 - yl, core))
+    to_sibling(1, out_rows(1 - yl, 1 - core))
+    total.relay()
+    to_partner(1, out_rows(1 - yl, core))
+    for sub in range(2):
+        hidden_units(yl, sub, n2, cot, two, acts_two)
+    to_sibling(2, grad_rows(yl, 1 - core))
+    keep[...] = grad_rows(yl, core)
+    for k in range(11, 14):
         loads[k].wait()
-    acts, accs, waits = (n2, cot, n2t, cott), (out_acc, grad_acc), {}
-    for step in range(4):
-        mlp_chunk(step, acts, weights, accs, staging, grads_out, put_sem, waits)
-        if step == 2:
-            total.relay()
-    own = rows_at(core * SEQ, SEQ)
-    other = rows_at((1 - core) * SEQ, SEQ)
-    grad_part[...] = grad_acc[...].astype(BF)
-    copies = [sent(grad_part, grad_in, send.at[0], recv.at[0], sibling())]
-    out_part[...] = out_acc[other].astype(BF)
-    copies.append(sent(out_part, out_in, send.at[1], recv.at[1], sibling()))
-    loads[9].wait()
-    total.spread()
-    copies[0].wait()
-
-    @pl.loop(0, ROWS // STEP)
+    pair[2].wait_recv()
+    far[0].wait_recv()
+
+    @pl.loop(0, SEQ // STEP)
     def _(i):
         rows = rows_at(i * STEP, STEP)
-        grad = grad_part[rows].astype(F32) + grad_in[rows].astype(F32)
+        grad = keep[rows] + (from_pair[2, rows].astype(F32) + from_far[0, rows].astype(F32))
         values = hidden[rows]
         inverse = inverse_rms(values)
         unit = values * inverse
         back = inverse * (grad - unit * jnp.mean(grad * unit, -1, keepdims=True))
-        grad_acc[rows] = cot[rows].astype(F32) + back
-        branch[rows] = grad_acc[rows].astype(BF)
-
-    outs = [moved(branch, branch_out, put.at[0]), moved(grad_acc.at[own], grad_hidden_out, put.at[1])]
-    copies[1].wait()
-    result[...] = (hidden[own] + (out_acc[own] + out_in[...].astype(F32))).astype(BF)
+        gh[rows] = cot[yl, core, i].astype(F32) + back
+        branch[rows] = gh[rows].astype(BF)
+
+    own = rows_at(core * SEQ, SEQ)
+    shared = sent(branch, branch_out.at[own], pair_send.at[4], pair_recv.at[4], sibling())
+    outs = [moved(branch, branch_out.at[own], put.at[0]), moved(gh, grad_hidden_out, put.at[1])]
+    to_sibling(3, out_rows(yl, 1 - core))
+    keep[...] = out_rows(yl, core)
+    total.spread()
+    pair[3].wait_recv()
+    far[1].wait_recv()
+
+    @pl.loop(0, SEQ // STEP)
+    def _(i):
+        rows = rows_at(i * STEP, STEP)
+        change = keep[rows] + (from_pair[3, rows].astype(F32) + from_far[1, rows].astype(F32))
+        result[rows] = (hidden[rows] + change).astype(BF)
+
     outs.append(moved(result, result_out, put.at[2]))
+    outs.extend(unit_gradients(n2t, cott, acts_two, staging, grads_out, put_sem))
     total.narrow()
     total.finish(sums_out)
-    for copy in (*outs, *waits.values()):
+    shared.wait()
+    for copy in (*pair.values(), *far.values()):
+        copy.wait_send()
+    for copy in outs:
         copy.wait()
 
 
-def middle(n2, cot, hidden, n2t, cott, out_acc, grad_acc, weights, data):
+def middle(n2, cot, hidden, n2t, cott, one, two, acts, data):
     rows, width = n2.shape
-    half = weights[0].shape[-1]
+    half = one[0].shape[-1]
+    block = (SEQ, width)
     return call(
         middle_kernel,
-        (n2, cot, hidden, n2t, cott, out_acc, grad_acc, *weights, *data),
-        [ANY] * 13,
+        (n2, cot, hidden, n2t, cott, *one, *two, *acts, *data),
+        [ANY] * 17,
         [shaped((2, 24, half), F32)] * 3
-        + [shaped((2, width, half))] * 3
-        + [shaped((SEQ, width)), shaped((rows, width)), shaped((SEQ, width), F32)],
+        + [shaped((width, half))] * 3
+        + [shaped(block), shaped((ROWS, width)), shaped(block, F32)],
         [ANY] * 9,
         [
             pltpu.VMEM((rows, width), BF),
-            pltpu.VMEM((rows, width), BF),
-            pltpu.VMEM((rows, width), F32),
+            pltpu.VMEM(cot.shape, BF),
+            pltpu.VMEM(block, F32),
             pltpu.VMEM((width, rows), BF),
             pltpu.VMEM((width, rows), BF),
-            pltpu.VMEM((rows, width), F32),
-            pltpu.VMEM((rows, width), F32),
-            pltpu.VMEM((2, 3, width, CHUNK), BF),
-            pltpu.VMEM((SEQ, width), BF),
-            pltpu.VMEM((SEQ, width), BF),
-            pltpu.VMEM((rows, width), BF),
-            pltpu.VMEM((rows, width), BF),
-            pltpu.VMEM((SEQ, width), BF),
-            pltpu.VMEM((rows, width), BF),
-            *[pltpu.VMEM((4, 4, 4, 48, half), BF) for _ in range(3)],
-            *Reduce.buffers(half),
+            pltpu.VMEM((4, width, CHUNK), BF),
+            pltpu.VMEM((4,) + block, BF),
+            pltpu.VMEM((4,) + block, BF),
+            pltpu.VMEM((2,) + block, BF),
+            pltpu.VMEM((2,) + block, BF),
+            pltpu.VMEM(block, F32),
+            pltpu.VMEM(block, BF),
+            pltpu.VMEM(block, BF),
+            pltpu.VMEM(block, F32),
+            *[pltpu.VMEM(one[0].shape, BF) for _ in range(6)],
+            *[pltpu.VMEM((rows, half), BF) for _ in range(6)],
+            *Reduce.buffers(half, PLANE_Z),
             *Reduce.semaphores,
-            pltpu.SemaphoreType.DMA((10,)),
+            pltpu.SemaphoreType.DMA((14,)),
             pltpu.SemaphoreType.DMA((3,)),
-            pltpu.SemaphoreType.DMA((3, 2)),
+            pltpu.SemaphoreType.DMA((4,)),
+            pltpu.SemaphoreType.DMA((5,)),
+            pltpu.SemaphoreType.DMA((5,)),
             pltpu.SemaphoreType.DMA((2,)),
             pltpu.SemaphoreType.DMA((2,)),
         ],
@@ -800,8 +874,8 @@
         )
     ]
     greet(at)
-    mlp_sum = Reduce(at, data, mlp_buffers, mlp_sems, SPARE_Y_TOO)
-    attn_sum = Reduce(at, attn_grads, attn_buffers, attn_sems, SPARE_Y)
+    mlp_sum = Reduce(at, data, mlp_buffers, mlp_sems, PLANE_X)
+    attn_sum = Reduce(at, attn_grads, attn_buffers, attn_sems, SPARE_X)
     mlp_sum.start()
     halves = [
         moved(result.at[yl], result_out.at[yl], put.at[0]),
@@ -934,8 +1008,8 @@
             pltpu.VMEM(half, F32),
             pltpu.VMEM(half[1:], BF),
             pltpu.VMEM((2, 2, 4, 4, 48, third), BF),
-            *Reduce.buffers(wide),
-            *Reduce.buffers(third),
+            *Reduce.buffers(wide, PLANE_X),
+            *Reduce.buffers(third, SPARE_X),
             *Reduce.semaphores,
             *Reduce.semaphores,
             pltpu.SemaphoreType.DMA((11,)),
@@ -993,18 +1067,21 @@
     third, wide = query_weight.shape[1] // 2, gate_weight.shape[1] // 2
     tables = jnp.asarray(np.concatenate([tables_for(SEQ, 4, 0), tables_for(SEQ, 2, 2 * HEAD)]))
 
-    *two, x, cot, cott, n1t, q, kv, probs, mixed, hidden, n2, n2t, out_acc, grad_acc, wq, wkv, wo, dg, du, dd = forward(
+    results = forward(
         own_weights, jnp.stack([attn_gain, mlp_gain], 1), lengths, inputs, out_grad, tables, third, wide
     )
+    two, one = results[:3], results[3:6]
+    x, n1t, q, kv, probs, mixed, hidden, n2, n2t, cot, cott = results[6:17]
+    (wq, wkv, wo), grads, acts = results[17:20], results[20:23], results[23:26]
 
     def joined(w):
         return w.reshape(2, width, -1)
 
     def blocked(w):
-        return w.reshape(4, 4, 4, 48, -1)
+        return w.reshape(2, 4, 4, 48, -1)
 
     *one_sums, dg, du, dd, result, branch, grad_hidden = middle(
-        n2, cot, hidden, n2t, cott, out_acc, grad_acc, two, [blocked(w) for w in (dg, du, dd)]
+        n2, cot, hidden, n2t, cott, one, two, acts, [blocked(w) for w in grads]
     )
     *sums, _, _, _, result, in_grad, in_grad_theirs = backward(
         x,

time: 296 us -> 278 us (0.939)
  Pallas kernels: 273 us -> 256 us
    pallas_call x3, Pallas kernels: 273 us -> 256 us  [call(): pl.pallas_call(kernel, out_shape=results, in_specs=in_specs, out_specs=ou...]
where the time goes in v5:
time: 278 us; the launch traced here: 274 us
  Pallas kernels  256 us (92%)
  local copies, waits for them, and re-layouts  6.91 us (2%)
  other arithmetic  6.58 us (2%)
  blocking collectives  3.79 us (1%)
    pallas_call x3, Pallas kernels, call(): pl.pallas_call(kernel, out_shape=results, in_specs=in_specs, out_specs=ou...  256 us

profile of v5, /device:TPU:1, one launch (start us, length us, event | category | flops | bytes accessed | tf_op | source)
XLA Modules:
  0.0 274.3 jit_solution(16262051148467480238)
XLA Ops:
  0.6 0.7 pad_maximum_fusion.1
  1.3 0.7 copy.37.refs_7_
  2.0 1.3 copy.38.refs_8_
  3.3 115.0 %gather_attn_forward_mlp.1 = (bf16[2,4,4,48,512]{4,3,2,1,0:T(8,128)(2,1)}, bf16[2,4,4,48,512]{4,3,2,1,0:T(8,128)(2,1)}, bf16[2,4,4,48,512]{4,3,2,1,0:T(8,128)(2,...) custom-call(bf16[24,768]{1,0:T(8,128)(2,1)} %refs_0_.1, ...), custom_call_target="tpu_custom_call" | custom-call | tf_op jit(solution)/shard_map/gather_attn_forward_mlp/pallas_call | solution.py:366
  118.3 63.2 %mlp_reduce.1 = (f32[2,24,512]{2,1,0:T(8,128)}, f32[2,24,512]{2,1,0:T(8,128)}, f32[2,24,512]{2,1,0:T(8,128)}, bf16[1536,512]{1,0:T(8,128)(2,1)}, bf16[1536,512]{...) custom-call(bf16[1024,1536]{1,0:T(8,128)(2,1)} %get-tuple-element.56, ...), custom_call_target="tpu_custom_call" | custom-call | tf_op jit(solution)/shard_map/mlp_reduce/pallas_call | solution.py:366
  181.6 0.0 copy-start.13
  181.6 0.0 copy-start.10
  181.6 0.0 copy-start.11
  181.6 0.0 copy-start.5
  181.6 0.0 copy-start.6
  181.6 0.0 copy-start.7
  181.7 77.6 %attn_backward_reduce.1 = (f32[2,24,512]{2,1,0:T(8,128)}, f32[2,24,512]{2,1,0:T(8,128)}, f32[2,24,512]{2,1,0:T(8,128)}, f32[2,24,384]{2,1,0:T(8,128)}, f32[2,24,...) custom-call(bf16[2,2,128,1536]{3,2,1,0:T(8,128)(2,1)} %get-tuple-ele, ...), custom_call_target="tpu_custom_call" | custom-call | tf_op jit(solution)/shard_map/attn_backward_reduce/pallas_call | solution.py:366
  259.3 0.0 copy-start.14
  259.3 0.0 copy-start.2
  259.3 0.0 copy-start.3
  259.3 1.0 slice_bitcast_fusion
  260.3 0.1 reshape.126
  260.4 0.1 reshape.127
  260.5 0.0 copy-done.13
  260.6 0.0 copy-start.8
  260.6 0.0 copy-start.9
  260.6 0.0 copy-done.10
  260.6 0.0 copy-done.11
  260.6 0.8 multiply_reduce_fusion.3
  261.4 0.9 copy.46
  262.3 0.0 copy-done.5
  262.3 0.8 multiply_reduce_fusion.2
  263.1 0.0 copy-done.6
  263.1 0.0 copy-done.7
  263.2 0.0 copy-start.4
  263.2 1.0 maximum_bitcast_fusion
  264.2 0.0 copy-done.14
  264.2 0.0 copy-done.2
  264.2 0.0 copy-start.1
  264.3 0.9 multiply_reduce_fusion.1
  265.1 0.0 copy-done.3
  265.2 0.9 multiply_reduce_fusion
  266.0 3.8 %psum.7 = f32[2,24]{1,0:T(2,128)S(1)} all-reduce(f32[2,24]{1,0:T(2,128)S(1)} %pad_maximum_fusion), channel_id=1, replica_groups=mesh['yh'=2,'x'=4,'z'=4,'core'=2,'yl'=2] {'yl'}, use_global_device_ids=true, to_apply=%region_5.6 | all-reduce | flops 48 | bytes 384 | tf_op jit(solution)/shard_map/psum | solution.py:1120
  269.8 0.5 slice_bitcast_fusion.2
  270.4 0.0 copy-done.8
  270.4 0.0 copy-done.9
  270.4 0.7 copy.50
  271.1 0.0 copy-done.4
  271.1 0.1 convert_element_type.25
  271.2 0.0 copy-done.1
  271.2 0.0 copy-start.12
  271.2 0.0 copy-start
  271.2 1.4 broadcast_select_fusion
  272.6 0.0 copy-done.12
  272.6 0.6 copy.47
  273.2 0.0 copy-done
  273.2 0.9 copy.52
  (11 shorter events, 0.1 us)
Async XLA Ops:
  181.6 79.0 %copy-start.13 = (bf16[24]{0:T(256)(128)(2,1)S(1)}, bf16[24]{0:T(256)(128)(2,1)}, u32[]{:S(2)}) copy-start(bf16[24]{0:T(256)(128)(2,1)} %param.23) | copy-start | bytes 148
  181.6 79.0 %copy-start.10 = (bf16[24,384]{1,0:T(8,128)(2,1)S(1)}, bf16[24,384]{1,0:T(8,128)(2,1)}, u32[]{:S(2)}) copy-start(bf16[24,384]{1,0:T(8,128)(2,1)} %refs_1_.1) | copy-start | bytes 55300
  181.6 79.0 %copy-start.11 = (bf16[24,384]{1,0:T(8,128)(2,1)S(1)}, bf16[24,384]{1,0:T(8,128)(2,1)}, u32[]{:S(2)}) copy-start(bf16[24,384]{1,0:T(8,128)(2,1)} %refs_2_.1) | copy-start | bytes 55300
  181.6 80.7 %copy-start.5 = (bf16[24,768]{1,0:T(8,128)(2,1)S(1)}, bf16[24,768]{1,0:T(8,128)(2,1)}, u32[]{:S(2)}) copy-start(bf16[24,768]{1,0:T(8,128)(2,1)} %refs_0_.1) | copy-start | bytes 110596
  181.6 81.5 %copy-start.6 = (f32[2,24,512]{2,1,0:T(8,128)S(1)}, f32[2,24,512]{2,1,0:T(8,128)}, u32[]{:S(2)}) copy-start(f32[2,24,512]{2,1,0:T(8,128)} %get-tuple-element.93) | copy-start | bytes 294916
  181.6 81.5 %copy-start.7 = (f32[2,24,512]{2,1,0:T(8,128)S(1)}, f32[2,24,512]{2,1,0:T(8,128)}, u32[]{:S(2)}) copy-start(f32[2,24,512]{2,1,0:T(8,128)} %get-tuple-element.95) | copy-start | bytes 294916
  259.3 4.9 %copy-start.14 = (bf16[24]{0:T(256)(128)(2,1)S(1)}, bf16[24]{0:T(256)(128)(2,1)}, u32[]{:S(2)}) copy-start(bf16[24]{0:T(256)(128)(2,1)} %param.24) | copy-start | bytes 148
  259.3 4.9 %copy-start.2 = (bf16[24,2048]{1,0:T(8,128)(2,1)S(1)}, bf16[24,2048]{1,0:T(8,128)(2,1)}, u32[]{:S(2)}) copy-start(bf16[24,2048]{1,0:T(8,128)(2,1)} %refs_4_.1) | copy-start | bytes 294916
  259.3 5.8 %copy-start.3 = (bf16[24,2048]{1,0:T(8,128)(2,1)S(1)}, bf16[24,2048]{1,0:T(8,128)(2,1)}, u32[]{:S(2)}) copy-start(bf16[24,2048]{1,0:T(8,128)(2,1)} %refs_5_.1) | copy-start | bytes 294916
  260.6 9.8 %copy-start.8 = (f32[2,24,512]{2,1,0:T(8,128)S(1)}, f32[2,24,512]{2,1,0:T(8,128)}, u32[]{:S(2)}) copy-start(f32[2,24,512]{2,1,0:T(8,128)} %get-tuple-element.97) | copy-start | bytes 294916
  260.6 9.8 %copy-start.9 = (f32[2,24,512]{2,1,0:T(8,128)S(1)}, f32[2,24,512]{2,1,0:T(8,128)}, u32[]{:S(2)}) copy-start(f32[2,24,512]{2,1,0:T(8,128)} %get-tuple-element.98) | copy-start | bytes 294916
  263.2 7.9 %copy-start.4 = (bf16[128,1536]{1,0:T(8,128)(2,1)S(1)}, bf16[128,1536]{1,0:T(8,128)(2,1)}, u32[]{:S(2)}) copy-start(bf16[128,1536]{1,0:T(8,128)(2,1)} %get-tuple-element.89) | copy-start | bytes 1179652
  264.2 6.9 %copy-start.1 = (f32[128,1536]{1,0:T(8,128)S(1)}, f32[128,1536]{1,0:T(8,128)}, u32[]{:S(2)}) copy-start(f32[128,1536]{1,0:T(8,128)} %get-tuple-element.88) | copy-start | bytes 2359300
  271.2 1.4 copy-start.12
  271.2 2.0 copy-start

commit v6 on v5

--- a/solution.py
+++ b/solution.py
@@ -18,7 +18,7 @@
 BF = jnp.bfloat16
 F32 = jnp.float32
 EVEN = (("x", "y", "z"), ("y", "z", "x"), ("z", "x", "y"))
-SPARE_X = (("y", "z", "x"), ("x", "y", "z"), ("x", "z", "y"))
+SPARE_Y = (("x", "z", "y"), ("y", "x", "z"), ("y", "z", "x"))
 PLANE_Z = (("w", "x", "z"), ("w", "z", "x"), ("w", "x", "z"))
 PLANE_X = (("w", "z", "x"), ("w", "x", "z"), ("w", "z", "x"))
 SEQ = 256
@@ -157,8 +157,9 @@
             peer(self.at, self.orders[p][stage], 1 - 2 * d),
         )
 
-    def spread(self, stage):
-        for p, order in enumerate(self.orders):
+    def spread(self, stage, *pieces):
+        for p in pieces or range(3):
+            order = self.orders[p]
             if stage == 1:
                 self.own[p].wait()
             self.arrive(p, stage - 1)
@@ -175,8 +176,6 @@
                 self.pass_on(p, stage, d, 2, self.outs[p].at[where])
 
     def finish(self):
-        for p in range(3):
-            self.arrive(p, 2)
         for copies in self.direct.values():
             for copy in copies:
                 copy.wait_send()
@@ -227,9 +226,10 @@
         whole = slice(None) if second is None else second
         return (first, whole) if self.left(p)[0] == self.orders[p][1] else (whole, first)
 
-    def start(self):
+    def start(self, *pieces):
         at, s, r = self.at, self.first_send, self.first_recv
-        for p, order in enumerate(self.orders):
+        for p in pieces or range(3):
+            order = self.orders[p]
             axis, cut = order[2], self.left(p)[0]
             size = extent(cut) // 2
             for d, by in enumerate((1, -1)):
@@ -383,7 +383,7 @@
     gate_w, up_w, down_w = (w[..., columns].reshape(-1, CHUNK) for w in weights)
     gate = nn(n2[rows], gate_w)
     up = nn(n2[rows], up_w)
-    sigma = jax.nn.sigmoid(gate)
+    sigma = 0.5 + 0.5 * jnp.tanh(0.5 * gate)
     silu = gate * sigma
     grad_active = nn(cot[m].reshape(ROWS, -1), down_w)
     acts[0][rows, columns] = (silu * up).astype(BF)
@@ -488,16 +488,17 @@
     two.to_all(0)
     attn.to_all(1)
     one.spread(1)
+    attn.spread(2, 0, 1)
     exchange(0)
-    attn.spread(2)
+    attn.spread(2, 2)
     one.forward(1)
     two.spread(1)
     attn.forward(2)
     two.forward(1)
     one.spread(2)
-    exchange(1)
     share(0)
     settle(0)
+    exchange(1)
     outs = [moved(xs, x_out, out_sem.at[0])]
 
     @pl.loop(0, ROWS // STEP)
@@ -506,10 +507,9 @@
         values = xs[i // 2, lax.rem(i, 2)].astype(F32)
         normed[block] = (values * inverse_rms(values)).astype(BF)
 
-    n1t[...] = normed[...].T
-    outs.append(moved(n1t, n1t_out, out_sem.at[1]))
-    attn.finish()
-    outs.extend(moved(full_attn[p], attn_out[p], out_sem.at[2 + p]) for p in range(3))
+    for p in range(2):
+        attn.arrive(p, 2)
+    two.spread(2)
     wq, wkv, wo = full_attn
 
     def weight(ref, y):
@@ -545,15 +545,16 @@
             scores = nt(queries[:, h * HEAD : (h + 1) * HEAD], keys[:, g * HEAD : (g + 1) * HEAD]) * scale
             scores = jnp.where(keep, scores, -1e30)
             terms = jnp.exp(scores - jnp.max(scores, -1, keepdims=True))
-            low_probs = (terms / jnp.sum(terms, -1, keepdims=True)).astype(BF)
+            low_probs = (terms * (1.0 / jnp.sum(terms, -1, keepdims=True))).astype(BF)
             probs[i, h] = low_probs
             results.append(nn(low_probs, keys[:, (2 + g) * HEAD : (3 + g) * HEAD]))
         mixed[y, block] = jnp.concatenate(results, -1).astype(BF)
 
     outs.append(moved(probs, probs_out, out_sem.at[7]))
     outs.append(moved(mixed, mixed_out, out_sem.at[8]))
-    two.spread(2)
-
+    two.forward(2)
+
+    attn.arrive(2, 2)
     copies = []
     for i in range(ROWS // STEP):
         block = rows_at(lax.rem(2 * (1 - core) + i, 4) * STEP, STEP)
@@ -575,6 +576,8 @@
         if i < 2:
             second_rows[0, i] = sent(n2.at[target], n2.at[target], far_send.at[0, i], far_recv.at[0, i], partner())
     outs.append(moved(hidden.at[rows_at(core * SEQ, SEQ)], hidden_out, out_sem.at[9]))
+    attn.finish()
+    outs.extend(moved(full_attn[p], attn_out[p], out_sem.at[2 + p]) for p in range(3))
     share(1)
     settle(1)
 
@@ -585,12 +588,10 @@
                 gs[m, c, h] = (gs[m, c, h].astype(F32) * mask).astype(BF)
     outs.append(moved(gs, cot_out, out_sem.at[10]))
 
+    for p in range(3):
+        one.arrive(p, 2)
     one.finish()
     outs.extend(moved(weights[p], full_one[p], out_sem.at[11 + p]) for p in range(3))
-    for i in range(2):
-        second_rows[0, i].wait_recv()
-        block = rows_at(theirs + (2 * core + i) * STEP, STEP)
-        second_rows[1, i] = sent(n2.at[block], n2.at[block], far_send.at[1, i], far_recv.at[1, i], sibling())
     for sub in range(2):
         hidden_units(yl, sub, n2, gs, weights, acts)
     for m in range(2):
@@ -598,7 +599,15 @@
             for h in range(2):
                 cott[:, pl.ds(m * ROWS + (2 * c + h) * STEP, STEP)] = gs[m, c, h].T
     outs.append(moved(cott, cott_out, out_sem.at[14]))
-    two.forward(2)
+    for i in range(ROWS // STEP):
+        block = rows_at(mine + i * STEP, STEP)
+        n2t[:, block] = n2[block].T
+    n1t[...] = normed[...].T
+    outs.append(moved(n1t, n1t_out, out_sem.at[1]))
+    for i in range(2):
+        second_rows[0, i].wait_recv()
+        block = rows_at(theirs + (2 * core + i) * STEP, STEP)
+        second_rows[1, i] = sent(n2.at[block], n2.at[block], far_send.at[1, i], far_recv.at[1, i], sibling())
     for i in range(2):
         second_rows[0, i].wait_send()
         second_rows[1, i].wait()
@@ -606,10 +615,13 @@
         hidden_units(1 - yl, sub, n2, gs, weights, acts)
     outs.extend(moved(acts[p], acts_out[p], out_sem.at[15 + p]) for p in range(3))
     outs.append(moved(n2, n2_out, out_sem.at[18]))
-    for i in range(2 * ROWS // STEP):
-        n2t[:, pl.ds(i * STEP, STEP)] = n2[pl.ds(i * STEP, STEP)].T
+    for i in range(ROWS // STEP):
+        block = rows_at(theirs + i * STEP, STEP)
+        n2t[:, block] = n2[block].T
     outs.append(moved(n2t, n2t_out, out_sem.at[19]))
     outs.extend(unit_gradients(n2t, cott, acts, staging, grads_out, put_sem))
+    for p in range(3):
+        two.arrive(p, 2)
     two.finish()
     for copy in outs:
         copy.wait()
@@ -690,11 +702,13 @@
     n2_in, cot_in, hidden_in, n2t_in, cott_in = refs[:5]
     one_in, two_in, acts_in, data = refs[5:8], refs[8:11], refs[11:14], refs[14:17]
     sums_out, grads_out = refs[17:20], refs[20:23]
-    result_out, branch_out, grad_hidden_out = refs[23:26]
-    n2, cot, hidden, n2t, cott, staging, to_pair, from_pair, to_far, from_far, keep, result, branch, gh = refs[26:40]
-    one, two, acts_one, acts_two = refs[40:43], refs[43:46], refs[46:49], refs[49:52]
-    buffers, reduce_sems = refs[52:73], refs[73:80]
-    load, put, put_sem, pair_send, pair_recv, far_send, far_recv = refs[80:]
+    kept_out, away_out, branch_out, grad_hidden_out = refs[23:27]
+    (
+        n2, cot, hidden, n2t, cott, staging, to_pair, from_pair, whole, from_far, keep, halves, to_far, branch, gh,
+    ) = refs[27:42]
+    one, two, acts_one, acts_two = refs[42:45], refs[45:48], refs[48:51], refs[51:54]
+    buffers, reduce_sems = refs[54:75], refs[75:82]
+    load, put, put_sem, pair_send, pair_recv, far_send, far_recv = refs[82:]
     core, yl = lax.axis_index("core"), lax.axis_index("yl")
     at = coordinates()
     order = (
@@ -743,27 +757,39 @@
 
     def to_partner(k, value):
         pair[k].wait_recv()
-        to_far[k] = (value + from_pair[k].astype(F32)).astype(BF)
-        far[k] = sent(to_far.at[k], from_far.at[k], far_send.at[k], far_recv.at[k], partner())
+        whole[...] = (value + from_pair[k].astype(F32)).astype(BF)
+        far[k] = sent(whole, from_far, far_send, far_recv, partner())
 
     to_sibling(0, grad_rows(1 - yl, 1 - core))
     to_partner(0, grad_rows(1 - yl, core))
-    to_sibling(1, out_rows(1 - yl, 1 - core))
     total.relay()
-    to_partner(1, out_rows(1 - yl, core))
     for sub in range(2):
         hidden_units(yl, sub, n2, cot, two, acts_two)
-    to_sibling(2, grad_rows(yl, 1 - core))
+    to_sibling(1, grad_rows(yl, 1 - core))
     keep[...] = grad_rows(yl, core)
+    to_sibling(2, out_rows(1 - yl, 1 - core))
+    to_sibling(3, out_rows(yl, 1 - core))
     for k in range(11, 14):
         loads[k].wait()
-    pair[2].wait_recv()
+    outs = unit_gradients(n2t, cott, acts_two, staging, grads_out, put_sem)
+    total.spread()
+
+    for k, m in ((2, 1 - yl), (3, yl)):
+        pair[k].wait_recv()
+        value = out_rows(m, core) + from_pair[k].astype(F32)
+        if k == 3:
+            value = value + hidden[...]
+        halves[k - 2] = value.reshape(2, STEP, -1)
+        to_far[k - 2] = halves[k - 2, 1 - yl].astype(BF)
+        outs.append(moved(halves.at[k - 2, yl], kept_out.at[k - 2], put.at[k]))
+        outs.append(moved(to_far.at[k - 2], away_out.at[k - 2], put.at[k + 2]))
+    pair[1].wait_recv()
     far[0].wait_recv()
 
     @pl.loop(0, SEQ // STEP)
     def _(i):
         rows = rows_at(i * STEP, STEP)
-        grad = keep[rows] + (from_pair[2, rows].astype(F32) + from_far[0, rows].astype(F32))
+        grad = keep[rows] + (from_pair[1, rows].astype(F32) + from_far[rows].astype(F32))
         values = hidden[rows]
         inverse = inverse_rms(values)
         unit = values * inverse
@@ -773,21 +799,7 @@
 
     own = rows_at(core * SEQ, SEQ)
     shared = sent(branch, branch_out.at[own], pair_send.at[4], pair_recv.at[4], sibling())
-    outs = [moved(branch, branch_out.at[own], put.at[0]), moved(gh, grad_hidden_out, put.at[1])]
-    to_sibling(3, out_rows(yl, 1 - core))
-    keep[...] = out_rows(yl, core)
-    total.spread()
-    pair[3].wait_recv()
-    far[1].wait_recv()
-
-    @pl.loop(0, SEQ // STEP)
-    def _(i):
-        rows = rows_at(i * STEP, STEP)
-        change = keep[rows] + (from_pair[3, rows].astype(F32) + from_far[1, rows].astype(F32))
-        result[rows] = (hidden[rows] + change).astype(BF)
-
-    outs.append(moved(result, result_out, put.at[2]))
-    outs.extend(unit_gradients(n2t, cott, acts_two, staging, grads_out, put_sem))
+    outs.extend((moved(branch, branch_out.at[own], put.at[0]), moved(gh, grad_hidden_out, put.at[1])))
     total.narrow()
     total.finish(sums_out)
     shared.wait()
@@ -807,8 +819,13 @@
         [ANY] * 17,
         [shaped((2, 24, half), F32)] * 3
         + [shaped((width, half))] * 3
-        + [shaped(block), shaped((ROWS, width)), shaped(block, F32)],
-        [ANY] * 9,
+        + [
+            shaped((2, STEP, width), F32),
+            shaped((2, STEP, width)),
+            shaped((ROWS, width)),
+            shaped(block, F32),
+        ],
+        [ANY] * 10,
         [
             pltpu.VMEM((rows, width), BF),
             pltpu.VMEM(cot.shape, BF),
@@ -818,10 +835,11 @@
             pltpu.VMEM((4, width, CHUNK), BF),
             pltpu.VMEM((4,) + block, BF),
             pltpu.VMEM((4,) + block, BF),
-            pltpu.VMEM((2,) + block, BF),
-            pltpu.VMEM((2,) + block, BF),
+            pltpu.VMEM(block, BF),
+            pltpu.VMEM(block, BF),
             pltpu.VMEM(block, F32),
-            pltpu.VMEM(block, BF),
+            pltpu.VMEM((2, 2, STEP, width), F32),
+            pltpu.VMEM((2, STEP, width), BF),
             pltpu.VMEM(block, BF),
             pltpu.VMEM(block, F32),
             *[pltpu.VMEM(one[0].shape, BF) for _ in range(6)],
@@ -829,12 +847,12 @@
             *Reduce.buffers(half, PLANE_Z),
             *Reduce.semaphores,
             pltpu.SemaphoreType.DMA((14,)),
-            pltpu.SemaphoreType.DMA((3,)),
+            pltpu.SemaphoreType.DMA((6,)),
             pltpu.SemaphoreType.DMA((4,)),
             pltpu.SemaphoreType.DMA((5,)),
             pltpu.SemaphoreType.DMA((5,)),
-            pltpu.SemaphoreType.DMA((2,)),
-            pltpu.SemaphoreType.DMA((2,)),
+            pltpu.SemaphoreType.DMA,
+            pltpu.SemaphoreType.DMA,
         ],
         "mlp_reduce",
         2,
@@ -843,16 +861,16 @@
 
 def backward_kernel(*refs):
     xall, grad_hidden_in, branch_in, n1t_in, q_in, kv_in, probs_in, mixed_in, wq_in, wkv_in, wo_in, tables = refs[:12]
-    data, result = refs[12:15], refs[15]
-    mlp_outs, attn_outs, attn_grads = refs[16:19], refs[19:22], refs[22:25]
-    result_out, in_grad_out, from_partner = refs[25:28]
+    data, kept_in, away = refs[12:15], refs[15], refs[16]
+    mlp_outs, attn_outs, result_out, in_grad_out, from_partner = refs[17:20], refs[20:23], *refs[23:26]
     (
         xs, gh, branch, branch_t, normed_t, q, kv, probs, mixed, wq, wkv, wo,
-        grad_mixed, dq, dkv, part, keep_part, arrived, in_grad, for_partner, stage,
-    ) = refs[28:49]
-    mlp_buffers, attn_buffers = refs[49:70], refs[70:91]
-    mlp_sems, attn_sems = refs[91:98], refs[98:105]
-    load, put, send, recv = refs[105:]
+        grad_mixed, dq, dkv, part, keep_part, arrived, in_grad, for_partner, kept, others_half, result,
+    ) = refs[26:49]
+    attn_grads = refs[49:52]
+    mlp_buffers, attn_buffers = refs[52:73], refs[73:94]
+    mlp_sems, attn_sems = refs[94:101], refs[101:108]
+    load, put, send, recv = refs[108:]
     at = coordinates()
     core, yl = lax.axis_index("core"), lax.axis_index("yl")
     loads = [
@@ -865,40 +883,25 @@
                 (q_in, q),
                 (kv_in, kv),
                 (probs_in, probs),
+                (n1t_in, normed_t),
                 (wq_in, wq),
                 (wkv_in, wkv),
-                (n1t_in, normed_t),
                 (grad_hidden_in, gh),
                 (xall.at[core], xs),
+                (kept_in, kept),
             )
         )
     ]
     greet(at)
     mlp_sum = Reduce(at, data, mlp_buffers, mlp_sems, PLANE_X)
-    attn_sum = Reduce(at, attn_grads, attn_buffers, attn_sems, SPARE_X)
+    attn_sum = Reduce(at, attn_grads, attn_buffers, attn_sems, SPARE_Y)
     mlp_sum.start()
-    halves = [
-        moved(result.at[yl], result_out.at[yl], put.at[0]),
-        sent(result.at[1 - yl], result_out.at[yl], send.at[0], recv.at[0], partner()),
-    ]
-    for k in range(3):
+    finals = [sent(away.at[k], others_half.at[k], send.at[2 + k], recv.at[2 + k], partner()) for k in range(2)]
+    for k in range(2):
         loads[k].wait()
-    branch_t[...] = branch[...].T
-    third = wq.shape[2]
-    outs = {}
-
-    def put_out(k, y, value):
-        slot = (2 * k + y) % 2
-        if (k, y) != (0, 0) and (k, y) != (0, 1):
-            outs.pop(slot).wait()
-        stage[slot] = value.astype(BF).reshape(stage.shape[1:])
-        target = (attn_grads[2], attn_grads[0], attn_grads[1])[k]
-        outs[slot] = moved(stage.at[slot], target.at[pl.ds(2 * y, 2)], put.at[1 + slot])
-
     for y in range(2):
         grad_mixed[y] = nn(branch[...], wo[y]).astype(BF)
-        put_out(0, y, nn(branch_t[...], mixed[y]))
-    for k in range(3, 6):
+    for k in range(2, 6):
         loads[k].wait()
     scale = 1.0 / math.sqrt(HEAD)
 
@@ -928,24 +931,31 @@
             values = jnp.concatenate(pieces, -1)
             target[y, rows] = (values * tables[2 * k] - swap(values, first) * tables[2 * k + 1]).astype(BF)
 
+    loads[6].wait()
+
+    def weight_grad(p, left, right):
+        for y in range(2):
+            target = attn_grads[p].at[pl.ds(2 * y, 2)]
+            target[...] = nn(left[...], right[y]).astype(BF).reshape(target.shape)
+        attn_sum.start(p)
+
+    weight_grad(0, normed_t, dq)
+    weight_grad(1, normed_t, dkv)
     mlp_sum.relay()
-    for k in range(6, 11):
+    branch_t[...] = branch[...].T
+    weight_grad(2, branch_t, mixed)
+    for k in range(7, 12):
         loads[k].wait()
-    for k, source in ((1, dq), (2, dkv)):
-        for y in range(2):
-            put_out(k, y, nn(normed_t[...], source[y]))
 
     def back(start):
         rows = rows_at(start, SEQ)
         return (nt(dq[0, rows], wq[0]) + nt(dq[1, rows], wq[1])) + (nt(dkv[0, rows], wkv[0]) + nt(dkv[1, rows], wkv[1]))
 
     part[...] = back((1 - core) * SEQ).astype(BF)
-    pair = sent(part, arrived, send.at[1], recv.at[1], sibling())
-    for copy in outs.values():
-        copy.wait()
-    attn_sum.start()
+    pair = sent(part, arrived, send.at[0], recv.at[0], sibling())
+    attn_sum.relay()
+    keep_part[...] = back(core * SEQ)
     mlp_sum.spread()
-    keep_part[...] = back(core * SEQ)
     pair.wait()
 
     @pl.loop(0, SEQ // STEP)
@@ -959,33 +969,38 @@
         in_grad[i] = gh[rows] + change
 
     for_partner[...] = in_grad[1 - yl].astype(BF)
-    halves.append(moved(in_grad.at[yl], in_grad_out, put.at[3]))
-    halves.append(sent(for_partner, from_partner, send.at[2], recv.at[2], partner()))
-    attn_sum.relay()
+    ends = [
+        moved(in_grad.at[yl], in_grad_out, put.at[0]),
+        sent(for_partner, from_partner, send.at[1], recv.at[1], partner()),
+    ]
     mlp_sum.narrow()
     attn_sum.spread()
+    for copy in finals:
+        copy.wait()
+    result[1 - yl] = (kept[0] + others_half[1].astype(F32)).astype(BF)
+    result[yl] = (kept[1] + others_half[0].astype(F32)).astype(BF)
+    ends.append(moved(result, result_out, put.at[1]))
     mlp_sum.finish(mlp_outs)
     attn_sum.narrow()
     attn_sum.finish(attn_outs)
-    for copy in halves:
+    for copy in ends:
         copy.wait()
 
 
-def backward(x, grad_hidden, branch, n1t, q, kv, probs, mixed, wq, wkv, wo, tables, data, result):
+def backward(x, grad_hidden, branch, n1t, q, kv, probs, mixed, wq, wkv, wo, tables, data, kept, away):
     rows, width = branch.shape
     third, wide = wq.shape[2], data[0].shape[-1]
     heads = (2, rows, third)
     weights = (2, width, third)
-    half = (2, 128, width)
+    half = (2, STEP, width)
     return call(
         backward_kernel,
-        (x, grad_hidden, branch, n1t, q, kv, probs, mixed, wq, wkv, wo, tables, *data, result),
-        [ANY] * 11 + [VMEM] + [ANY] * 4,
+        (x, grad_hidden, branch, n1t, q, kv, probs, mixed, wq, wkv, wo, tables, *data, kept, away),
+        [ANY] * 11 + [VMEM] + [ANY] * 5,
         [shaped((2, 24, wide), F32)] * 3
         + [shaped((2, 24, third), F32)] * 3
-        + [shaped((4, 4, 4, 48, third))] * 3
         + [shaped(half), shaped(half[1:], F32), shaped(half[1:])],
-        [ANY] * 12,
+        [ANY] * 9,
         [
             pltpu.VMEM(half, BF),
             pltpu.VMEM((SEQ, width), F32),
@@ -1007,15 +1022,18 @@
             pltpu.VMEM((SEQ, width), BF),
             pltpu.VMEM(half, F32),
             pltpu.VMEM(half[1:], BF),
-            pltpu.VMEM((2, 2, 4, 4, 48, third), BF),
+            pltpu.VMEM(half, F32),
+            pltpu.VMEM(half, BF),
+            pltpu.VMEM(half, BF),
+            *[pltpu.VMEM((4, 4, 4, 48, third), BF) for _ in range(3)],
             *Reduce.buffers(wide, PLANE_X),
-            *Reduce.buffers(third, SPARE_X),
+            *Reduce.buffers(third, SPARE_Y),
             *Reduce.semaphores,
             *Reduce.semaphores,
-            pltpu.SemaphoreType.DMA((11,)),
+            pltpu.SemaphoreType.DMA((12,)),
+            pltpu.SemaphoreType.DMA((2,)),
             pltpu.SemaphoreType.DMA((4,)),
-            pltpu.SemaphoreType.DMA((3,)),
-            pltpu.SemaphoreType.DMA((3,)),
+            pltpu.SemaphoreType.DMA((4,)),
         ],
         "attn_backward_reduce",
         3,
@@ -1080,10 +1098,10 @@
     def blocked(w):
         return w.reshape(2, 4, 4, 48, -1)
 
-    *one_sums, dg, du, dd, result, branch, grad_hidden = middle(
+    *one_sums, dg, du, dd, kept, away, branch, grad_hidden = middle(
         n2, cot, hidden, n2t, cott, one, two, acts, [blocked(w) for w in grads]
     )
-    *sums, _, _, _, result, in_grad, in_grad_theirs = backward(
+    *sums, result, in_grad, in_grad_theirs = backward(
         x,
         grad_hidden,
         branch,
@@ -1097,7 +1115,8 @@
         joined(wo),
         tables,
         [blocked(w) for w in (dg, du, dd)],
-        result.reshape(2, 128, width),
+        kept,
+        away,
     )
     mine = jnp.arange(2)[:, None, None] == lax.axis_index("yl")
     in_grad = jnp.where(mine, in_grad[None], in_grad_theirs[None].astype(F32))

time: 278 us -> 267 us (0.960)
  Pallas kernels: 256 us -> 245 us
    pallas_call x3, Pallas kernels: 256 us -> 245 us  [call(): pl.pallas_call(kernel, out_shape=results, in_specs=in_specs, out_specs=ou...]
where the time goes in v6:
time: 267 us; the launch traced here: 264 us
  Pallas kernels  245 us (92%)
  local copies, waits for them, and re-layouts  6.91 us (3%)
  other arithmetic  6.59 us (2%)
  blocking collectives  3.79 us (1%)
    pallas_call x3, Pallas kernels, call(): pl.pallas_call(kernel, out_shape=results, in_specs=in_specs, out_specs=ou...  245 us

profile of v6, /device:TPU:1, one launch (start us, length us, event | category | flops | bytes accessed | tf_op | source)
XLA Modules:
  0.0 263.5 jit_solution(15393171190997767120)
XLA Ops:
  0.6 0.7 pad_maximum_fusion.1
  1.3 0.7 copy.37.refs_7_
  2.0 1.3 copy.38.refs_8_
  3.3 117.3 %gather_attn_forward_mlp.1 = (bf16[2,4,4,48,512]{4,3,2,1,0:T(8,128)(2,1)}, bf16[2,4,4,48,512]{4,3,2,1,0:T(8,128)(2,1)}, bf16[2,4,4,48,512]{4,3,2,1,0:T(8,128)(2,...) custom-call(bf16[24,768]{1,0:T(8,128)(2,1)} %refs_0_.1, ...), custom_call_target="tpu_custom_call" | custom-call | tf_op jit(solution)/shard_map/gather_attn_forward_mlp/pallas_call | solution.py:366
  120.6 50.5 %mlp_reduce.1 = (f32[2,24,512]{2,1,0:T(8,128)}, f32[2,24,512]{2,1,0:T(8,128)}, f32[2,24,512]{2,1,0:T(8,128)}, bf16[1536,512]{1,0:T(8,128)(2,1)}, bf16[1536,512]{...) custom-call(bf16[1024,1536]{1,0:T(8,128)(2,1)} %get-tuple-element.57, ...), custom_call_target="tpu_custom_call" | custom-call | tf_op jit(solution)/shard_map/mlp_reduce/pallas_call | solution.py:366
  171.2 0.0 copy-start.13
  171.2 0.0 copy-start.10
  171.2 0.0 copy-start.11
  171.2 0.0 copy-start.5
  171.2 0.0 copy-start.6
  171.2 0.0 copy-start.7
  171.2 77.2 %attn_backward_reduce.1 = (f32[2,24,512]{2,1,0:T(8,128)}, f32[2,24,512]{2,1,0:T(8,128)}, f32[2,24,512]{2,1,0:T(8,128)}, f32[2,24,384]{2,1,0:T(8,128)}, f32[2,24,...) custom-call(bf16[2,2,128,1536]{3,2,1,0:T(8,128)(2,1)} %get-tuple-ele, ...), custom_call_target="tpu_custom_call" | custom-call | tf_op jit(solution)/shard_map/attn_backward_reduce/pallas_call | solution.py:366
  248.5 0.0 copy-start.14
  248.5 0.0 copy-start.2
  248.5 0.0 copy-start.3
  248.5 1.0 slice_bitcast_fusion
  249.5 0.1 reshape.122
  249.6 0.1 reshape.123
  249.7 0.0 copy-done.13
  249.7 0.0 copy-start.8
  249.7 0.0 copy-start.9
  249.7 0.0 copy-done.10
  249.8 0.0 copy-done.11
  249.8 0.8 multiply_reduce_fusion.3
  250.6 0.9 copy.46
  251.5 0.0 copy-done.5
  251.5 0.8 multiply_reduce_fusion.2
  252.3 0.0 copy-done.6
  252.3 0.0 copy-done.7
  252.3 0.0 copy-start.4
  252.3 1.0 maximum_bitcast_fusion
  253.4 0.0 copy-done.14
  253.4 0.0 copy-done.2
  253.4 0.0 copy-start.1
  253.4 0.9 multiply_reduce_fusion
  254.3 0.0 copy-done.3
  254.3 0.9 multiply_reduce_fusion.1
  255.2 3.8 %psum.7 = f32[2,24]{1,0:T(2,128)S(1)} all-reduce(f32[2,24]{1,0:T(2,128)S(1)} %pad_maximum_fusion), channel_id=1, replica_groups=mesh['yh'=2,'x'=4,'z'=4,'core'=2,'yl'=2] {'yl'}, use_global_device_ids=true, to_apply=%region_5.6 | all-reduce | flops 48 | bytes 384 | tf_op jit(solution)/shard_map/psum | solution.py:1139
  259.0 0.5 slice_bitcast_fusion.2
  259.5 0.0 copy-done.8
  259.5 0.0 copy-done.9
  259.5 0.7 copy.50
  260.2 0.0 copy-done.4
  260.2 0.1 convert_element_type.25
  260.3 0.0 copy-done.1
  260.3 0.0 copy-start.12
  260.3 0.0 copy-start
  260.4 1.4 broadcast_select_fusion
  261.8 0.0 copy-done.12
  261.8 0.6 copy.47
  262.4 0.0 copy-done
  262.4 0.9 copy.52
  (11 shorter events, 0.1 us)
Async XLA Ops:
  171.2 78.5 %copy-start.13 = (bf16[24]{0:T(256)(128)(2,1)S(1)}, bf16[24]{0:T(256)(128)(2,1)}, u32[]{:S(2)}) copy-start(bf16[24]{0:T(256)(128)(2,1)} %param.23) | copy-start | bytes 148
  171.2 78.6 %copy-start.10 = (bf16[24,384]{1,0:T(8,128)(2,1)S(1)}, bf16[24,384]{1,0:T(8,128)(2,1)}, u32[]{:S(2)}) copy-start(bf16[24,384]{1,0:T(8,128)(2,1)} %refs_1_.1) | copy-start | bytes 55300
  171.2 78.6 %copy-start.11 = (bf16[24,384]{1,0:T(8,128)(2,1)S(1)}, bf16[24,384]{1,0:T(8,128)(2,1)}, u32[]{:S(2)}) copy-start(bf16[24,384]{1,0:T(8,128)(2,1)} %refs_2_.1) | copy-start | bytes 55300
  171.2 80.3 %copy-start.5 = (bf16[24,768]{1,0:T(8,128)(2,1)S(1)}, bf16[24,768]{1,0:T(8,128)(2,1)}, u32[]{:S(2)}) copy-start(bf16[24,768]{1,0:T(8,128)(2,1)} %refs_0_.1) | copy-start | bytes 110596
  171.2 81.1 %copy-start.6 = (f32[2,24,512]{2,1,0:T(8,128)S(1)}, f32[2,24,512]{2,1,0:T(8,128)}, u32[]{:S(2)}) copy-start(f32[2,24,512]{2,1,0:T(8,128)} %get-tuple-element.95) | copy-start | bytes 294916
  171.2 81.1 %copy-start.7 = (f32[2,24,512]{2,1,0:T(8,128)S(1)}, f32[2,24,512]{2,1,0:T(8,128)}, u32[]{:S(2)}) copy-start(f32[2,24,512]{2,1,0:T(8,128)} %get-tuple-element.97) | copy-start | bytes 294916
  248.5 4.9 %copy-start.14 = (bf16[24]{0:T(256)(128)(2,1)S(1)}, bf16[24]{0:T(256)(128)(2,1)}, u32[]{:S(2)}) copy-start(bf16[24]{0:T(256)(128)(2,1)} %param.24) | copy-start | bytes 148
  248.5 4.9 %copy-start.2 = (bf16[24,2048]{1,0:T(8,128)(2,1)S(1)}, bf16[24,2048]{1,0:T(8,128)(2,1)}, u32[]{:S(2)}) copy-start(bf16[24,2048]{1,0:T(8,128)(2,1)} %refs_5_.1) | copy-start | bytes 294916
  248.5 5.8 %copy-start.3 = (bf16[24,2048]{1,0:T(8,128)(2,1)S(1)}, bf16[24,2048]{1,0:T(8,128)(2,1)}, u32[]{:S(2)}) copy-start(bf16[24,2048]{1,0:T(8,128)(2,1)} %refs_4_.1) | copy-start | bytes 294916
  249.7 9.8 %copy-start.8 = (f32[2,24,512]{2,1,0:T(8,128)S(1)}, f32[2,24,512]{2,1,0:T(8,128)}, u32[]{:S(2)}) copy-start(f32[2,24,512]{2,1,0:T(8,128)} %get-tuple-element.99) | copy-start | bytes 294916
  249.7 9.8 %copy-start.9 = (f32[2,24,512]{2,1,0:T(8,128)S(1)}, f32[2,24,512]{2,1,0:T(8,128)}, u32[]{:S(2)}) copy-start(f32[2,24,512]{2,1,0:T(8,128)} %get-tuple-element.100) | copy-start | bytes 294916
  252.3 7.9 %copy-start.4 = (bf16[128,1536]{1,0:T(8,128)(2,1)S(1)}, bf16[128,1536]{1,0:T(8,128)(2,1)}, u32[]{:S(2)}) copy-start(bf16[128,1536]{1,0:T(8,128)(2,1)} %get-tuple-element.91) | copy-start | bytes 1179652
  253.4 6.9 %copy-start.1 = (f32[128,1536]{1,0:T(8,128)S(1)}, f32[128,1536]{1,0:T(8,128)}, u32[]{:S(2)}) copy-start(f32[128,1536]{1,0:T(8,128)} %get-tuple-element.90) | copy-start | bytes 2359300
  260.3 1.4 copy-start.12
  260.3 2.0 copy-start

commit v7 on v6

--- a/solution.py
+++ b/solution.py
@@ -350,6 +350,13 @@
     return lax.rem(lax.broadcasted_iota(jnp.int32, shape, 1), HEAD) < HEAD // 2
 
 
+def as_column(row):
+    size = row.shape[1]
+    square = jnp.broadcast_to(row[...].astype(F32), (size, size))
+    diagonal = lax.broadcasted_iota(jnp.int32, (size, size), 0) == lax.broadcasted_iota(jnp.int32, (size, size), 1)
+    return jnp.sum(jnp.where(diagonal, square, 0.0), -1, keepdims=True)
+
+
 def rows_at(start, size):
     return pl.ds(pl.multiple_of(start, size), size)
 
@@ -377,40 +384,43 @@
     )(*operands)
 
 
-def hidden_units(m, sub, n2, cot, weights, acts):
-    rows = rows_at(m * ROWS, ROWS)
+def hidden_units(m, c, count, sub, n2, cot, weights, acts):
+    rows = pl.ds(pl.multiple_of(m * ROWS + c * SEQ, SEQ), count * SEQ)
     columns = pl.ds(sub * CHUNK, CHUNK)
     gate_w, up_w, down_w = (w[..., columns].reshape(-1, CHUNK) for w in weights)
     gate = nn(n2[rows], gate_w)
     up = nn(n2[rows], up_w)
     sigma = 0.5 + 0.5 * jnp.tanh(0.5 * gate)
     silu = gate * sigma
-    grad_active = nn(cot[m].reshape(ROWS, -1), down_w)
+    grad_active = nn(cot[m, pl.ds(c, count)].reshape(count * SEQ, -1), down_w)
     acts[0][rows, columns] = (silu * up).astype(BF)
     acts[1][rows, columns] = (grad_active * up * (sigma + silu * (1.0 - sigma))).astype(BF)
     acts[2][rows, columns] = (grad_active * silu).astype(BF)
 
 
-def unit_gradients(n2t, cott, acts, staging, outs, sems):
-    waits = {}
+def unit_gradients(n2t, cott, acts, staging, outs, sems, rows=None, added=False, written=True):
+    whole, copies = slice(None) if rows is None else rows, []
     for k, (left, right, target) in enumerate(((n2t, acts[1], 0), (n2t, acts[2], 1), (cott, acts[0], 2))):
         for sub in range(2):
             columns = pl.ds(sub * CHUNK, CHUNK)
-            place_in = (2 * k + sub) % 4
-            if place_in in waits:
-                waits[place_in].wait()
-            staging[place_in] = nn(left[...], right[:, columns]).astype(BF)
-            waits[place_in] = moved(staging.at[place_in], outs[target].at[:, columns], sems.at[place_in])
-    return list(waits.values())
+            value = nn(left[:, whole], right[whole, columns])
+            if added:
+                value = value + staging[2 * k + sub].astype(F32)
+            staging[2 * k + sub] = value.astype(BF)
+            if written:
+                copies.append(moved(staging.at[2 * k + sub], outs[target].at[:, columns], sems.at[2 * k + sub]))
+    return copies
 
 
 def forward_kernel(third, wide, *refs):
-    own_weights, gains, lengths, xin, gin, tables = refs[:7], *refs[7:12]
+    own_weights, gains_one, gains_two, lengths, xin, gin, tables = refs[:7], *refs[7:13]
+    refs = refs[1:]
     full_two, full_one = refs[12:15], refs[15:18]
     (
         x_out, n1t_out, q_out, kv_out, probs_out, mixed_out, hidden_out, n2_out, n2t_out, cot_out, cott_out,
     ) = refs[18:29]
-    attn_out, grads_out, acts_out = refs[29:32], refs[32:35], refs[35:38]
+    attn_out, grads_out, acts_out, shard_out = refs[29:32], refs[32:35], refs[35:38], refs[38]
+    refs = refs[1:]
     (
         shard, got_shard, packed, xs, gs, normed, q, kv, probs, mixed, hidden, n2, n2t, cott, part, arrived, n1t,
         valid, staging,
@@ -424,7 +434,7 @@
     own_g = moved(gin, gs.at[:, core, yl], own_sem.at[1])
 
     query, key, value, output, *mlp_weights = (ref[...].astype(F32) for ref in own_weights)
-    gain_one, gain_two = gains[:, 0:1].astype(F32), gains[:, 1:2].astype(F32)
+    gain_one, gain_two = as_column(gains_one), as_column(gains_two)
     small = key.shape[1] // 2
     for c in range(2):
         thin = slice(c * small, (c + 1) * small)
@@ -442,7 +452,7 @@
             shard[c, :24, column : column + part_value.shape[1]] = part_value
             column += part_value.shape[1]
         lane = lax.broadcasted_iota(jnp.int32, (8, 2 * SEQ), 1)
-        ends = jnp.where(lane < SEQ, lengths[0, 0], lengths[1, 0] + SEQ)
+        ends = jnp.where(lane < SEQ, lengths[:, 0:1], lengths[:, 1:2] + SEQ)
         shard[c, 24:, : 2 * SEQ] = jnp.where(lane < ends, 1.0, 0.0)
     greet(at)
     swap_shard = sent(shard.at[1 - core], got_shard, pair_send.at[0], pair_recv.at[0], sibling())
@@ -499,7 +509,7 @@
     share(0)
     settle(0)
     exchange(1)
-    outs = [moved(xs, x_out, out_sem.at[0])]
+    outs = [moved(xs, x_out, out_sem.at[0]), moved(shard, shard_out, out_sem.at[24])]
 
     @pl.loop(0, ROWS // STEP)
     def _(i):
@@ -592,8 +602,11 @@
         one.arrive(p, 2)
     one.finish()
     outs.extend(moved(weights[p], full_one[p], out_sem.at[11 + p]) for p in range(3))
+    mine_rows, their_rows = rows_at(mine, ROWS), rows_at(theirs, ROWS)
     for sub in range(2):
-        hidden_units(yl, sub, n2, gs, weights, acts)
+        hidden_units(yl, 0, 2, sub, n2, gs, weights, acts)
+    outs.extend(moved(acts[p].at[mine_rows], acts_out[p].at[mine_rows], out_sem.at[15 + p]) for p in range(3))
+    outs.append(moved(n2.at[mine_rows], n2_out.at[mine_rows], out_sem.at[18]))
     for m in range(2):
         for c in range(2):
             for h in range(2):
@@ -602,24 +615,28 @@
     for i in range(ROWS // STEP):
         block = rows_at(mine + i * STEP, STEP)
         n2t[:, block] = n2[block].T
+    unit_gradients(n2t, cott, acts, staging, grads_out, put_sem, mine_rows, written=False)
     n1t[...] = normed[...].T
     outs.append(moved(n1t, n1t_out, out_sem.at[1]))
+
     for i in range(2):
         second_rows[0, i].wait_recv()
         block = rows_at(theirs + (2 * core + i) * STEP, STEP)
         second_rows[1, i] = sent(n2.at[block], n2.at[block], far_send.at[1, i], far_recv.at[1, i], sibling())
+    for sub in range(2):
+        hidden_units(1 - yl, core, 1, sub, n2, gs, weights, acts)
     for i in range(2):
         second_rows[0, i].wait_send()
         second_rows[1, i].wait()
     for sub in range(2):
-        hidden_units(1 - yl, sub, n2, gs, weights, acts)
-    outs.extend(moved(acts[p], acts_out[p], out_sem.at[15 + p]) for p in range(3))
-    outs.append(moved(n2, n2_out, out_sem.at[18]))
+        hidden_units(1 - yl, 1 - core, 1, sub, n2, gs, weights, acts)
+    outs.extend(moved(acts[p].at[their_rows], acts_out[p].at[their_rows], out_sem.at[20 + p]) for p in range(3))
+    outs.append(moved(n2.at[their_rows], n2_out.at[their_rows], out_sem.at[23]))
     for i in range(ROWS // STEP):
         block = rows_at(theirs + i * STEP, STEP)
         n2t[:, block] = n2[block].T
     outs.append(moved(n2t, n2t_out, out_sem.at[19]))
-    outs.extend(unit_gradients(n2t, cott, acts, staging, grads_out, put_sem))
+    outs.extend(unit_gradients(n2t, cott, acts, staging, grads_out, put_sem, their_rows, added=True))
     for p in range(3):
         two.arrive(p, 2)
     two.finish()
@@ -637,8 +654,8 @@
     piece = (2, 4, 4, 48, half)
     return call(
         lambda *refs: forward_kernel(third, wide, *refs),
-        (*own_weights, gains, lengths, xin, gin, tables),
-        [VMEM] * 8 + [pl.BlockSpec(memory_space=pltpu.SMEM), ANY, ANY, VMEM],
+        (*own_weights, *gains, lengths, xin, gin, tables),
+        [VMEM] * 10 + [ANY, ANY, VMEM],
         [shaped(piece)] * 6
         + [
             shaped((2, 2, 128, width)),
@@ -655,8 +672,9 @@
         ]
         + [shaped((4, 4, 4, 48, third))] * 3
         + [shaped((width, half))] * 3
-        + [shaped((2 * ROWS, half))] * 3,
-        [ANY] * 26,
+        + [shaped((2 * ROWS, half))] * 3
+        + [shaped((2, 32, 3 * third + 3 * wide), F32)],
+        [ANY] * 27,
         [
             pltpu.VMEM((2, 32, 3 * third + 3 * wide), F32),
             pltpu.VMEM((32, 3 * third + 3 * wide), F32),
@@ -676,7 +694,7 @@
             pltpu.VMEM(rows, BF),
             pltpu.VMEM(rows[::-1], BF),
             pltpu.VMEM((2, 2, 8, SEQ), F32),
-            pltpu.VMEM((4, width, CHUNK), BF),
+            pltpu.VMEM((6, width, CHUNK), BF),
             *[pltpu.VMEM((4, 4, 4, 48, third), BF) for _ in range(3)],
             *[pltpu.VMEM(piece, BF) for _ in range(3)],
             *[pltpu.VMEM((2 * ROWS, half), BF) for _ in range(3)],
@@ -690,8 +708,8 @@
             pltpu.SemaphoreType.DMA((2, 2)),
             pltpu.SemaphoreType.DMA((2, 2)),
             pltpu.SemaphoreType.DMA((2,)),
-            pltpu.SemaphoreType.DMA((20,)),
-            pltpu.SemaphoreType.DMA((4,)),
+            pltpu.SemaphoreType.DMA((25,)),
+            pltpu.SemaphoreType.DMA((6,)),
         ],
         "gather_attn_forward_mlp",
         1,
@@ -708,7 +726,7 @@
     ) = refs[27:42]
     one, two, acts_one, acts_two = refs[42:45], refs[45:48], refs[48:51], refs[51:54]
     buffers, reduce_sems = refs[54:75], refs[75:82]
-    load, put, put_sem, pair_send, pair_recv, far_send, far_recv = refs[82:]
+    load, put, put_sem, pair_send, pair_recv, part_send, part_recv, far_send, far_recv = refs[82:]
     core, yl = lax.axis_index("core"), lax.axis_index("yl")
     at = coordinates()
     order = (
@@ -732,7 +750,7 @@
     for k in range(5):
         loads[k].wait()
     for sub in range(2):
-        hidden_units(1 - yl, sub, n2, cot, two, acts_two)
+        hidden_units(1 - yl, 0, 2, sub, n2, cot, two, acts_two)
     for k in range(5, 11):
         loads[k].wait()
 
@@ -749,22 +767,26 @@
         rows = rows_at(m * ROWS + c * SEQ, SEQ)
         return nt(acts_one[0][rows], weight(one[2])) + nt(acts_two[0][rows], weight(two[2]))
 
-    pair, far = {}, {}
+    pair, far, shared = {}, {}, []
 
     def to_sibling(k, value):
         to_pair[k] = value.astype(BF)
         pair[k] = sent(to_pair.at[k], from_pair.at[k], pair_send.at[k], pair_recv.at[k], sibling())
 
-    def to_partner(k, value):
-        pair[k].wait_recv()
-        whole[...] = (value + from_pair[k].astype(F32)).astype(BF)
-        far[k] = sent(whole, from_far, far_send, far_recv, partner())
-
-    to_sibling(0, grad_rows(1 - yl, 1 - core))
-    to_partner(0, grad_rows(1 - yl, core))
+    blocks = [pl.ds(i * STEP, STEP) for i in range(2)]
+    to_pair[0] = grad_rows(1 - yl, 1 - core).astype(BF)
+    for i, rows in enumerate(blocks):
+        pair["far", i] = sent(
+            to_pair.at[0, rows], from_pair.at[0, rows], part_send.at[0, i], part_recv.at[0, i], sibling()
+        )
+    keep[...] = grad_rows(1 - yl, core)
+    for i, rows in enumerate(blocks):
+        pair["far", i].wait_recv()
+        whole[rows] = (keep[rows] + from_pair[0, rows].astype(F32)).astype(BF)
+        far[i] = sent(whole.at[rows], from_far.at[rows], far_send.at[i], far_recv.at[i], partner())
     total.relay()
     for sub in range(2):
-        hidden_units(yl, sub, n2, cot, two, acts_two)
+        hidden_units(yl, 0, 2, sub, n2, cot, two, acts_two)
     to_sibling(1, grad_rows(yl, 1 - core))
     keep[...] = grad_rows(yl, core)
     to_sibling(2, out_rows(1 - yl, 1 - core))
@@ -784,11 +806,9 @@
         outs.append(moved(halves.at[k - 2, yl], kept_out.at[k - 2], put.at[k]))
         outs.append(moved(to_far.at[k - 2], away_out.at[k - 2], put.at[k + 2]))
     pair[1].wait_recv()
-    far[0].wait_recv()
-
-    @pl.loop(0, SEQ // STEP)
-    def _(i):
-        rows = rows_at(i * STEP, STEP)
+
+    for i, rows in enumerate(blocks):
+        far[i].wait_recv()
         grad = keep[rows] + (from_pair[1, rows].astype(F32) + from_far[rows].astype(F32))
         values = hidden[rows]
         inverse = inverse_rms(values)
@@ -796,13 +816,16 @@
         back = inverse * (grad - unit * jnp.mean(grad * unit, -1, keepdims=True))
         gh[rows] = cot[yl, core, i].astype(F32) + back
         branch[rows] = gh[rows].astype(BF)
-
-    own = rows_at(core * SEQ, SEQ)
-    shared = sent(branch, branch_out.at[own], pair_send.at[4], pair_recv.at[4], sibling())
-    outs.extend((moved(branch, branch_out.at[own], put.at[0]), moved(gh, grad_hidden_out, put.at[1])))
+        target = rows_at(core * SEQ + i * STEP, STEP)
+        shared.append(
+            sent(branch.at[rows], branch_out.at[target], part_send.at[1, i], part_recv.at[1, i], sibling())
+        )
+        outs.append(moved(branch.at[rows], branch_out.at[target], put.at[6 + i]))
+    outs.append(moved(gh, grad_hidden_out, put.at[0]))
     total.narrow()
     total.finish(sums_out)
-    shared.wait()
+    for copy in shared:
+        copy.wait()
     for copy in (*pair.values(), *far.values()):
         copy.wait_send()
     for copy in outs:
@@ -832,7 +855,7 @@
             pltpu.VMEM(block, F32),
             pltpu.VMEM((width, rows), BF),
             pltpu.VMEM((width, rows), BF),
-            pltpu.VMEM((4, width, CHUNK), BF),
+            pltpu.VMEM((6, width, CHUNK), BF),
             pltpu.VMEM((4,) + block, BF),
             pltpu.VMEM((4,) + block, BF),
             pltpu.VMEM(block, BF),
@@ -847,12 +870,14 @@
             *Reduce.buffers(half, PLANE_Z),
             *Reduce.semaphores,
             pltpu.SemaphoreType.DMA((14,)),
+            pltpu.SemaphoreType.DMA((8,)),
             pltpu.SemaphoreType.DMA((6,)),
             pltpu.SemaphoreType.DMA((4,)),
-            pltpu.SemaphoreType.DMA((5,)),
-            pltpu.SemaphoreType.DMA((5,)),
-            pltpu.SemaphoreType.DMA,
-            pltpu.SemaphoreType.DMA,
+            pltpu.SemaphoreType.DMA((4,)),
+            pltpu.SemaphoreType.DMA((2, 2)),
+            pltpu.SemaphoreType.DMA((2, 2)),
+            pltpu.SemaphoreType.DMA((2,)),
+            pltpu.SemaphoreType.DMA((2,)),
         ],
         "mlp_reduce",
         2,
@@ -861,8 +886,11 @@
 
 def backward_kernel(*refs):
     xall, grad_hidden_in, branch_in, n1t_in, q_in, kv_in, probs_in, mixed_in, wq_in, wkv_in, wo_in, tables = refs[:12]
-    data, kept_in, away = refs[12:15], refs[15], refs[16]
+    data, kept_in, away, shard_in, one_in = refs[12:15], *refs[15:18], refs[18:20]
+    refs = refs[3:]
     mlp_outs, attn_outs, result_out, in_grad_out, from_partner = refs[17:20], refs[20:23], *refs[23:26]
+    gains_out = refs[26]
+    refs = refs[1:]
     (
         xs, gh, branch, branch_t, normed_t, q, kv, probs, mixed, wq, wkv, wo,
         grad_mixed, dq, dkv, part, keep_part, arrived, in_grad, for_partner, kept, others_half, result,
@@ -870,7 +898,8 @@
     attn_grads = refs[49:52]
     mlp_buffers, attn_buffers = refs[52:73], refs[73:94]
     mlp_sems, attn_sems = refs[94:101], refs[101:108]
-    load, put, send, recv = refs[108:]
+    mlp_ends, attn_ends, shard, one_sums, gain_part, gain_in = refs[108:111], refs[111:114], *refs[114:118]
+    load, put, send, recv = refs[118:]
     at = coordinates()
     core, yl = lax.axis_index("core"), lax.axis_index("yl")
     loads = [
@@ -889,6 +918,9 @@
                 (grad_hidden_in, gh),
                 (xall.at[core], xs),
                 (kept_in, kept),
+                (shard_in, shard),
+                (one_in[0], one_sums.at[0]),
+                (one_in[1], one_sums.at[1]),
             )
         )
     ]
@@ -944,7 +976,7 @@
     mlp_sum.relay()
     branch_t[...] = branch[...].T
     weight_grad(2, branch_t, mixed)
-    for k in range(7, 12):
+    for k in range(7, 15):
         loads[k].wait()
 
     def back(start):
@@ -980,14 +1012,34 @@
     result[1 - yl] = (kept[0] + others_half[1].astype(F32)).astype(BF)
     result[yl] = (kept[1] + others_half[0].astype(F32)).astype(BF)
     ends.append(moved(result, result_out, put.at[1]))
-    mlp_sum.finish(mlp_outs)
+    mlp_sum.finish(mlp_ends)
     attn_sum.narrow()
-    attn_sum.finish(attn_outs)
+    ends.extend(moved(mlp_ends[p], mlp_outs[p], put.at[2 + p]) for p in range(3))
+
+    def along(start, gradient):
+        weights = shard[:, :24, start : start + gradient.shape[2]]
+        total = jnp.sum(weights * gradient, -1, keepdims=True)
+        return total[0] + total[1]
+
+    thin, half = attn_ends[0].shape[2], mlp_ends[0].shape[2]
+    second = sum(
+        along(3 * thin + 2 * half * p, one_sums[p]) + along(3 * thin + 2 * half * p + half, mlp_ends[p][...])
+        for p in range(2)
+    )
+    attn_sum.finish(attn_ends)
+    ends.extend(moved(attn_ends[p], attn_outs[p], put.at[5 + p]) for p in range(3))
+    first = sum(along(thin * p, attn_ends[p][...]) for p in range(2))
+    lane = lax.broadcasted_iota(jnp.int32, gain_part.shape, 1)
+    gain_part[...] = jnp.where(lane == 0, first, second)
+    swapped = sent(gain_part, gain_in, send.at[4], recv.at[4], partner())
+    swapped.wait()
+    gain_part[...] = gain_part[...] + gain_in[...]
+    ends.append(moved(gain_part, gains_out, put.at[8]))
     for copy in ends:
         copy.wait()
 
 
-def backward(x, grad_hidden, branch, n1t, q, kv, probs, mixed, wq, wkv, wo, tables, data, kept, away):
+def backward(x, grad_hidden, branch, n1t, q, kv, probs, mixed, wq, wkv, wo, tables, data, kept, away, shard, one_sums):
     rows, width = branch.shape
     third, wide = wq.shape[2], data[0].shape[-1]
     heads = (2, rows, third)
@@ -995,12 +1047,12 @@
     half = (2, STEP, width)
     return call(
         backward_kernel,
-        (x, grad_hidden, branch, n1t, q, kv, probs, mixed, wq, wkv, wo, tables, *data, kept, away),
-        [ANY] * 11 + [VMEM] + [ANY] * 5,
+        (x, grad_hidden, branch, n1t, q, kv, probs, mixed, wq, wkv, wo, tables, *data, kept, away, shard, *one_sums),
+        [ANY] * 11 + [VMEM] + [ANY] * 8,
         [shaped((2, 24, wide), F32)] * 3
         + [shaped((2, 24, third), F32)] * 3
-        + [shaped(half), shaped(half[1:], F32), shaped(half[1:])],
-        [ANY] * 9,
+        + [shaped(half), shaped(half[1:], F32), shaped(half[1:]), shaped((24, 128), F32)],
+        [ANY] * 10,
         [
             pltpu.VMEM(half, BF),
             pltpu.VMEM((SEQ, width), F32),
@@ -1030,14 +1082,75 @@
             *Reduce.buffers(third, SPARE_Y),
             *Reduce.semaphores,
             *Reduce.semaphores,
-            pltpu.SemaphoreType.DMA((12,)),
-            pltpu.SemaphoreType.DMA((2,)),
-            pltpu.SemaphoreType.DMA((4,)),
-            pltpu.SemaphoreType.DMA((4,)),
+            *[pltpu.VMEM((2, 24, wide), F32) for _ in range(3)],
+            *[pltpu.VMEM((2, 24, third), F32) for _ in range(3)],
+            pltpu.VMEM(shard.shape, F32),
+            pltpu.VMEM((2, 2, 24, wide), F32),
+            pltpu.VMEM((24, 128), F32),
+            pltpu.VMEM((24, 128), F32),
+            pltpu.SemaphoreType.DMA((15,)),
+            pltpu.SemaphoreType.DMA((9,)),
+            pltpu.SemaphoreType.DMA((5,)),
+            pltpu.SemaphoreType.DMA((5,)),
         ],
         "attn_backward_reduce",
         3,
     )
+
+
+def last_kernel(own, theirs, result_in, one, two, attn, gains_one, gains_two, gain_sums, outs):
+    result, in_grad, dq, dk, dv, do, dg, du, dd, gain_one_grad, gain_two_grad = outs
+    yl = lax.axis_index("yl")
+    result[...] = result_in[...]
+    in_grad[yl] = own[...]
+    in_grad[1 - yl] = theirs[...].astype(F32)
+    gain_one, gain_two = as_column(gains_one), as_column(gains_two)
+    thin, half = attn[0].shape[2], two[0].shape[2]
+    keys = [[], []]
+    for c in range(2):
+        dq[:, c * thin : (c + 1) * thin] = attn[0][c] * gain_one
+        for k in range(2):
+            keys[k].append(attn[1][c, :, k * (thin // 2) : (k + 1) * (thin // 2)] * gain_one)
+        do[:, c * thin : (c + 1) * thin] = attn[2][c]
+        for k, part in enumerate((one, two)):
+            start = (2 * c + k) * half
+            dg[:, start : start + half] = part[0][c] * gain_two
+            du[:, start : start + half] = part[1][c] * gain_two
+            dd[:, start : start + half] = part[2][c]
+    dk[...] = jnp.concatenate(keys[0], -1)
+    dv[...] = jnp.concatenate(keys[1], -1)
+    lane = lax.broadcasted_iota(jnp.int32, gain_sums.shape, 1)
+    grads = (gain_sums[...] / jnp.where(lane == 0, gain_one, gain_two)).T
+    gain_one_grad[...] = grads[0:1, :24]
+    gain_two_grad[...] = grads[1:2, :24]
+
+
+def placed_outputs(own, theirs, result, one, two, attn, gains, gain_sums):
+    width, thin, half = own.shape[1], attn[0].shape[2], two[0].shape[2]
+
+    def kernel(*refs):
+        last_kernel(*refs[:3], refs[3:6], refs[6:9], refs[9:12], *refs[12:15], refs[15:])
+
+    return pl.pallas_call(
+        kernel,
+        out_shape=[
+            shaped((2, STEP, width)),
+            shaped((2, STEP, width), F32),
+            shaped((24, 2 * thin), F32),
+            shaped((24, thin), F32),
+            shaped((24, thin), F32),
+            shaped((24, 2 * thin), F32),
+            shaped((24, 4 * half), F32),
+            shaped((24, 4 * half), F32),
+            shaped((24, 4 * half), F32),
+            shaped((1, 24), F32),
+            shaped((1, 24), F32),
+        ],
+        in_specs=[VMEM] * 15,
+        out_specs=[VMEM] * 11,
+        compiler_params=pltpu.CompilerParams(vmem_limit_bytes=VMEM_LIMIT),
+        name="place_outputs",
+    )(own, theirs, result, *one, *two, *attn, *gains, gain_sums)
 
 
 def tables_for(count, heads, plain):
@@ -1067,9 +1180,6 @@
     mlp_gain,
 ):
     width = inputs.shape[2]
-    gain_one = attn_gain.astype(F32)[:, None]
-    gain_two = mlp_gain.astype(F32)[:, None]
-
     own_weights = (
         query_weight,
         key_matrix,
@@ -1079,18 +1189,16 @@
         up_weight,
         down_weight.T,
     )
-    query32, key32, value32, gate32, up32 = (
-        w.astype(F32) for w in (query_weight, key_matrix, value_matrix, gate_weight, up_weight)
-    )
+    gains = (attn_gain.reshape(1, -1), mlp_gain.reshape(1, -1))
     third, wide = query_weight.shape[1] // 2, gate_weight.shape[1] // 2
     tables = jnp.asarray(np.concatenate([tables_for(SEQ, 4, 0), tables_for(SEQ, 2, 2 * HEAD)]))
 
     results = forward(
-        own_weights, jnp.stack([attn_gain, mlp_gain], 1), lengths, inputs, out_grad, tables, third, wide
+        own_weights, gains, lengths.reshape(1, -1), inputs, out_grad, tables, third, wide
     )
     two, one = results[:3], results[3:6]
     x, n1t, q, kv, probs, mixed, hidden, n2, n2t, cot, cott = results[6:17]
-    (wq, wkv, wo), grads, acts = results[17:20], results[20:23], results[23:26]
+    (wq, wkv, wo), grads, acts, shard = results[17:20], results[20:23], results[23:26], results[26]
 
     def joined(w):
         return w.reshape(2, width, -1)
@@ -1101,7 +1209,7 @@
     *one_sums, dg, du, dd, kept, away, branch, grad_hidden = middle(
         n2, cot, hidden, n2t, cott, one, two, acts, [blocked(w) for w in grads]
     )
-    *sums, result, in_grad, in_grad_theirs = backward(
+    *sums, result, in_grad, in_grad_theirs, gain_sums = backward(
         x,
         grad_hidden,
         branch,
@@ -1117,39 +1225,13 @@
         [blocked(w) for w in (dg, du, dd)],
         kept,
         away,
-    )
-    mine = jnp.arange(2)[:, None, None] == lax.axis_index("yl")
-    in_grad = jnp.where(mine, in_grad[None], in_grad_theirs[None].astype(F32))
-    mlp_sums = [jnp.concatenate(parts, -1) for parts in zip(one_sums, sums[:3])]
-    attn_sums = sums[3:]
-
-    def whole(part):
-        return jnp.moveaxis(part, 0, 1).reshape(24, -1)
-
-    key_size = key_matrix.shape[1] // 2
-    dquery, doutput = whole(attn_sums[0]), whole(attn_sums[2])
-    dkey, dvalue = whole(attn_sums[1][..., :key_size]), whole(attn_sums[1][..., key_size:])
-    dgate, dup, ddown = (whole(part) for part in mlp_sums)
-    gain_grads = jnp.stack(
-        [
-            sum(jnp.sum(w * g, -1) for w, g in ((query32, dquery), (key32, dkey), (value32, dvalue))),
-            sum(jnp.sum(w * g, -1) for w, g in ((gate32, dgate), (up32, dup))),
-        ]
-    )
-    gain_grads = lax.psum(gain_grads, "yl")
-    return (
-        result,
-        in_grad,
-        dquery * gain_one,
-        dkey * gain_one,
-        dvalue * gain_one,
-        doutput.T,
-        dgate * gain_two,
-        dup * gain_two,
-        ddown.T,
-        gain_grads[0],
-        gain_grads[1],
-    )
+        shard,
+        one_sums[:2],
+    )
+    result, in_grad, dq, dk, dv, do, dg, du, dd, gain_one_grad, gain_two_grad = placed_outputs(
+        in_grad, in_grad_theirs, result, one_sums, sums[:3], sums[3:], gains, gain_sums
+    )
+    return result, in_grad, dq, dk, dv, do.T, dg, du, dd.T, gain_one_grad.reshape(24), gain_two_grad.reshape(24)
 
 
 def solution(mesh):

time: 267 us -> 250 us (0.936)
  local copies, waits for them, and re-layouts: 6.91 us -> 0 us
  other arithmetic: 6.59 us -> 0 us
  blocking collectives: 3.79 us -> 0 us
    psum x1 -> x0, blocking collectives: 3.79 us -> none  [body(): gain_grads = lax.psum(gain_grads, 'yl')]
    pallas_call x0 -> x1, Pallas kernels: none -> 3.57 us  [placed_outputs(): pl.pallas_call(kernel, out_shape=[shaped((2, STEP, width)), shaped((2, ST...]
    reduce_sum x4 -> x0, other arithmetic: 3.37 us -> none  [body(): jnp.sum(w * g, -1)]
    pallas_call x3, Pallas kernels: 245 us -> 242 us  [call(): pl.pallas_call(kernel, out_shape=results, in_specs=in_specs, out_specs=ou...]
where the time goes in v7:
time: 250 us; the launch traced here: 246 us
  Pallas kernels  245 us (98%)
    pallas_call x3, Pallas kernels, call(): pl.pallas_call(kernel, out_shape=results, in_specs=in_specs, out_specs=ou...  242 us

profile of v7, /device:TPU:1, one launch (start us, length us, event | category | flops | bytes accessed | tf_op | source)
XLA Modules:
  0.0 246.2 jit_solution(14905952496363117900)
XLA Ops:
  0.6 113.4 %gather_attn_forward_mlp.1 = (bf16[2,4,4,48,512]{4,3,2,1,0:T(8,128)(2,1)}, bf16[2,4,4,48,512]{4,3,2,1,0:T(8,128)(2,1)}, bf16[2,4,4,48,512]{4,3,2,1,0:T(8,128)(2,...) custom-call(bf16[24,768]{1,0:T(8,128)(2,1)} %refs_0_.1, ...), custom_call_target="tpu_custom_call" | custom-call | tf_op jit(solution)/shard_map/gather_attn_forward_mlp/pallas_call | solution.py:373
  114.1 48.9 %mlp_reduce.1 = (f32[2,24,512]{2,1,0:T(8,128)}, f32[2,24,512]{2,1,0:T(8,128)}, f32[2,24,512]{2,1,0:T(8,128)}, bf16[1536,512]{1,0:T(8,128)(2,1)}, bf16[1536,512]{...) custom-call(bf16[1024,1536]{1,0:T(8,128)(2,1)} %get-tuple-element.70, ...), custom_call_target="tpu_custom_call" | custom-call | tf_op jit(solution)/shard_map/mlp_reduce/pallas_call | solution.py:373
  163.0 79.5 %attn_backward_reduce.1 = (f32[2,24,512]{2,1,0:T(8,128)}, f32[2,24,512]{2,1,0:T(8,128)}, f32[2,24,512]{2,1,0:T(8,128)}, f32[2,24,384]{2,1,0:T(8,128)}, f32[2,24,...) custom-call(bf16[2,2,128,1536]{3,2,1,0:T(8,128)(2,1)} %get-tuple-ele, ...), custom_call_target="tpu_custom_call" | custom-call | tf_op jit(solution)/shard_map/attn_backward_reduce/pallas_call | solution.py:373
  242.4 3.6 %place_outputs.1 = (bf16[2,128,1536]{2,1,0:T(8,128)(2,1)}, f32[2,128,1536]{2,1,0:T(8,128)}, f32[24,768]{1,0:T(8,128)}, f32[24,384]{1,0:T(8,128)}, f32[24,384]{1,...) custom-call(f32[128,1536]{1,0:T(8,128)} %get-tuple-element.105.refs_, ...), custom_call_target="tpu_custom_call" | custom-call | tf_op jit(solution)/shard_map/place_outputs/pallas_call | solution.py:1134

commit v8 on v7

--- a/solution.py
+++ b/solution.py
@@ -21,6 +21,7 @@
 SPARE_Y = (("x", "z", "y"), ("y", "x", "z"), ("y", "z", "x"))
 PLANE_Z = (("w", "x", "z"), ("w", "z", "x"), ("w", "x", "z"))
 PLANE_X = (("w", "z", "x"), ("w", "x", "z"), ("w", "z", "x"))
+PLANE = (("w", "x", "z"), ("w", "z", "x"), ("w", "x", "z"), ("w", "z", "x"))
 SEQ = 256
 ROWS = 512
 STEP = 128
@@ -107,13 +108,11 @@
 
 
 class Gather:
-    semaphores = (
-        pltpu.SemaphoreType.DMA((3,)),
-        pltpu.SemaphoreType.DMA((3, 2, 3)),
-        pltpu.SemaphoreType.DMA((3, 2, 3)),
-        pltpu.SemaphoreType.DMA((3, 2, 2, 3)),
-        pltpu.SemaphoreType.DMA((3, 2, 2, 3)),
-    )
+    @staticmethod
+    def semaphores(orders):
+        count = len(orders)
+        shapes = (count,), (count, 2, 3), (count, 2, 3), (count, 2, 2, 3), (count, 2, 2, 3)
+        return [pltpu.SemaphoreType.DMA(shape) for shape in shapes]
 
     def __init__(self, at, srcs, outs, semaphores, orders):
         self.at, self.srcs, self.outs, self.orders = at, srcs, outs, orders
@@ -158,7 +157,7 @@
         )
 
     def spread(self, stage, *pieces):
-        for p in pieces or range(3):
+        for p in pieces or range(len(self.orders)):
             order = self.orders[p]
             if stage == 1:
                 self.own[p].wait()
@@ -184,20 +183,16 @@
 
 
 class Reduce:
-    semaphores = (
-        pltpu.SemaphoreType.DMA((3, 3)),
-        pltpu.SemaphoreType.DMA((3, 2, 3)),
-        pltpu.SemaphoreType.DMA((3, 2, 3)),
-        pltpu.SemaphoreType.DMA((3, 2, 3)),
-        pltpu.SemaphoreType.DMA((3, 2, 3)),
-        pltpu.SemaphoreType.DMA((3, 2)),
-        pltpu.SemaphoreType.DMA((3, 2)),
-    )
+    @staticmethod
+    def semaphores(orders):
+        count = len(orders)
+        shapes = (count, 3), *[(count, 2, 3)] * 4, (count, 2), (count, 2)
+        return [pltpu.SemaphoreType.DMA(shape) for shape in shapes]
 
     @staticmethod
     def buffers(columns, orders):
         def per_piece(*shape):
-            return [pltpu.VMEM(shape + (48, columns), BF) for _ in range(3)]
+            return [pltpu.VMEM(shape + (48, width), BF) for width in columns]
 
         size = extent(dimensions(orders[0])[0])
         return [
@@ -207,13 +202,13 @@
             *per_piece(2, size, 4),
             *per_piece(3, size),
             *per_piece(3),
-            *[pltpu.VMEM((48, columns), F32) for _ in range(3)],
+            *[pltpu.VMEM((48, width), F32) for width in columns],
         ]
 
     def __init__(self, at, data, buffers, semaphores, orders):
         self.at, self.data, self.orders = at, data, orders
         self.side, self.kept, self.far, self.near, self.second, self.third, self.sums = (
-            buffers[3 * k : 3 * k + 3] for k in range(7)
+            buffers[len(orders) * k : len(orders) * (k + 1)] for k in range(7)
         )
         self.load, self.first_send, self.first_recv, self.send, self.recv, self.end_send, self.end_recv = semaphores
         self.loads, self.copies = {}, {}
@@ -228,7 +223,7 @@
 
     def start(self, *pieces):
         at, s, r = self.at, self.first_send, self.first_recv
-        for p in pieces or range(3):
+        for p in pieces or range(len(self.orders)):
             order = self.orders[p]
             axis, cut = order[2], self.left(p)[0]
             size = extent(cut) // 2
@@ -274,18 +269,23 @@
                 self.copies[p, d, 1].wait_recv()
                 self.copies[p, d, 2].wait_recv()
             kept, near = self.kept[p], self.near[p]
-
-            @pl.loop(0, 4 * extent(self.left(p)[0]))
-            def _(i, kept=kept, near=near):
-                a, b = i // 4, lax.rem(i, 4)
-                total = kept[a, b].astype(F32) + near[0, a, b].astype(F32) + near[1, a, b].astype(F32)
-                kept[a, b] = total.astype(BF)
-
-            for d, by in enumerate(others(order[1])):
-                block = kept.at[self.inside(p, slot(at, order[1], by))]
-                self.copies[p, "b", d] = sent(
-                    block, self.second[p].at[d], self.send.at[p, 0, d], self.recv.at[p, 0, d], peer(at, order[1], by)
-                )
+            for d, by in enumerate((*others(order[1]), 0)):
+                group = slot(at, order[1], by)
+
+                @pl.loop(0, extent(order[0]))
+                def _(i, p=p, kept=kept, near=near, group=group):
+                    where = self.inside(p, group, i)
+                    total = kept[where].astype(F32) + near[(0, *where)].astype(F32) + near[(1, *where)].astype(F32)
+                    kept[where] = total.astype(BF)
+
+                if by:
+                    self.copies[p, "b", d] = sent(
+                        kept.at[self.inside(p, group)],
+                        self.second[p].at[d],
+                        self.send.at[p, 0, d],
+                        self.recv.at[p, 0, d],
+                        peer(at, order[1], by),
+                    )
 
     def narrow(self):
         at = self.at
@@ -293,19 +293,21 @@
             for d in range(len(others(order[1]))):
                 self.copies[p, "b", d].wait_recv()
             kept, second, mine = self.kept[p], self.second[p], slot(at, order[1])
-
-            @pl.loop(0, extent(order[0]))
-            def _(i, p=p, kept=kept, second=second, mine=mine):
-                total = kept[self.inside(p, mine, i)].astype(F32)
-                for d in range(3):
-                    total = total + second[d, i].astype(F32)
-                kept[self.inside(p, mine, i)] = total.astype(BF)
-
-            for d, by in enumerate(others(order[0])):
-                block = kept.at[self.inside(p, mine, slot(at, order[0], by))]
-                self.copies[p, "c", d] = sent(
-                    block, self.third[p].at[d], self.send.at[p, 1, d], self.recv.at[p, 1, d], peer(at, order[0], by)
-                )
+            for d, by in enumerate((*others(order[0]), 0)):
+                index = slot(at, order[0], by)
+                where = self.inside(p, mine, index)
+                total = kept[where].astype(F32)
+                for k in range(3):
+                    total = total + second[k, index].astype(F32)
+                kept[where] = total.astype(BF)
+                if by:
+                    self.copies[p, "c", d] = sent(
+                        kept.at[where],
+                        self.third[p].at[d],
+                        self.send.at[p, 1, d],
+                        self.recv.at[p, 1, d],
+                        peer(at, order[0], by),
+                    )
 
     def finish(self, outs):
         at, core, ends = self.at, lax.axis_index("core"), []
@@ -323,6 +325,12 @@
             copy.wait_send()
         for copy in ends:
             copy.wait()
+
+
+def in_four(refs):
+    half = refs[2].shape[-1] // 2
+    lead = (slice(None),) * (len(refs[2].shape) - 1)
+    return [refs[0], refs[1], *(refs[2].at[(*lead, pl.ds(k * half, half))] for k in range(2))]
 
 
 def nn(left, right):
@@ -495,16 +503,14 @@
     two = Gather(at, pieces(3 * third + half, half, wide), full_two, two_sems, PLANE_X)
     attn.to_all(0)
     one.to_all(0)
-    two.to_all(0)
     attn.to_all(1)
     one.spread(1)
     attn.spread(2, 0, 1)
     exchange(0)
     attn.spread(2, 2)
+    two.to_all(0)
     one.forward(1)
-    two.spread(1)
     attn.forward(2)
-    two.forward(1)
     one.spread(2)
     share(0)
     settle(0)
@@ -519,7 +525,7 @@
 
     for p in range(2):
         attn.arrive(p, 2)
-    two.spread(2)
+    two.spread(1)
     wq, wkv, wo = full_attn
 
     def weight(ref, y):
@@ -538,6 +544,7 @@
 
     outs.append(moved(q, q_out, out_sem.at[5]))
     outs.append(moved(kv, kv_out, out_sem.at[6]))
+    two.forward(1)
     one.forward(2)
     scale = 1.0 / math.sqrt(HEAD)
 
@@ -562,7 +569,7 @@
 
     outs.append(moved(probs, probs_out, out_sem.at[7]))
     outs.append(moved(mixed, mixed_out, out_sem.at[8]))
-    two.forward(2)
+    two.spread(2)
 
     attn.arrive(2, 2)
     copies = []
@@ -586,6 +593,7 @@
         if i < 2:
             second_rows[0, i] = sent(n2.at[target], n2.at[target], far_send.at[0, i], far_recv.at[0, i], partner())
     outs.append(moved(hidden.at[rows_at(core * SEQ, SEQ)], hidden_out, out_sem.at[9]))
+    two.forward(2)
     attn.finish()
     outs.extend(moved(full_attn[p], attn_out[p], out_sem.at[2 + p]) for p in range(3))
     share(1)
@@ -698,9 +706,9 @@
             *[pltpu.VMEM((4, 4, 4, 48, third), BF) for _ in range(3)],
             *[pltpu.VMEM(piece, BF) for _ in range(3)],
             *[pltpu.VMEM((2 * ROWS, half), BF) for _ in range(3)],
-            *Gather.semaphores,
-            *Gather.semaphores,
-            *Gather.semaphores,
+            *Gather.semaphores(EVEN),
+            *Gather.semaphores(PLANE_Z),
+            *Gather.semaphores(PLANE_X),
             pltpu.SemaphoreType.DMA((5,)),
             pltpu.SemaphoreType.DMA((5,)),
             pltpu.SemaphoreType.DMA((2, 3)),
@@ -725,8 +733,8 @@
         n2, cot, hidden, n2t, cott, staging, to_pair, from_pair, whole, from_far, keep, halves, to_far, branch, gh,
     ) = refs[27:42]
     one, two, acts_one, acts_two = refs[42:45], refs[45:48], refs[48:51], refs[51:54]
-    buffers, reduce_sems = refs[54:75], refs[75:82]
-    load, put, put_sem, pair_send, pair_recv, part_send, part_recv, far_send, far_recv = refs[82:]
+    buffers, reduce_sems = refs[54:82], refs[82:89]
+    load, put, put_sem, pair_send, pair_recv, part_send, part_recv, far_send, far_recv = refs[89:]
     core, yl = lax.axis_index("core"), lax.axis_index("yl")
     at = coordinates()
     order = (
@@ -745,7 +753,7 @@
     )
     loads = [moved(src, dst, load.at[k]) for k, (src, dst) in enumerate(order)]
     greet(at)
-    total = Reduce(at, data, buffers, reduce_sems, PLANE_Z)
+    total = Reduce(at, in_four(data), buffers, reduce_sems, PLANE)
     total.start()
     for k in range(5):
         loads[k].wait()
@@ -793,8 +801,9 @@
     to_sibling(3, out_rows(yl, 1 - core))
     for k in range(11, 14):
         loads[k].wait()
+    total.spread()
     outs = unit_gradients(n2t, cott, acts_two, staging, grads_out, put_sem)
-    total.spread()
+    total.narrow()
 
     for k, m in ((2, 1 - yl), (3, yl)):
         pair[k].wait_recv()
@@ -822,8 +831,7 @@
         )
         outs.append(moved(branch.at[rows], branch_out.at[target], put.at[6 + i]))
     outs.append(moved(gh, grad_hidden_out, put.at[0]))
-    total.narrow()
-    total.finish(sums_out)
+    total.finish(in_four(sums_out))
     for copy in shared:
         copy.wait()
     for copy in (*pair.values(), *far.values()):
@@ -867,8 +875,8 @@
             pltpu.VMEM(block, F32),
             *[pltpu.VMEM(one[0].shape, BF) for _ in range(6)],
             *[pltpu.VMEM((rows, half), BF) for _ in range(6)],
-            *Reduce.buffers(half, PLANE_Z),
-            *Reduce.semaphores,
+            *Reduce.buffers((half, half, half // 2, half // 2), PLANE),
+            *Reduce.semaphores(PLANE),
             pltpu.SemaphoreType.DMA((14,)),
             pltpu.SemaphoreType.DMA((8,)),
             pltpu.SemaphoreType.DMA((6,)),
@@ -896,10 +904,10 @@
         grad_mixed, dq, dkv, part, keep_part, arrived, in_grad, for_partner, kept, others_half, result,
     ) = refs[26:49]
     attn_grads = refs[49:52]
-    mlp_buffers, attn_buffers = refs[52:73], refs[73:94]
-    mlp_sems, attn_sems = refs[94:101], refs[101:108]
-    mlp_ends, attn_ends, shard, one_sums, gain_part, gain_in = refs[108:111], refs[111:114], *refs[114:118]
-    load, put, send, recv = refs[118:]
+    mlp_buffers, attn_buffers = refs[52:80], refs[80:101]
+    mlp_sems, attn_sems = refs[101:108], refs[108:115]
+    mlp_ends, attn_ends, shard, one_sums, gain_part, gain_in = refs[115:118], refs[118:121], *refs[121:125]
+    load, put, send, recv = refs[125:]
     at = coordinates()
     core, yl = lax.axis_index("core"), lax.axis_index("yl")
     loads = [
@@ -925,7 +933,7 @@
         )
     ]
     greet(at)
-    mlp_sum = Reduce(at, data, mlp_buffers, mlp_sems, PLANE_X)
+    mlp_sum = Reduce(at, in_four(data), mlp_buffers, mlp_sems, PLANE)
     attn_sum = Reduce(at, attn_grads, attn_buffers, attn_sems, SPARE_Y)
     mlp_sum.start()
     finals = [sent(away.at[k], others_half.at[k], send.at[2 + k], recv.at[2 + k], partner()) for k in range(2)]
@@ -937,8 +945,7 @@
         loads[k].wait()
     scale = 1.0 / math.sqrt(HEAD)
 
-    @pl.loop(0, 4)
-    def _(i):
+    def attention(i):
         y, n = i // 2, lax.rem(i, 2)
         rows = rows_at(n * SEQ, SEQ)
         queries, keys, grads = q[y, rows], kv[y, rows], grad_mixed[y, rows]
@@ -963,6 +970,9 @@
             values = jnp.concatenate(pieces, -1)
             target[y, rows] = (values * tables[2 * k] - swap(values, first) * tables[2 * k + 1]).astype(BF)
 
+    pl.loop(0, 2)(attention)
+    mlp_sum.relay()
+    pl.loop(2, 4)(attention)
     loads[6].wait()
 
     def weight_grad(p, left, right):
@@ -973,7 +983,7 @@
 
     weight_grad(0, normed_t, dq)
     weight_grad(1, normed_t, dkv)
-    mlp_sum.relay()
+    mlp_sum.spread()
     branch_t[...] = branch[...].T
     weight_grad(2, branch_t, mixed)
     for k in range(7, 15):
@@ -987,7 +997,7 @@
     pair = sent(part, arrived, send.at[0], recv.at[0], sibling())
     attn_sum.relay()
     keep_part[...] = back(core * SEQ)
-    mlp_sum.spread()
+    mlp_sum.narrow()
     pair.wait()
 
     @pl.loop(0, SEQ // STEP)
@@ -1005,14 +1015,13 @@
         moved(in_grad.at[yl], in_grad_out, put.at[0]),
         sent(for_partner, from_partner, send.at[1], recv.at[1], partner()),
     ]
-    mlp_sum.narrow()
     attn_sum.spread()
     for copy in finals:
         copy.wait()
     result[1 - yl] = (kept[0] + others_half[1].astype(F32)).astype(BF)
     result[yl] = (kept[1] + others_half[0].astype(F32)).astype(BF)
     ends.append(moved(result, result_out, put.at[1]))
-    mlp_sum.finish(mlp_ends)
+    mlp_sum.finish(in_four(mlp_ends))
     attn_sum.narrow()
     ends.extend(moved(mlp_ends[p], mlp_outs[p], put.at[2 + p]) for p in range(3))
 
@@ -1078,10 +1087,10 @@
             pltpu.VMEM(half, BF),
             pltpu.VMEM(half, BF),
             *[pltpu.VMEM((4, 4, 4, 48, third), BF) for _ in range(3)],
-            *Reduce.buffers(wide, PLANE_X),
-            *Reduce.buffers(third, SPARE_Y),
-            *Reduce.semaphores,
-            *Reduce.semaphores,
+            *Reduce.buffers((wide, wide, wide // 2, wide // 2), PLANE),
+            *Reduce.buffers((third,) * 3, SPARE_Y),
+            *Reduce.semaphores(PLANE),
+            *Reduce.semaphores(SPARE_Y),
             *[pltpu.VMEM((2, 24, wide), F32) for _ in range(3)],
             *[pltpu.VMEM((2, 24, third), F32) for _ in range(3)],
             pltpu.VMEM(shard.shape, F32),

time: 250 us -> 235 us (0.940)
  Pallas kernels: 245 us -> 231 us
    pallas_call x3, Pallas kernels: 242 us -> 227 us  [call(): pl.pallas_call(kernel, out_shape=results, in_specs=in_specs, out_specs=ou...]
where the time goes in v8:
time: 235 us; the launch traced here: 231 us
  Pallas kernels  231 us (98%)
    pallas_call x3, Pallas kernels, call(): pl.pallas_call(kernel, out_shape=results, in_specs=in_specs, out_specs=ou...  227 us

profile of v8, /device:TPU:1, one launch (start us, length us, event | category | flops | bytes accessed | tf_op | source)
XLA Modules:
  0.0 231.5 jit_solution(748564170140718171)
XLA Ops:
  0.6 112.4 %gather_attn_forward_mlp.1 = (bf16[2,4,4,48,512]{4,3,2,1,0:T(8,128)(2,1)}, bf16[2,4,4,48,512]{4,3,2,1,0:T(8,128)(2,1)}, bf16[2,4,4,48,512]{4,3,2,1,0:T(8,128)(2,...) custom-call(bf16[24,768]{1,0:T(8,128)(2,1)} %refs_0_.1, ...), custom_call_target="tpu_custom_call" | custom-call | tf_op jit(solution)/shard_map/gather_attn_forward_mlp/pallas_call | solution.py:381
  113.1 38.9 %mlp_reduce.1 = (f32[2,24,512]{2,1,0:T(8,128)}, f32[2,24,512]{2,1,0:T(8,128)}, f32[2,24,512]{2,1,0:T(8,128)}, bf16[1536,512]{1,0:T(8,128)(2,1)}, bf16[1536,512]{...) custom-call(bf16[1024,1536]{1,0:T(8,128)(2,1)} %get-tuple-element.70, ...), custom_call_target="tpu_custom_call" | custom-call | tf_op jit(solution)/shard_map/mlp_reduce/pallas_call | solution.py:381
  152.0 75.6 %attn_backward_reduce.1 = (f32[2,24,512]{2,1,0:T(8,128)}, f32[2,24,512]{2,1,0:T(8,128)}, f32[2,24,512]{2,1,0:T(8,128)}, f32[2,24,384]{2,1,0:T(8,128)}, f32[2,24,...) custom-call(bf16[2,2,128,1536]{3,2,1,0:T(8,128)(2,1)} %get-tuple-ele, ...), custom_call_target="tpu_custom_call" | custom-call | tf_op jit(solution)/shard_map/attn_backward_reduce/pallas_call | solution.py:381
  227.7 3.6 %place_outputs.1 = (bf16[2,128,1536]{2,1,0:T(8,128)(2,1)}, f32[2,128,1536]{2,1,0:T(8,128)}, f32[24,768]{1,0:T(8,128)}, f32[24,384]{1,0:T(8,128)}, f32[24,384]{1,...) custom-call(f32[128,1536]{1,0:T(8,128)} %get-tuple-element.105.refs_, ...), custom_call_target="tpu_custom_call" | custom-call | tf_op jit(solution)/shard_map/place_outputs/pallas_call | solution.py:1143

commit v9 on v8

--- a/solution.py
+++ b/solution.py
@@ -421,7 +421,7 @@
 
 
 def forward_kernel(third, wide, *refs):
-    own_weights, gains_one, gains_two, lengths, xin, gin, tables = refs[:7], *refs[7:13]
+    own_weights, gains_one, gains_two, lengths, xin, gin, tables_in = refs[:7], *refs[7:13]
     refs = refs[1:]
     full_two, full_one = refs[12:15], refs[15:18]
     (
@@ -435,11 +435,12 @@
     ) = refs[38:57]
     full_attn, weights, acts = refs[57:60], refs[60:63], refs[63:66]
     attn_sems, one_sems, two_sems = refs[66:71], refs[71:76], refs[76:81]
-    pair_send, pair_recv, row_send, row_recv, far_send, far_recv, own_sem, out_sem, put_sem = refs[81:]
+    tables, pair_send, pair_recv, row_send, row_recv, far_send, far_recv, own_sem, out_sem, put_sem = refs[81:]
     at = coordinates()
     core, yl = lax.axis_index("core"), lax.axis_index("yl")
     own_x = moved(xin.at[yl], xs.at[core, yl], own_sem.at[0])
     own_g = moved(gin, gs.at[:, core, yl], own_sem.at[1])
+    table_copy = moved(tables_in, tables, own_sem.at[2])
 
     query, key, value, output, *mlp_weights = (ref[...].astype(F32) for ref in own_weights)
     gain_one, gain_two = as_column(gains_one), as_column(gains_two)
@@ -527,6 +528,7 @@
         attn.arrive(p, 2)
     two.spread(1)
     wq, wkv, wo = full_attn
+    table_copy.wait()
 
     def weight(ref, y):
         return ref[pl.ds(2 * y, 2)].reshape(-1, third)
@@ -593,7 +595,6 @@
         if i < 2:
             second_rows[0, i] = sent(n2.at[target], n2.at[target], far_send.at[0, i], far_recv.at[0, i], partner())
     outs.append(moved(hidden.at[rows_at(core * SEQ, SEQ)], hidden_out, out_sem.at[9]))
-    two.forward(2)
     attn.finish()
     outs.extend(moved(full_attn[p], attn_out[p], out_sem.at[2 + p]) for p in range(3))
     share(1)
@@ -613,6 +614,7 @@
     mine_rows, their_rows = rows_at(mine, ROWS), rows_at(theirs, ROWS)
     for sub in range(2):
         hidden_units(yl, 0, 2, sub, n2, gs, weights, acts)
+    two.forward(2)
     outs.extend(moved(acts[p].at[mine_rows], acts_out[p].at[mine_rows], out_sem.at[15 + p]) for p in range(3))
     outs.append(moved(n2.at[mine_rows], n2_out.at[mine_rows], out_sem.at[18]))
     for m in range(2):
@@ -663,7 +665,7 @@
     return call(
         lambda *refs: forward_kernel(third, wide, *refs),
         (*own_weights, *gains, lengths, xin, gin, tables),
-        [VMEM] * 10 + [ANY, ANY, VMEM],
+        [VMEM] * 10 + [ANY, ANY, ANY],
         [shaped(piece)] * 6
         + [
             shaped((2, 2, 128, width)),
@@ -709,13 +711,14 @@
             *Gather.semaphores(EVEN),
             *Gather.semaphores(PLANE_Z),
             *Gather.semaphores(PLANE_X),
+            pltpu.VMEM(tables.shape, F32),
             pltpu.SemaphoreType.DMA((5,)),
             pltpu.SemaphoreType.DMA((5,)),
             pltpu.SemaphoreType.DMA((2, 3)),
             pltpu.SemaphoreType.DMA((2, 3)),
             pltpu.SemaphoreType.DMA((2, 2)),
             pltpu.SemaphoreType.DMA((2, 2)),
-            pltpu.SemaphoreType.DMA((2,)),
+            pltpu.SemaphoreType.DMA((3,)),
             pltpu.SemaphoreType.DMA((25,)),
             pltpu.SemaphoreType.DMA((6,)),
         ],
@@ -893,12 +896,12 @@
 
 
 def backward_kernel(*refs):
-    xall, grad_hidden_in, branch_in, n1t_in, q_in, kv_in, probs_in, mixed_in, wq_in, wkv_in, wo_in, tables = refs[:12]
+    xall, grad_hidden_in, branch_in, n1t_in, q_in, kv_in, probs_in, mixed_in, wq_in, wkv_in, wo_in, tables_in = refs[:12]
     data, kept_in, away, shard_in, one_in = refs[12:15], *refs[15:18], refs[18:20]
     refs = refs[3:]
     mlp_outs, attn_outs, result_out, in_grad_out, from_partner = refs[17:20], refs[20:23], *refs[23:26]
-    gains_out = refs[26]
-    refs = refs[1:]
+    gains_out, gain_in = refs[26:28]
+    refs = refs[2:]
     (
         xs, gh, branch, branch_t, normed_t, q, kv, probs, mixed, wq, wkv, wo,
         grad_mixed, dq, dkv, part, keep_part, arrived, in_grad, for_partner, kept, others_half, result,
@@ -906,7 +909,7 @@
     attn_grads = refs[49:52]
     mlp_buffers, attn_buffers = refs[52:80], refs[80:101]
     mlp_sems, attn_sems = refs[101:108], refs[108:115]
-    mlp_ends, attn_ends, shard, one_sums, gain_part, gain_in = refs[115:118], refs[118:121], *refs[121:125]
+    mlp_ends, attn_ends, shard, one_sums, gain_part, tables = refs[115:118], refs[118:121], *refs[121:125]
     load, put, send, recv = refs[125:]
     at = coordinates()
     core, yl = lax.axis_index("core"), lax.axis_index("yl")
@@ -929,6 +932,7 @@
                 (shard_in, shard),
                 (one_in[0], one_sums.at[0]),
                 (one_in[1], one_sums.at[1]),
+                (tables_in, tables),
             )
         )
     ]
@@ -941,7 +945,7 @@
         loads[k].wait()
     for y in range(2):
         grad_mixed[y] = nn(branch[...], wo[y]).astype(BF)
-    for k in range(2, 6):
+    for k in (2, 3, 4, 5, 15):
         loads[k].wait()
     scale = 1.0 / math.sqrt(HEAD)
 
@@ -1040,9 +1044,7 @@
     first = sum(along(thin * p, attn_ends[p][...]) for p in range(2))
     lane = lax.broadcasted_iota(jnp.int32, gain_part.shape, 1)
     gain_part[...] = jnp.where(lane == 0, first, second)
-    swapped = sent(gain_part, gain_in, send.at[4], recv.at[4], partner())
-    swapped.wait()
-    gain_part[...] = gain_part[...] + gain_in[...]
+    ends.append(sent(gain_part, gain_in, send.at[4], recv.at[4], partner()))
     ends.append(moved(gain_part, gains_out, put.at[8]))
     for copy in ends:
         copy.wait()
@@ -1057,11 +1059,12 @@
     return call(
         backward_kernel,
         (x, grad_hidden, branch, n1t, q, kv, probs, mixed, wq, wkv, wo, tables, *data, kept, away, shard, *one_sums),
-        [ANY] * 11 + [VMEM] + [ANY] * 8,
+        [ANY] * 20,
         [shaped((2, 24, wide), F32)] * 3
         + [shaped((2, 24, third), F32)] * 3
-        + [shaped(half), shaped(half[1:], F32), shaped(half[1:]), shaped((24, 128), F32)],
-        [ANY] * 10,
+        + [shaped(half), shaped(half[1:], F32), shaped(half[1:])]
+        + [shaped((24, 128), F32)] * 2,
+        [ANY] * 11,
         [
             pltpu.VMEM(half, BF),
             pltpu.VMEM((SEQ, width), F32),
@@ -1096,8 +1099,8 @@
             pltpu.VMEM(shard.shape, F32),
             pltpu.VMEM((2, 2, 24, wide), F32),
             pltpu.VMEM((24, 128), F32),
-            pltpu.VMEM((24, 128), F32),
-            pltpu.SemaphoreType.DMA((15,)),
+            pltpu.VMEM(tables.shape, F32),
+            pltpu.SemaphoreType.DMA((16,)),
             pltpu.SemaphoreType.DMA((9,)),
             pltpu.SemaphoreType.DMA((5,)),
             pltpu.SemaphoreType.DMA((5,)),
@@ -1107,7 +1110,7 @@
     )
 
 
-def last_kernel(own, theirs, result_in, one, two, attn, gains_one, gains_two, gain_sums, outs):
+def last_kernel(own, theirs, result_in, one, two, attn, gains_one, gains_two, gain_sums, more, outs):
     result, in_grad, dq, dk, dv, do, dg, du, dd, gain_one_grad, gain_two_grad = outs
     yl = lax.axis_index("yl")
     result[...] = result_in[...]
@@ -1129,16 +1132,16 @@
     dk[...] = jnp.concatenate(keys[0], -1)
     dv[...] = jnp.concatenate(keys[1], -1)
     lane = lax.broadcasted_iota(jnp.int32, gain_sums.shape, 1)
-    grads = (gain_sums[...] / jnp.where(lane == 0, gain_one, gain_two)).T
+    grads = ((gain_sums[...] + more[...]) / jnp.where(lane == 0, gain_one, gain_two)).T
     gain_one_grad[...] = grads[0:1, :24]
     gain_two_grad[...] = grads[1:2, :24]
 
 
-def placed_outputs(own, theirs, result, one, two, attn, gains, gain_sums):
+def placed_outputs(own, theirs, result, one, two, attn, gains, gain_sums, more_gain_sums):
     width, thin, half = own.shape[1], attn[0].shape[2], two[0].shape[2]
 
     def kernel(*refs):
-        last_kernel(*refs[:3], refs[3:6], refs[6:9], refs[9:12], *refs[12:15], refs[15:])
+        last_kernel(*refs[:3], refs[3:6], refs[6:9], refs[9:12], *refs[12:16], refs[16:])
 
     return pl.pallas_call(
         kernel,
@@ -1155,11 +1158,11 @@
             shaped((1, 24), F32),
             shaped((1, 24), F32),
         ],
-        in_specs=[VMEM] * 15,
+        in_specs=[VMEM] * 16,
         out_specs=[VMEM] * 11,
         compiler_params=pltpu.CompilerParams(vmem_limit_bytes=VMEM_LIMIT),
         name="place_outputs",
-    )(own, theirs, result, *one, *two, *attn, *gains, gain_sums)
+    )(own, theirs, result, *one, *two, *attn, *gains, gain_sums, more_gain_sums)
 
 
 def tables_for(count, heads, plain):
@@ -1218,7 +1221,7 @@
     *one_sums, dg, du, dd, kept, away, branch, grad_hidden = middle(
         n2, cot, hidden, n2t, cott, one, two, acts, [blocked(w) for w in grads]
     )
-    *sums, result, in_grad, in_grad_theirs, gain_sums = backward(
+    *sums, result, in_grad, in_grad_theirs, gain_sums, more_gain_sums = backward(
         x,
         grad_hidden,
         branch,
@@ -1238,7 +1241,7 @@
         one_sums[:2],
     )
     result, in_grad, dq, dk, dv, do, dg, du, dd, gain_one_grad, gain_two_grad = placed_outputs(
-        in_grad, in_grad_theirs, result, one_sums, sums[:3], sums[3:], gains, gain_sums
+        in_grad, in_grad_theirs, result, one_sums, sums[:3], sums[3:], gains, gain_sums, more_gain_sums
     )
     return result, in_grad, dq, dk, dv, do.T, dg, du, dd.T, gain_one_grad.reshape(24), gain_two_grad.reshape(24)
 

time: 235 us -> 229 us (0.974)
  Pallas kernels: 231 us -> 225 us
    pallas_call x3, Pallas kernels: 227 us -> 221 us  [call(): pl.pallas_call(kernel, out_shape=results, in_specs=in_specs, out_specs=ou...]
where the time goes in v9:
time: 229 us; the launch traced here: 226 us
  Pallas kernels  225 us (98%)
    pallas_call x3, Pallas kernels, call(): pl.pallas_call(kernel, out_shape=results, in_specs=in_specs, out_specs=ou...  221 us

profile of v9, /device:TPU:1, one launch (start us, length us, event | category | flops | bytes accessed | tf_op | source)
XLA Modules:
  0.0 225.7 jit_solution(15628749067968266729)
XLA Ops:
  0.6 108.3 %gather_attn_forward_mlp.1 = (bf16[2,4,4,48,512]{4,3,2,1,0:T(8,128)(2,1)}, bf16[2,4,4,48,512]{4,3,2,1,0:T(8,128)(2,1)}, bf16[2,4,4,48,512]{4,3,2,1,0:T(8,128)(2,...) custom-call(bf16[24,768]{1,0:T(8,128)(2,1)} %refs_0_.1, ...), custom_call_target="tpu_custom_call" | custom-call | tf_op jit(solution)/shard_map/gather_attn_forward_mlp/pallas_call | solution.py:381
  109.0 39.0 %mlp_reduce.1 = (f32[2,24,512]{2,1,0:T(8,128)}, f32[2,24,512]{2,1,0:T(8,128)}, f32[2,24,512]{2,1,0:T(8,128)}, bf16[1536,512]{1,0:T(8,128)(2,1)}, bf16[1536,512]{...) custom-call(bf16[1024,1536]{1,0:T(8,128)(2,1)} %get-tuple-element.71, ...), custom_call_target="tpu_custom_call" | custom-call | tf_op jit(solution)/shard_map/mlp_reduce/pallas_call | solution.py:381
  147.9 73.9 %attn_backward_reduce.1 = (f32[2,24,512]{2,1,0:T(8,128)}, f32[2,24,512]{2,1,0:T(8,128)}, f32[2,24,512]{2,1,0:T(8,128)}, f32[2,24,384]{2,1,0:T(8,128)}, f32[2,24,...) custom-call(bf16[2,2,128,1536]{3,2,1,0:T(8,128)(2,1)} %get-tuple-ele, ...), custom_call_target="tpu_custom_call" | custom-call | tf_op jit(solution)/shard_map/attn_backward_reduce/pallas_call | solution.py:381
  221.9 3.6 %place_outputs.1 = (bf16[2,128,1536]{2,1,0:T(8,128)(2,1)}, f32[2,128,1536]{2,1,0:T(8,128)}, f32[24,768]{1,0:T(8,128)}, f32[24,384]{1,0:T(8,128)}, f32[24,384]{1,...) custom-call(f32[128,1536]{1,0:T(8,128)} %get-tuple-element.106.refs_, ...), custom_call_target="tpu_custom_call" | custom-call | tf_op jit(solution)/shard_map/place_outputs/pallas_call | solution.py:1146

commit v10 on v9

--- a/solution.py
+++ b/solution.py
@@ -251,7 +251,7 @@
                 @pl.loop(0, 4 * size)
                 def _(i, d=d, side=side, far=far):
                     a, b = i // 4, lax.rem(i, 4)
-                    side[d, a, b] = (side[d, a, b].astype(F32) + far[d, a, b].astype(F32)).astype(BF)
+                    side[d, a, b] = side[d, a, b] + far[d, a, b]
 
                 self.copies[p, d, 2] = sent(
                     side.at[d],
@@ -398,7 +398,7 @@
     gate_w, up_w, down_w = (w[..., columns].reshape(-1, CHUNK) for w in weights)
     gate = nn(n2[rows], gate_w)
     up = nn(n2[rows], up_w)
-    sigma = 0.5 + 0.5 * jnp.tanh(0.5 * gate)
+    sigma = jax.nn.sigmoid(gate)
     silu = gate * sigma
     grad_active = nn(cot[m, pl.ds(c, count)].reshape(count * SEQ, -1), down_w)
     acts[0][rows, columns] = (silu * up).astype(BF)
@@ -636,14 +636,17 @@
     for sub in range(2):
         hidden_units(1 - yl, core, 1, sub, n2, gs, weights, acts)
     for i in range(2):
+        block = rows_at(theirs + (2 * core + i) * STEP, STEP)
+        n2t[:, block] = n2[block].T
+    for i in range(2):
         second_rows[0, i].wait_send()
         second_rows[1, i].wait()
     for sub in range(2):
         hidden_units(1 - yl, 1 - core, 1, sub, n2, gs, weights, acts)
     outs.extend(moved(acts[p].at[their_rows], acts_out[p].at[their_rows], out_sem.at[20 + p]) for p in range(3))
     outs.append(moved(n2.at[their_rows], n2_out.at[their_rows], out_sem.at[23]))
-    for i in range(ROWS // STEP):
-        block = rows_at(theirs + i * STEP, STEP)
+    for i in range(2):
+        block = rows_at(theirs + (2 * (1 - core) + i) * STEP, STEP)
         n2t[:, block] = n2[block].T
     outs.append(moved(n2t, n2t_out, out_sem.at[19]))
     outs.extend(unit_gradients(n2t, cott, acts, staging, grads_out, put_sem, their_rows, added=True))

time: 229 us -> 229 us (level)
  no operation moved by 1% of the time
where the time goes in v10:
time: 229 us; the launch traced here: 226 us
  Pallas kernels  225 us (98%)
    pallas_call x3, Pallas kernels, call(): pl.pallas_call(kernel, out_shape=results, in_specs=in_specs, out_specs=ou...  221 us

profile of v10, /device:TPU:1, one launch (start us, length us, event | category | flops | bytes accessed | tf_op | source)
XLA Modules:
  0.0 225.6 jit_solution(9422043264927490214)
XLA Ops:
  0.6 108.1 %gather_attn_forward_mlp.1 = (bf16[2,4,4,48,512]{4,3,2,1,0:T(8,128)(2,1)}, bf16[2,4,4,48,512]{4,3,2,1,0:T(8,128)(2,1)}, bf16[2,4,4,48,512]{4,3,2,1,0:T(8,128)(2,...) custom-call(bf16[24,768]{1,0:T(8,128)(2,1)} %refs_0_.1, ...), custom_call_target="tpu_custom_call" | custom-call | tf_op jit(solution)/shard_map/gather_attn_forward_mlp/pallas_call | solution.py:381
  108.7 38.9 %mlp_reduce.1 = (f32[2,24,512]{2,1,0:T(8,128)}, f32[2,24,512]{2,1,0:T(8,128)}, f32[2,24,512]{2,1,0:T(8,128)}, bf16[1536,512]{1,0:T(8,128)(2,1)}, bf16[1536,512]{...) custom-call(bf16[1024,1536]{1,0:T(8,128)(2,1)} %get-tuple-element.71, ...), custom_call_target="tpu_custom_call" | custom-call | tf_op jit(solution)/shard_map/mlp_reduce/pallas_call | solution.py:381
  147.7 73.9 %attn_backward_reduce.1 = (f32[2,24,512]{2,1,0:T(8,128)}, f32[2,24,512]{2,1,0:T(8,128)}, f32[2,24,512]{2,1,0:T(8,128)}, f32[2,24,384]{2,1,0:T(8,128)}, f32[2,24,...) custom-call(bf16[2,2,128,1536]{3,2,1,0:T(8,128)(2,1)} %get-tuple-ele, ...), custom_call_target="tpu_custom_call" | custom-call | tf_op jit(solution)/shard_map/attn_backward_reduce/pallas_call | solution.py:381
  221.6 3.6 %place_outputs.1 = (bf16[2,128,1536]{2,1,0:T(8,128)(2,1)}, f32[2,128,1536]{2,1,0:T(8,128)}, f32[24,768]{1,0:T(8,128)}, f32[24,384]{1,0:T(8,128)}, f32[24,384]{1,...) custom-call(f32[128,1536]{1,0:T(8,128)} %get-tuple-element.106.refs_, ...), custom_call_target="tpu_custom_call" | custom-call | tf_op jit(solution)/shard_map/place_outputs/pallas_call | solution.py:1149

commit v11 on v10

--- a/solution.py
+++ b/solution.py
@@ -1113,12 +1113,12 @@
     )
 
 
-def last_kernel(own, theirs, result_in, one, two, attn, gains_one, gains_two, gain_sums, more, outs):
+def last_kernel(own, theirs, result_in, one, two, attn, gains_one, gains_two, gain_sums, more, outs, wide, sems):
     result, in_grad, dq, dk, dv, do, dg, du, dd, gain_one_grad, gain_two_grad = outs
     yl = lax.axis_index("yl")
-    result[...] = result_in[...]
-    in_grad[yl] = own[...]
-    in_grad[1 - yl] = theirs[...].astype(F32)
+    copies = [moved(own, in_grad.at[yl], sems.at[0]), moved(result_in, result, sems.at[1])]
+    wide[...] = theirs[...].astype(F32)
+    copies.append(moved(wide, in_grad.at[1 - yl], sems.at[2]))
     gain_one, gain_two = as_column(gains_one), as_column(gains_two)
     thin, half = attn[0].shape[2], two[0].shape[2]
     keys = [[], []]
@@ -1138,13 +1138,15 @@
     grads = ((gain_sums[...] + more[...]) / jnp.where(lane == 0, gain_one, gain_two)).T
     gain_one_grad[...] = grads[0:1, :24]
     gain_two_grad[...] = grads[1:2, :24]
+    for copy in copies:
+        copy.wait()
 
 
 def placed_outputs(own, theirs, result, one, two, attn, gains, gain_sums, more_gain_sums):
     width, thin, half = own.shape[1], attn[0].shape[2], two[0].shape[2]
 
     def kernel(*refs):
-        last_kernel(*refs[:3], refs[3:6], refs[6:9], refs[9:12], *refs[12:16], refs[16:])
+        last_kernel(*refs[:3], refs[3:6], refs[6:9], refs[9:12], *refs[12:16], refs[16:27], *refs[27:])
 
     return pl.pallas_call(
         kernel,
@@ -1161,8 +1163,9 @@
             shaped((1, 24), F32),
             shaped((1, 24), F32),
         ],
-        in_specs=[VMEM] * 16,
-        out_specs=[VMEM] * 11,
+        in_specs=[ANY, VMEM, ANY] + [VMEM] * 13,
+        out_specs=[ANY] * 2 + [VMEM] * 9,
+        scratch_shapes=[pltpu.VMEM((STEP, width), F32), pltpu.SemaphoreType.DMA((3,))],
         compiler_params=pltpu.CompilerParams(vmem_limit_bytes=VMEM_LIMIT),
         name="place_outputs",
     )(own, theirs, result, *one, *two, *attn, *gains, gain_sums, more_gain_sums)

time: 229 us -> 276 us (1.21)
  Pallas kernels: 225 us -> 272 us
    pallas_call x1, Pallas kernels: 3.58 us -> 51 us  [placed_outputs(): pl.pallas_call(kernel, out_shape=[shaped((2, STEP, width)), shaped((2, ST...]
where the time goes in v11:
time: 276 us; the launch traced here: 273 us
  Pallas kernels  272 us (99%)
    pallas_call x3, Pallas kernels, call(): pl.pallas_call(kernel, out_shape=results, in_specs=in_specs, out_specs=ou...  221 us
    pallas_call x1, Pallas kernels, placed_outputs(): pl.pallas_call(kernel, out_shape=[shaped((2, STEP, width)), shaped((2, ST...  51 us

profile of v11, /device:TPU:1, one launch (start us, length us, event | category | flops | bytes accessed | tf_op | source)
XLA Modules:
  0.0 273.1 jit_solution(14724026766200517700)
XLA Ops:
  0.6 108.1 %gather_attn_forward_mlp.1 = (bf16[2,4,4,48,512]{4,3,2,1,0:T(8,128)(2,1)}, bf16[2,4,4,48,512]{4,3,2,1,0:T(8,128)(2,1)}, bf16[2,4,4,48,512]{4,3,2,1,0:T(8,128)(2,...) custom-call(bf16[24,768]{1,0:T(8,128)(2,1)} %refs_0_.1, ...), custom_call_target="tpu_custom_call" | custom-call | tf_op jit(solution)/shard_map/gather_attn_forward_mlp/pallas_call | solution.py:381
  108.7 38.9 %mlp_reduce.1 = (f32[2,24,512]{2,1,0:T(8,128)}, f32[2,24,512]{2,1,0:T(8,128)}, f32[2,24,512]{2,1,0:T(8,128)}, bf16[1536,512]{1,0:T(8,128)(2,1)}, bf16[1536,512]{...) custom-call(bf16[1024,1536]{1,0:T(8,128)(2,1)} %get-tuple-element.71, ...), custom_call_target="tpu_custom_call" | custom-call | tf_op jit(solution)/shard_map/mlp_reduce/pallas_call | solution.py:381
  147.7 73.9 %attn_backward_reduce.1 = (f32[2,24,512]{2,1,0:T(8,128)}, f32[2,24,512]{2,1,0:T(8,128)}, f32[2,24,512]{2,1,0:T(8,128)}, f32[2,24,384]{2,1,0:T(8,128)}, f32[2,24,...) custom-call(bf16[2,2,128,1536]{3,2,1,0:T(8,128)(2,1)} %get-tuple-ele, ...), custom_call_target="tpu_custom_call" | custom-call | tf_op jit(solution)/shard_map/attn_backward_reduce/pallas_call | solution.py:381
  221.6 51.0 %place_outputs.1 = (bf16[2,128,1536]{2,1,0:T(8,128)(2,1)}, f32[2,128,1536]{2,1,0:T(8,128)}, f32[24,768]{1,0:T(8,128)}, f32[24,384]{1,0:T(8,128)}, f32[24,384]{1,...) custom-call(f32[128,1536]{1,0:T(8,128)} %get-tuple-element.106.refs_, ...), custom_call_target="tpu_custom_call" | custom-call | tf_op jit(solution)/shard_map/place_outputs/pallas_call | solution.py:1151
